TPU v7x, 32 devices: a whole 2x2x4 slice. The times are simulated.
32 devices in a mesh: dp: 8 (over y, x, core), expert: 4 (over z).
Axes of the slice: x: 2, y: 2, z: 4, core: 2. Of those that a mesh axis runs over, the one named last changes fastest.
Arguments:
- hidden_in: bfloat16 [4096, 2048], P(('dp', 'expert')), may hold values from -6 to 6
- seq_lengths: int32 [32], P(('dp', 'expert')), may hold values from 32 to 128, as said below
- attn_routes: int32 [4096, 2], P(('dp', 'expert')), may hold values from 0 to 3, all different within a row; in each aligned block of 128 rows (0 to 127, 128 to 255, ...) at most 96 rows name the same one
- attn_gates: float32 [4096, 2], P(('dp', 'expert')), may hold values from 0.25 to 1
- mlp_routes: int32 [4096, 2], P(('dp', 'expert')), may hold values from 0 to 3, all different within a row; in each aligned block of 128 rows (0 to 127, 128 to 255, ...) at most 96 rows name the same one
- mlp_gates: float32 [4096, 2], P(('dp', 'expert')), may hold values from 0.25 to 1
- attn_gain: bfloat16 [2048], P(('dp', 'expert')), may hold values from 0.5 to 1.5
- mlp_gain: bfloat16 [2048], P(('dp', 'expert')), may hold values from 0.5 to 1.5
- k_weight: bfloat16 [2048, 2048], P(('dp', 'expert')), may hold values from -0.125 to 0.125
- v_weight: bfloat16 [2048, 2048], P(('dp', 'expert')), may hold values from -0.125 to 0.125
- attn_experts: bfloat16 [4, 2048, 2, 2048], P('expert', 'dp'), may hold values from -0.25 to 0.25
- mlp_experts: bfloat16 [4, 5632, 3, 2048], P('expert', 'dp'), may hold values from -0.125 to 0.125
- logit_limit: float32 [16], replicated, may hold values from 1.5 to 4.5
- out_grad: bfloat16 [4096, 2048], P(('dp', 'expert')), may hold values from -6 to 6
Outputs:
- block_out: bfloat16 [4096, 2048], P(('dp', 'expert'))
- grad_input: float32 [4096, 2048], P(('dp', 'expert'))
- grad_k_weight: float32 [2048, 2048], P(('dp', 'expert'))
- grad_v_weight: float32 [2048, 2048], P(('dp', 'expert'))
- grad_attn_gain: float32 [2048], P(('dp', 'expert'))
- grad_mlp_gain: float32 [2048], P(('dp', 'expert'))
- grad_attn_experts: float32 [4, 2048, 2, 2048], P('expert', 'dp')
- grad_mlp_experts: float32 [4, 5632, 3, 2048], P('expert', 'dp')
- clipped_query: bfloat16 [4, 2048, 2048], P('expert', 'dp')
- clipped_key: bfloat16 [2048, 2048], P(('dp', 'expert'))
- clip_factors: float32 [16], replicated
Inputs may be any that keep to these rules, and one draw needn't show every extreme that they name: `seq_lengths`: one sequence has all 128 slots live in every draw. `attn_routes`: each token names 2 different experts; among the tokens of one sequence no expert is named more than 96 times. `mlp_routes`: each token names 2 different experts; among the tokens of one sequence no expert is named more than 96 times.
All inputs are finite; a program needn't handle non-finite values.
Results may differ from a plain program's by a relative error of at most 0.02.
Values may be sent and summed in bfloat16 or wider, within the bound.
No kernel may reach another device: no remote copies, remote signals or barrier semaphores. Data moves between devices by JAX's collectives and lax.ppermute only.
A program may use at most 704 MiB of HBM per device.

v0:
```python
import jax
import jax.numpy as jnp
from jax import lax
from jax.sharding import PartitionSpec as P

KVH = 16
HD = 128
TOPK = 2


eps = 1e-06
rope_base = 10000.0
masked_value = -1e30
highest = lax.Precision.HIGHEST


def rms_norm(values, gain_vec):
    return values * lax.rsqrt(jnp.mean(values * values, axis=-1, keepdims=True) + eps) * gain_vec


def norm_back(values, gain_vec, grad_out):
    inverse = lax.rsqrt(jnp.mean(values * values, axis=-1, keepdims=True) + eps)
    scaled = grad_out * gain_vec
    inner = jnp.mean(scaled * values, axis=-1, keepdims=True)
    grad_values = inverse * scaled - values * inverse * inverse * inverse * inner
    grad_gain = jnp.sum(grad_out * values * inverse, axis=0)
    return (grad_values, grad_gain)


def rotate(values, places):
    half_dim = values.shape[-1] // 2
    freqs = rope_base ** (-jnp.arange(half_dim, dtype=jnp.float32) / half_dim)
    angles = places.astype(jnp.float32)[..., None, None] * freqs
    cosine = jnp.cos(angles)
    sine_val = jnp.sin(angles)
    first_half = values[..., :half_dim]
    second_half = values[..., half_dim:]
    return jnp.concatenate(
        [
            first_half * cosine - second_half * sine_val,
            second_half * cosine + first_half * sine_val,
        ],
        axis=-1,
    )


def tables(routes, gate_vals, length, expert_count, slot_cap):
    seq_len = routes.shape[0]
    choices_per = routes.shape[1]
    flat_ids = routes.reshape(-1)
    places = jnp.arange(seq_len, dtype=jnp.int32)
    labels = jnp.arange(expert_count, dtype=jnp.int32)
    onehot = (flat_ids[:, None] == labels[None, :]).astype(jnp.int32)
    ranking = jnp.sum((jnp.cumsum(onehot, axis=0) - onehot) * onehot, axis=1)
    slot_ids = jnp.arange(slot_cap, dtype=jnp.int32)
    is_live = jnp.repeat(places < length, choices_per)
    matches = (
        (flat_ids[None, None, :] == labels[:, None, None])
        & (ranking[None, None, :] == slot_ids[None, :, None])
        & is_live[None, None, :]
    )
    matches = matches.reshape(expert_count, slot_cap, seq_len, choices_per).astype(jnp.int32)
    taken_rows = jnp.sum(matches, axis=3)
    slot_place = jnp.sum(taken_rows * places[None, None, :], axis=2)
    filled = jnp.sum(taken_rows, axis=2)
    weighted = jnp.sum(matches.astype(jnp.float32) * gate_vals[None, None, :, :], axis=3)
    return (taken_rows.astype(jnp.float32), weighted, slot_place, filled)


def dot_rows(left, right):
    return lax.dot_general(
        left, right, (((1,), (1,)), ((), ())), preferred_element_type=jnp.float32
    )


def dot_cols(left, right, precision=None):
    return lax.dot_general(
        left,
        right,
        (((0,), (0,)), ((), ())),
        preferred_element_type=jnp.float32,
        precision=precision,
    )


def head_scale(index, roots, head_dim):
    owners = (
        index[:, None] // head_dim == jnp.arange(roots.shape[0], dtype=jnp.int32)[None, :]
    ).astype(jnp.float32)
    return jnp.dot(owners, roots, precision=highest)


def to_experts(slots):
    return lax.all_to_all(slots, "expert", split_axis=0, concat_axis=0, tiled=True)


def from_experts(slots):
    return lax.all_to_all(slots, "expert", split_axis=0, concat_axis=0, tiled=True)


def on_device(
    hidden_in,
    seq_lengths,
    attn_routes,
    attn_gates,
    mlp_routes,
    mlp_gates,
    attn_gain,
    mlp_gain,
    k_weight,
    v_weight,
    attn_experts,
    mlp_experts,
    logit_limit,
    out_grad,
):
    experts = lax.axis_size("expert")
    expert_id = lax.axis_index("expert")
    dp_id = lax.axis_index("dp")
    seq_len = hidden_in.shape[0]
    model_width = hidden_in.shape[1]
    capacity = seq_len * TOPK * 3 // (2 * experts)
    head_count = KVH
    head_dim = HD
    features = head_count * head_dim
    score_scale = head_dim ** (-0.5)
    length = seq_lengths[0]
    places = jnp.arange(seq_len, dtype=jnp.int32)
    keep_mask = (places < length).astype(jnp.float32)[:, None]
    k_full, v_full, gain_one, gain_two = (
        lax.all_gather(k_weight, ("dp", "expert"), axis=0, tiled=True),
        lax.all_gather(v_weight, ("dp", "expert"), axis=0, tiled=True),
        lax.all_gather(attn_gain, ("dp", "expert"), axis=0, tiled=True),
        lax.all_gather(mlp_gain, ("dp", "expert"), axis=0, tiled=True),
    )
    attn_full, mlp_full = (
        lax.all_gather(attn_experts, "dp", axis=1, tiled=True),
        lax.all_gather(mlp_experts, "dp", axis=1, tiled=True),
    )
    query_w = attn_full[0, :, 0, :]
    output_w = attn_full[0, :, 1, :]
    gate_w = mlp_full[0, :, 0, :]
    up_w = mlp_full[0, :, 1, :]
    down_w = mlp_full[0, :, 2, :]
    hidden = hidden_in.astype(jnp.float32)
    gain_first = gain_one.astype(jnp.float32)
    gain_second = gain_two.astype(jnp.float32)
    norm_one = rms_norm(hidden, gain_first).astype(jnp.bfloat16)
    key_raw = dot_rows(norm_one, k_full)
    key_rows = (
        rotate(key_raw.reshape(seq_len, head_count, head_dim), places)
        .reshape(seq_len, features)
        .astype(jnp.bfloat16)
    )
    val_rows = dot_rows(norm_one, v_full).astype(jnp.bfloat16)
    attn_disp, attn_comb, attn_place, attn_fill = tables(
        attn_routes, attn_gates, length, experts, capacity
    )
    mlp_disp, mlp_comb, mlp_place, mlp_fill = tables(
        mlp_routes, mlp_gates, length, experts, capacity
    )
    attn_flat = attn_disp.reshape(experts * capacity, seq_len)
    mlp_flat = mlp_disp.reshape(experts * capacity, seq_len)
    attn_comb_flat = attn_comb.reshape(experts * capacity, seq_len)
    mlp_comb_flat = mlp_comb.reshape(experts * capacity, seq_len)
    attn_slots = (
        jnp.dot(attn_flat.astype(jnp.bfloat16), norm_one, preferred_element_type=jnp.float32)
        .astype(jnp.bfloat16)
        .reshape(experts, capacity, model_width)
    )
    attn_rows = to_experts(attn_slots)
    seq_keys, seq_values, seq_routes, seq_lens = (
        lax.all_gather(key_rows, "expert", axis=0, tiled=True),
        lax.all_gather(val_rows, "expert", axis=0, tiled=True),
        lax.all_gather(attn_routes, "expert", axis=0, tiled=True),
        lax.all_gather(seq_lengths, "expert", axis=0, tiled=True),
    )

    def source_places(routes, length_one):
        outcome = tables(
            routes, jnp.zeros(routes.shape, jnp.float32), length_one, experts, capacity
        )
        return (outcome[2], outcome[3])

    all_place, all_fill = jax.vmap(source_places)(
        seq_routes.reshape(experts, seq_len, TOPK), seq_lens
    )
    here_place = lax.dynamic_index_in_dim(all_place, expert_id, 1, keepdims=False)
    here_fill = lax.dynamic_index_in_dim(all_fill, expert_id, 1, keepdims=False)
    flat_rows = attn_rows.reshape(experts * capacity, model_width)
    query_raw = dot_rows(flat_rows, query_w)
    queries = (
        rotate(query_raw.reshape(experts * capacity, head_count, head_dim), here_place.reshape(-1))
        .astype(jnp.bfloat16)
        .reshape(experts, capacity, head_count, head_dim)
    )
    key_seq = seq_keys.reshape(experts, seq_len, head_count, head_dim)
    val_seq = seq_values.reshape(experts, seq_len, head_count, head_dim)
    allowed = (
        (places[None, None, :] <= here_place[:, :, None])
        & (places[None, None, :] < seq_lens[:, None, None])
    )[:, None]
    scores = (
        jnp.einsum("schk,sthk->shct", queries, key_seq, preferred_element_type=jnp.float32)
        * score_scale
    )
    masked = jnp.where(allowed, scores, masked_value)
    row_top = jnp.max(masked, axis=-1, keepdims=True)
    shifted = jnp.exp(masked - row_top)
    row_total = jnp.sum(shifted, axis=-1, keepdims=True)
    log_total = row_top + jnp.log(row_total)
    prob_low = (shifted / row_total).astype(jnp.bfloat16)
    mixed_heads = (
        jnp.einsum("shct,sthk->schk", prob_low, val_seq, preferred_element_type=jnp.float32)
        .astype(jnp.bfloat16)
        .reshape(experts * capacity, features)
    )
    attn_result = (
        jnp.dot(mixed_heads, output_w, preferred_element_type=jnp.float32)
        .astype(jnp.bfloat16)
        .reshape(experts, capacity, model_width)
    )
    live_rows = (here_fill > 0)[:, None, :, None]
    local_peak = jnp.max(jnp.where(allowed & live_rows, scores, masked_value), axis=(0, 2, 3))
    attn_back = from_experts(attn_result)
    attn_out = dot_cols(
        attn_comb_flat, attn_back.reshape(-1, model_width).astype(jnp.float32), precision=highest
    )
    middle = hidden + attn_out
    norm_two = rms_norm(middle, gain_second).astype(jnp.bfloat16)
    mlp_slots = (
        jnp.dot(mlp_flat.astype(jnp.bfloat16), norm_two, preferred_element_type=jnp.float32)
        .astype(jnp.bfloat16)
        .reshape(experts, capacity, model_width)
    )
    mlp_rows = to_experts(mlp_slots)
    unit_rows = mlp_rows.reshape(-1, model_width)
    gate_pre = dot_rows(unit_rows, gate_w)
    up_pre = dot_rows(unit_rows, up_w)
    gate_sig = jax.nn.sigmoid(gate_pre)
    silu_val = gate_pre * gate_sig
    units = (silu_val * up_pre).astype(jnp.bfloat16)
    mlp_result = (
        jnp.dot(units, down_w, preferred_element_type=jnp.float32)
        .astype(jnp.bfloat16)
        .reshape(experts, capacity, model_width)
    )
    mlp_back = from_experts(mlp_result)
    mlp_out = dot_cols(
        mlp_comb_flat, mlp_back.reshape(-1, model_width).astype(jnp.float32), precision=highest
    )
    block_out = (keep_mask * (middle + mlp_out)).astype(jnp.bfloat16)
    grad_top = out_grad.astype(jnp.float32) * keep_mask
    grad_slots = (
        jnp.dot(mlp_comb_flat, grad_top, precision=highest)
        .astype(jnp.bfloat16)
        .reshape(experts, capacity, model_width)
    )
    grad_rows = to_experts(grad_slots)
    grad_unit_rows = grad_rows.reshape(-1, model_width)
    grad_units = dot_rows(grad_unit_rows, down_w)
    grad_gate = (grad_units * up_pre * gate_sig * (1.0 + gate_pre * (1.0 - gate_sig))).astype(
        jnp.bfloat16
    )
    grad_up = (grad_units * silu_val).astype(jnp.bfloat16)
    grad_in_rows = (
        (
            jnp.dot(grad_gate, gate_w, preferred_element_type=jnp.float32)
            + jnp.dot(grad_up, up_w, preferred_element_type=jnp.float32)
        )
        .astype(jnp.bfloat16)
        .reshape(experts, capacity, model_width)
    )
    mlp_grad = lax.psum_scatter(
        jnp.stack(
            [
                dot_cols(grad_gate, unit_rows),
                dot_cols(grad_up, unit_rows),
                dot_cols(units, grad_unit_rows),
            ],
            axis=1,
        ).astype(jnp.bfloat16),
        "dp",
        scatter_dimension=0,
        tiled=True,
    ).astype(jnp.float32)[None]
    grad_back = from_experts(grad_in_rows)
    grad_norm_two = dot_cols(
        mlp_flat, grad_back.reshape(-1, model_width).astype(jnp.float32), precision=highest
    )
    grad_mid_norm, gain_two_grad = norm_back(middle, gain_second, grad_norm_two)
    grad_middle = grad_top + grad_mid_norm
    attn_grad_slots = (
        jnp.dot(attn_comb_flat, grad_middle, precision=highest)
        .astype(jnp.bfloat16)
        .reshape(experts, capacity, model_width)
    )
    attn_grad_rows = to_experts(attn_grad_slots).reshape(-1, model_width)
    grad_mixed = dot_rows(attn_grad_rows, output_w).astype(jnp.bfloat16)
    grad_mixed_heads = grad_mixed.reshape(experts, capacity, head_count, head_dim)
    scores_again = (
        jnp.einsum("schk,sthk->shct", queries, key_seq, preferred_element_type=jnp.float32)
        * score_scale
    )
    probs_again = jnp.exp(jnp.where(allowed, scores_again, masked_value) - log_total)
    prob_again_low = probs_again.astype(jnp.bfloat16)
    grad_prob = jnp.einsum(
        "schk,sthk->shct", grad_mixed_heads, val_seq, preferred_element_type=jnp.float32
    )
    grad_scores = (
        probs_again * (grad_prob - jnp.sum(probs_again * grad_prob, axis=-1, keepdims=True))
    ).astype(jnp.bfloat16)
    grad_val_seq = jnp.einsum(
        "shct,schk->sthk", prob_again_low, grad_mixed_heads, preferred_element_type=jnp.float32
    )
    grad_queries = (
        jnp.einsum("shct,sthk->schk", grad_scores, key_seq, preferred_element_type=jnp.float32)
        * score_scale
    )
    grad_key_seq = (
        jnp.einsum("shct,schk->sthk", grad_scores, queries, preferred_element_type=jnp.float32)
        * score_scale
    )
    grad_query_raw = (
        rotate(
            grad_queries.reshape(experts * capacity, head_count, head_dim), -here_place.reshape(-1)
        )
        .reshape(experts * capacity, features)
        .astype(jnp.bfloat16)
    )
    grad_attn_slots = (
        jnp.dot(grad_query_raw, query_w, preferred_element_type=jnp.float32)
        .astype(jnp.bfloat16)
        .reshape(experts, capacity, model_width)
    )
    attn_input_back = from_experts(grad_attn_slots)
    query_part = dot_cols(grad_query_raw, flat_rows)
    output_part = dot_cols(mixed_heads, attn_grad_rows)
    attn_grad = lax.psum_scatter(
        jnp.stack([query_part, output_part], axis=1).astype(jnp.bfloat16),
        "dp",
        scatter_dimension=0,
        tiled=True,
    ).astype(jnp.float32)[None]
    key_sum, val_sum = (
        lax.psum_scatter(
            grad_key_seq.reshape(experts * seq_len, features).astype(jnp.bfloat16),
            "expert",
            scatter_dimension=0,
            tiled=True,
        ).astype(jnp.float32),
        lax.psum_scatter(
            grad_val_seq.reshape(experts * seq_len, features).astype(jnp.bfloat16),
            "expert",
            scatter_dimension=0,
            tiled=True,
        ).astype(jnp.float32),
    )
    grad_key = (
        rotate(key_sum.reshape(seq_len, head_count, head_dim), -places)
        .reshape(seq_len, features)
        .astype(jnp.bfloat16)
    )
    grad_val = val_sum.astype(jnp.bfloat16)
    grad_norm_one = dot_cols(
        attn_flat, attn_input_back.reshape(-1, model_width).astype(jnp.float32), precision=highest
    )
    grad_norm_one = (
        grad_norm_one
        + jnp.dot(grad_key, k_full, preferred_element_type=jnp.float32)
        + jnp.dot(grad_val, v_full, preferred_element_type=jnp.float32)
    )
    grad_hid_norm, gain_one_grad = norm_back(hidden, gain_first, grad_norm_one)
    grad_input = grad_middle + grad_hid_norm
    key_w_grad = dot_cols(grad_key, norm_one)
    val_w_grad = dot_cols(grad_val, norm_one)
    k_grad, v_grad, first_gain_grad, second_gain_grad = (
        lax.psum_scatter(key_w_grad, ("dp", "expert"), scatter_dimension=0, tiled=True),
        lax.psum_scatter(val_w_grad, ("dp", "expert"), scatter_dimension=0, tiled=True),
        lax.psum_scatter(gain_one_grad, ("dp", "expert"), scatter_dimension=0, tiled=True),
        lax.psum_scatter(gain_two_grad, ("dp", "expert"), scatter_dimension=0, tiled=True),
    )
    global_peak = lax.pmax(local_peak, ("dp", "expert"))
    factors = logit_limit / jnp.maximum(global_peak, logit_limit)
    roots = jnp.sqrt(factors)
    query_count = attn_experts.shape[1]
    query_index = dp_id * query_count + jnp.arange(query_count, dtype=jnp.int32)
    clipped_query = (
        attn_experts[0, :, 0, :].astype(jnp.float32)
        * head_scale(query_index, roots, head_dim)[:, None]
    ).astype(jnp.bfloat16)[None]
    key_count = k_weight.shape[0]
    device_id = dp_id * experts + expert_id
    key_index = device_id * key_count + jnp.arange(key_count, dtype=jnp.int32)
    clipped_key = (
        k_weight.astype(jnp.float32) * head_scale(key_index, roots, head_dim)[:, None]
    ).astype(jnp.bfloat16)
    return (
        block_out,
        grad_input,
        k_grad,
        v_grad,
        first_gain_grad,
        second_gain_grad,
        attn_grad,
        mlp_grad,
        clipped_query,
        clipped_key,
        factors,
    )


def solution(mesh):
    return jax.shard_map(
        on_device,
        mesh=mesh,
        in_specs=(
            P(("dp", "expert"), None),
            P(("dp", "expert")),
            P(("dp", "expert"), None),
            P(("dp", "expert"), None),
            P(("dp", "expert"), None),
            P(("dp", "expert"), None),
            P(("dp", "expert")),
            P(("dp", "expert")),
            P(("dp", "expert"), None),
            P(("dp", "expert"), None),
            P("expert", "dp", None, None),
            P("expert", "dp", None, None),
            P(),
            P(("dp", "expert"), None),
        ),
        out_specs=(
            P(("dp", "expert"), None),
            P(("dp", "expert"), None),
            P(("dp", "expert"), None),
            P(("dp", "expert"), None),
            P(("dp", "expert")),
            P(("dp", "expert")),
            P("expert", "dp", None, None),
            P("expert", "dp", None, None),
            P("expert", "dp", None),
            P(("dp", "expert"), None),
            P(),
        ),
        check_vma=False,
    )
```

profile of v0, /device:TPU:0, one launch (start us, length us, event | category | flops | bytes accessed | tf_op | source)
XLA Modules:
  0.0 2243.5 jit_solution(1476934826293097889)
XLA Ops:
  10.4 43.2 %all-reduce.6 = (bf16[2048]{0:T(1024)(128)(2,1)S(1)}, bf16[2048]{0:T(1024)(128)(2,1)S(1)}) all-reduce(bf16[2048]{0:T(1024)(128)(2,1)S(1)} %dynamic-update-slice, bf16[2048]{0:T(1024)(128)(2,1)S(1)} %dynamic-update-slice.2), channel_id=1, replica_groups=mesh['dp'=8,'expert'=4] {'dp','expert'}, use_global_device_ids=true, to_apply=%add | all-reduce | flops 4096 | bytes 16384
  54.9 36.6 %all-gather.7.cloned.1.call-done = bf16[2048,2048]{1,0:T(8,128)(2,1)} async-done(((bf16[64,2048]{1,0:T(8,128)(2,1)}), bf16[2048,2048]{1,0:T(8,128)(2,1)}) %all-gather.7.cloned.1.call-update) | async-done | bytes 8388624 | tf_op jit(solution)/shard_map/all_gather | solution.py:132
  91.5 7.3 convolution_convert_fusion.4
  99.8 70.6 %all-gather.13.cloned.1.call-done = bf16[2048,2048]{1,0:T(8,128)(2,1)} async-done(((bf16[64,2048]{1,0:T(8,128)(2,1)}), bf16[2048,2048]{1,0:T(8,128)(2,1)}) %all-gather.13.cloned.1.call-update) | async-done | bytes 8388624 | tf_op jit(solution)/shard_map/all_gather | solution.py:131
  170.4 6.3 convolution_bitcast_fusion.4
  194.5 56.0 %all-reduce.1 = s32[4]{0:T(128)S(1)} all-reduce(s32[4]{0:T(128)S(1)} %dynamic-update-slice.1), channel_id=1, replica_groups=mesh['dp'=8,'expert'=4] {'expert'}, use_global_device_ids=true, to_apply=%add.1 | all-reduce | flops 4 | bytes 32
  250.6 8.6 all_gather.33
  259.7 5.1 reduce-window.24
  271.9 18.7 all-gather.15.cloned.1.call-done
  294.1 86.6 %all-gather.11.cloned.1.call-done = bf16[1,2048,2,2048]{3,1,2,0:T(8,128)(2,1)} async-done(((bf16[1,256,2,2048]{3,1,2,0:T(8,128)(2,1)}), bf16[1,2048,2,2048]{3,1,2,0:T(8,128)(2,1)}) %all-gather.11.cloned.1.call-update) | async-done | bytes 16777232 | tf_op jit(solution)/shard_map/all_gather | solution.py:137
  380.8 8.4 slice.83
  389.2 9.5 fusion.109
  405.5 5.0 fusion.56
  416.6 20.4 fusion.12
  437.0 4.8 all-to-all-start.1
  442.8 36.6 %all-to-all-done.1 = bf16[4,96,2048]{2,1,0:T(8,128)(2,1)} async-done(((bf16[4,96,2048]{2,1,0:T(8,128)(2,1)}), bf16[4,96,2048]{2,1,0:T(8,128)(2,1)}, u32[]{:S(2)}, u32[]{:S(2)}) %all-to-all-start.1) | async-done | bytes 1572896 | tf_op jit(solution)/shard_map/all_to_all | solution.py:98
  489.2 5.2 convolution_convert_fusion.1
  494.4 31.4 %all-to-all-done.2 = bf16[4,96,2048]{2,1,0:T(8,128)(2,1)} async-done(((bf16[4,96,2048]{2,1,0:T(8,128)(2,1)}), bf16[4,96,2048]{2,1,0:T(8,128)(2,1)}, u32[]{:S(2)}, u32[]{:S(2)}) %all-to-all-start.2) | async-done | bytes 1572896 | tf_op jit(solution)/shard_map/all_to_all | solution.py:94
  530.2 164.2 %all-gather.17.cloned.1.call-done = bf16[1,5632,3,2048]{3,1,2,0:T(8,128)(2,1)} async-done(((bf16[1,704,3,2048]{3,1,2,0:T(8,128)(2,1)}), bf16[1,5632,3,2048]{3,1,2,0:T(8,128)(2,1)}) %all-gather.17.cloned.1.call-update) | async-done | bytes 69206032 | tf_op jit(solution)/shard_map/all_gather | solution.py:138
  694.4 16.2 fusion.3
  710.5 16.1 fusion.1
  726.6 24.0 %multiply_convert_fusion = (bf16[384,5632]{1,0:T(8,128)(2,1)}, bf16[384,5632]{1,0:T(8,128)(2,1)}, bf16[384,5632]{1,0:T(8,128)(2,1)}) fusion(f32[384,5632]{1,0:T(8,128)} %fusion.1, f32[384,5632]{1,0:T(8,128)} %fusion.3, bf16[384,2048]{1,0:T(8,128)(2,1)} %bitcast.30, bf16[1,5632,3,2048]{3,1,2,0:T(8,128)(2,1)} %all-gather.17.cloned.1.call-done), kind=kOutput, calls=%fused_computation.15 | convolution fusion | flops 8890810368 | bytes 54919168 | tf_op jit(solution)/shard_map/dot_general | solution.py:71
  750.6 16.5 fusion
  767.1 14.4 add_convert_fusion.1
  781.6 41.9 %all_to_all.40 = bf16[4,96,2048]{2,1,0:T(8,128)(2,1)S(1)} all-to-all(bf16[4,96,2048]{2,1,0:T(8,128)(2,1)S(1)} %bitcast.289), channel_id=1, replica_groups=mesh['dp'=8,'expert'=4] {'expert'}, dimensions={0} | all-to-all | bytes 3145728 | tf_op jit(solution)/shard_map/all_to_all | solution.py:98
  834.2 36.3 %all-to-all-done.6 = bf16[4,96,2048]{2,1,0:T(8,128)(2,1)} async-done(((bf16[4,96,2048]{2,1,0:T(8,128)(2,1)}), bf16[4,96,2048]{2,1,0:T(8,128)(2,1)}, u32[]{:S(2)}, u32[]{:S(2)}) %all-to-all-start.6) | async-done | bytes 1572896 | tf_op jit(solution)/shard_map/all_to_all | solution.py:94
  870.5 7.3 fusion.47
  916.8 7.0 convert_bitcast_fusion.3
  923.8 5.0 convert_bitcast_fusion.4
  928.9 6.8 pad_maximum_fusion.1
  936.1 18.8 convert_bitcast_fusion.1
  954.9 18.6 convert_bitcast_fusion.2
  973.5 18.9 convert_bitcast_fusion
  992.4 51.5 %pad_maximum_fusion = bf16[5632,3,2048]{2,0,1:T(8,128)(2,1)} fusion(bf16[5632,1,2048]{2,0,1:T(8,128)(2,1)} %convert_bitcast_fusion, bf16[5632,1,2048]{2,0,1:T(8,128)(2,1)} %convert_bitcast_fusion.1, bf16[5632,1,2048]{2,0,1:T(8,128)(2,1)} %convert_bitcast_fusion.2), kind=kLoop, calls=%fused_computation | loop fusion | flops 69206016 | bytes 138412032 | tf_op jit(solution)/shard_map/stack | solution.py:275
  1046.3 8.5 fusion.66
  1055.2 9.6 fusion.102
  1064.8 15.8 fusion.11
  1085.2 55.5 %pmax.7 = f32[16]{0:T(128)S(1)} all-reduce(f32[16]{0:T(128)S(1)} %copy-done.51), channel_id=1, replica_groups=mesh['dp'=8,'expert'=4] {'dp','expert'}, use_global_device_ids=true, to_apply=%region_34.35 | all-reduce | flops 16 | bytes 128 | tf_op jit(solution)/shard_map/pmax | solution.py:383
  1141.1 10.4 fusion.14
  1163.7 7.3 fusion.110
  1173.3 19.4 all-to-all-done.7
  1192.7 4.9 fusion.65
  1197.6 38.5 %all-reduce.5 = (f32[2048]{0:T(1024)S(1)}, f32[2048]{0:T(1024)S(1)}) all-reduce(f32[2048]{0:T(1024)S(1)} %get-tuple-element.70, f32[2048]{0:T(1024)S(1)} %copy-done.38), channel_id=6, replica_groups=mesh['dp'=8,'expert'=4] {'dp','expert'}, use_global_device_ids=true, to_apply=%region_27.28.clone | all-reduce | flops 4096 | bytes 32768
  1242.5 5.3 copy.184
  1247.8 256.4 %reduce-scatter.17.cloned.1.call-done = bf16[704,3,2048]{2,0,1:T(8,128)(2,1)} async-done(((bf16[5632,3,2048]{2,0,1:T(8,128)(2,1)}), bf16[704,3,2048]{2,0,1:T(8,128)(2,1)}) %reduce-scatter.17.cloned.1.call-update) | async-done | bytes 8650768 | tf_op jit(solution)/shard_map/reduce_scatter | solution.py:274
  1504.2 12.0 bitcast_convert_fusion
  1516.1 355.1 %reduce-scatter.11.cloned.1.call-done = f32[64,2048]{1,0:T(8,128)} async-done(((f32[2048,2048]{1,0:T(8,128)}), f32[64,2048]{1,0:T(8,128)}) %reduce-scatter.11.cloned.1.call-update) | async-done | bytes 524304 | tf_op jit(solution)/shard_map/reduce_scatter | solution.py:378
  1871.2 364.9 %reduce-scatter.13.cloned.1.call-done = f32[64,2048]{1,0:T(8,128)} async-done(((f32[2048,2048]{1,0:T(8,128)}), f32[64,2048]{1,0:T(8,128)}) %reduce-scatter.13.cloned.1.call-update) | async-done | bytes 524304 | tf_op jit(solution)/shard_map/reduce_scatter | solution.py:379
  (287 shorter events, 139.6 us)
Async XLA Ops:
  7.2 84.3 %all-gather.7.cloned.1.call-start = ((), (), s32[]{:S(2)}) async-start(), calls=%async_computation.14 | async-start | bytes 8650752 | tf_op jit(solution)/shard_map/all_gather | solution.py:132
  7.9 162.5 %all-gather.13.cloned.1.call-start = ((), (), s32[]{:S(2)}) async-start(), calls=%async_computation.17 | async-start | bytes 8650752 | tf_op jit(solution)/shard_map/all_gather | solution.py:131
  8.7 259.6 %all-gather.9.cloned.1.call-start = ((), (), s32[]{:S(2)}) async-start(), calls=%async_computation.15 | async-start | bytes 2621440 | tf_op jit(solution)/shard_map/all_gather | solution.py:174
  53.6 135.5 %copy-start.28 = (f32[2048]{0:T(1024)}, f32[2048]{0:T(1024)S(1)}, u32[]{:S(2)}) copy-start(f32[2048]{0:T(1024)S(1)} %convert_element_type.276) | copy-start | bytes 24580
  54.9 134.3 %copy-start.39 = (f32[128]{0:T(128)}, f32[128]{0:T(128)S(1)}, u32[]{:S(2)}) copy-start(f32[128]{0:T(128)S(1)} %add_rsqrt_fusion.1) | copy-start | bytes 1540
  54.9 115.6 %copy-start = (bf16[128,2048]{1,0:T(8,128)(2,1)S(1)}, bf16[128,2048]{1,0:T(8,128)(2,1)}, u32[]{:S(2)}) copy-start(bf16[128,2048]{1,0:T(8,128)(2,1)} %param.14) | copy-start | bytes 1572868
  98.8 191.8 %all-gather.15.cloned.1.call-start = ((), (), s32[]{:S(2)}) async-start(), calls=%async_computation.18 | async-start | bytes 2621440 | tf_op jit(solution)/shard_map/all_gather | solution.py:173
  178.8 202.0 %all-gather.11.cloned.1.call-start = ((), (), s32[]{:S(2)}) async-start(), calls=%async_computation.16 | async-start | bytes 18874368 | tf_op jit(solution)/shard_map/all_gather | solution.py:137
  181.1 513.3 %all-gather.17.cloned.1.call-start = ((), (), s32[]{:S(2)}) async-start(), calls=%async_computation.19 | async-start | bytes 77856768 | tf_op jit(solution)/shard_map/all_gather | solution.py:138
  191.0 198.3 %all-to-all-start = ((bf16[4,96,2048]{2,1,0:T(8,128)(2,1)}), bf16[4,96,2048]{2,1,0:T(8,128)(2,1)S(1)}, u32[]{:S(2)}, u32[]{:S(2)}) async-start(bf16[4,96,2048]{2,1,0:T(8,128)(2,1)} %bitcast.10), calls=%async_computation | async-start | bytes 3145728 | tf_op jit(solution)/shard_map/all_to_all | solution.py:94
  389.2 9.5 copy-start.22
  416.6 20.4 copy-start.24
  437.0 42.3 %all-to-all-start.1 = ((bf16[4,96,2048]{2,1,0:T(8,128)(2,1)}), bf16[4,96,2048]{2,1,0:T(8,128)(2,1)}, u32[]{:S(2)}, u32[]{:S(2)}) async-start(bf16[4,96,2048]{2,1,0:T(8,128)(2,1)} %bitcast.288), calls=%async_computation.1 | async-start | bytes 3145728 | tf_op jit(solution)/shard_map/all_to_all | solution.py:98
  441.9 383.5 %copy-start.34 = (f32[2048]{0:T(1024)}, f32[2048]{0:T(1024)S(1)}, u32[]{:S(2)}) copy-start(f32[2048]{0:T(1024)S(1)} %convert_element_type.301) | copy-start | bytes 24580
  482.1 343.2 %copy-start.42 = (f32[128]{0:T(128)}, f32[128]{0:T(128)S(1)}, u32[]{:S(2)}) copy-start(f32[128]{0:T(128)S(1)} %add_rsqrt_fusion) | copy-start | bytes 1540
  484.8 41.0 %all-to-all-start.2 = ((bf16[4,96,2048]{2,1,0:T(8,128)(2,1)}), bf16[4,96,2048]{2,1,0:T(8,128)(2,1)}, u32[]{:S(2)}, u32[]{:S(2)}) async-start(bf16[4,96,2048]{2,1,0:T(8,128)(2,1)} %bitcast.275), calls=%async_computation.2 | async-start | bytes 3145728 | tf_op jit(solution)/shard_map/all_to_all | solution.py:94
  489.2 336.1 %copy-start.44 = (f32[128]{0:T(128)}, f32[128]{0:T(128)S(1)}, u32[]{:S(2)}) copy-start(f32[128]{0:T(128)S(1)} %fusion.101) | copy-start | bytes 1540
  525.8 200.8 %all-to-all-start.4 = ((bf16[4,96,2048]{2,1,0:T(8,128)(2,1)}), bf16[4,96,2048]{2,1,0:T(8,128)(2,1)}, u32[]{:S(2)}, u32[]{:S(2)}) async-start(bf16[4,96,2048]{2,1,0:T(8,128)(2,1)} %bitcast.273), calls=%async_computation.4 | async-start | bytes 3145728 | tf_op jit(solution)/shard_map/all_to_all | solution.py:94
  750.6 16.5 copy-start.55
  781.6 41.9 %copy-start.3 = (f32[128,2048]{1,0:T(8,128)S(1)}, f32[128,2048]{1,0:T(8,128)}, u32[]{:S(2)}) copy-start(f32[128,2048]{1,0:T(8,128)} %copy-done.2) | copy-start | bytes 3145732
  781.6 43.7 %copy-start.14 = (bf16[128,2048]{1,0:T(8,128)(2,1)S(1)}, bf16[128,2048]{1,0:T(8,128)(2,1)}, u32[]{:S(2)}) copy-start(bf16[128,2048]{1,0:T(8,128)(2,1)} %param.27) | copy-start | bytes 1572868
  781.6 43.7 %copy-start.20 = (f32[4,96,128]{2,1,0:T(8,128)S(1)}, f32[4,96,128]{2,1,0:T(8,128)}, u32[]{:S(2)}) copy-start(f32[4,96,128]{2,1,0:T(8,128)} %get-tuple-element.79) | copy-start | bytes 589828
  825.4 8.8 copy-start.37
  829.5 41.0 %all-to-all-start.6 = ((bf16[4,96,2048]{2,1,0:T(8,128)(2,1)}), bf16[4,96,2048]{2,1,0:T(8,128)(2,1)}, u32[]{:S(2)}, u32[]{:S(2)}) async-start(bf16[4,96,2048]{2,1,0:T(8,128)(2,1)} %bitcast.274), calls=%async_computation.6 | async-start | bytes 3145728 | tf_op jit(solution)/shard_map/all_to_all | solution.py:94
  833.9 210.1 %reduce-scatter.7.cloned.1.call-start = ((), (), s32[]{:S(2)}) async-start(), calls=%async_computation.20 | async-start | bytes 2621440 | tf_op jit(solution)/shard_map/reduce_scatter | solution.py:346
  897.0 158.1 %reduce-scatter.9.cloned.1.call-start = ((), (), s32[]{:S(2)}) async-start(), calls=%async_computation.21 | async-start | bytes 2621440 | tf_op jit(solution)/shard_map/reduce_scatter | solution.py:352
  909.5 330.8 %reduce-scatter.15.cloned.1.call-start = ((), (), s32[]{:S(2)}) async-start(), calls=%async_computation.24 | async-start | bytes 18874368 | tf_op jit(solution)/shard_map/reduce_scatter | solution.py:339
  916.8 7.1 copy-start.23
  935.7 568.5 %reduce-scatter.17.cloned.1.call-start = ((), (), s32[]{:S(2)}) async-start(), calls=%async_computation.25 | async-start | bytes 77856768 | tf_op jit(solution)/shard_map/reduce_scatter | solution.py:274
  1044.0 827.3 %reduce-scatter.11.cloned.1.call-start = ((), (), s32[]{:S(2)}) async-start(), calls=%async_computation.22 | async-start | bytes 17301504 | tf_op jit(solution)/shard_map/reduce_scatter | solution.py:378
  1054.9 1181.3 %reduce-scatter.13.cloned.1.call-start = ((), (), s32[]{:S(2)}) async-start(), calls=%async_computation.23 | async-start | bytes 17301504 | tf_op jit(solution)/shard_map/reduce_scatter | solution.py:379
  1080.6 60.0 %copy-start.52 = (f32[16]{0:T(128)S(1)}, f32[16]{0:T(128)}, u32[]{:S(2)}) copy-start(f32[16]{0:T(128)} %param.26) | copy-start | bytes 196
  1080.6 70.9 %all-to-all-start.3 = ((bf16[4,96,2048]{2,1,0:T(8,128)(2,1)}), bf16[4,96,2048]{2,1,0:T(8,128)(2,1)}, u32[]{:S(2)}, u32[]{:S(2)}) async-start(bf16[4,96,2048]{2,1,0:T(8,128)(2,1)} %bitcast.286), calls=%async_computation.3 | async-start | bytes 3145728 | tf_op jit(solution)/shard_map/all_to_all | solution.py:98
  1140.6 10.8 copy-start.54
  1151.5 8.5 copy-start.4
  1151.5 8.5 copy-start.21
  1151.5 8.5 copy-start.45
  1151.5 41.2 %all-to-all-start.7 = ((bf16[4,96,2048]{2,1,0:T(8,128)(2,1)}), bf16[4,96,2048]{2,1,0:T(8,128)(2,1)}, u32[]{:S(2)}, u32[]{:S(2)}) async-start(bf16[4,96,2048]{2,1,0:T(8,128)(2,1)} %bitcast.287), calls=%async_computation.7 | async-start | bytes 3145728 | tf_op jit(solution)/shard_map/all_to_all | solution.py:98
  1156.3 7.3 copy-start.16
  1157.2 13.8 slice-start
  1163.7 7.3 slice-start.1
  1171.0 21.7 copy-start.19
  1173.2 24.3 %copy-start.38 = (f32[2048]{0:T(1024)S(1)}, f32[2048]{0:T(1024)}, u32[]{:S(2)}) copy-start(f32[2048]{0:T(1024)} %get-tuple-element.68) | copy-start | bytes 24580
  1173.2 64.0 %copy-start.11 = (f32[128,2048]{1,0:T(8,128)S(1)}, f32[128,2048]{1,0:T(8,128)}, u32[]{:S(2)}) copy-start(f32[128,2048]{1,0:T(8,128)} %copy-done.10) | copy-start | bytes 3145732
  1173.2 64.0 %copy-start.15 = (bf16[128,2048]{1,0:T(8,128)(2,1)S(1)}, bf16[128,2048]{1,0:T(8,128)(2,1)}, u32[]{:S(2)}) copy-start(bf16[128,2048]{1,0:T(8,128)(2,1)} %param.27) | copy-start | bytes 1572868
  1173.2 64.0 %copy-start.35 = (f32[2048]{0:T(1024)S(1)}, f32[2048]{0:T(1024)}, u32[]{:S(2)}) copy-start(f32[2048]{0:T(1024)} %copy-done.34) | copy-start | bytes 24580
  1173.2 64.0 %copy-start.43 = (f32[128]{0:T(128)S(1)}, f32[128]{0:T(128)}, u32[]{:S(2)}) copy-start(f32[128]{0:T(128)} %copy-done.42) | copy-start | bytes 1540
  1173.3 64.0 %copy-start.48 = (f32[128]{0:T(128)S(1)}, f32[128]{0:T(128)}, u32[]{:S(2)}) copy-start(f32[128]{0:T(128)} %copy-done.47) | copy-start | bytes 1540
  (29 other events, 81.2 us)
Sparse Core Ops, SparseCore 0:
  10.9 80.5 all-gather.6
  94.4 75.9 all-gather.12
  172.6 70.8 all-gather.8
  245.4 45.0 all-gather.14
  292.3 88.4 all-gather.10
  382.5 311.7 all-gather.16
  897.1 42.0 reduce-scatter.6
  942.2 43.1 reduce-scatter.8
  989.5 116.0 reduce-scatter.14
  1109.1 395.0 reduce-scatter.16
  1507.0 364.1 reduce-scatter.10
  1874.0 362.1 reduce-scatter.12
where the time goes:
time: 2250 us; the launch traced here: 2240 us
  waiting for transfers between devices  1480 us (66%)
  matrix products  307 us (14%)
  blocking collectives  244 us (11%)
  other arithmetic  103 us (5%)
  local copies, waits for them, and re-layouts  62.2 us (3%)
  starting transfers between devices  32.3 us (1%)
    reduce_scatter x1, waiting for transfers between devices, on_device(): lax.psum_scatter(val_w_grad, ('dp', 'expert'), scatter_dimension=0, tiled...  365 us
    reduce_scatter x1, waiting for transfers between devices, on_device(): lax.psum_scatter(key_w_grad, ('dp', 'expert'), scatter_dimension=0, tiled...  355 us
    reduce_scatter x1, waiting for transfers between devices, on_device(): lax.psum_scatter(jnp.stack([dot_cols(grad_gate, unit_rows), dot_cols(grad...  256 us
    all_gather x1, waiting for transfers between devices, on_device(): lax.all_gather(mlp_experts, 'dp', axis=1, tiled=True)  164 us
    unnamed x3, blocking collectives  138 us
    dot_general x11, matrix products, dot_cols(): lax.dot_general(left, right, (((0,), (0,)), ((), ())), preferred_element_...  99.6 us
    all_gather x1, waiting for transfers between devices, on_device(): lax.all_gather(attn_experts, 'dp', axis=1, tiled=True)  86.6 us
    dot_general x7, matrix products, dot_rows(): lax.dot_general(left, right, (((1,), (1,)), ((), ())), preferred_element_...  86.6 us
  transfers between devices with their start and end apart: 19, of which 12 were waited for; matrix products, arithmetic and copies ran while one was open for 17% of the time, Pallas kernels for 0%

commit v1 on v0

v1 whole, which is shorter than its diff:
```python
import functools

import jax
import jax.numpy as jnp
from jax import lax
from jax.experimental import pallas as pl
from jax.experimental.pallas import tpu as pltpu
from jax.sharding import PartitionSpec as P

HD = 128
eps = 1e-06
rope_base = 10000.0
masked_value = -1e30
f32 = jnp.float32
bf16 = jnp.bfloat16


def rms_inverse(values):
    return lax.rsqrt(jnp.mean(values * values, axis=-1, keepdims=True) + eps)


def norm_back(values, gain_vec, grad_out):
    inverse = rms_inverse(values)
    scaled = grad_out * gain_vec
    inner = jnp.mean(scaled * values, axis=-1, keepdims=True)
    grad_values = inverse * scaled - values * inverse * inverse * inverse * inner
    grad_gain = jnp.sum(grad_out * values * inverse, axis=0)
    return (grad_values, grad_gain)


def dot_nt(left, right):
    return lax.dot_general(left, right, (((1,), (1,)), ((), ())), preferred_element_type=f32)


def dot_nn(left, right):
    return lax.dot_general(left, right, (((1,), (0,)), ((), ())), preferred_element_type=f32)


def dot_tn(left, right):
    return lax.dot_general(left, right, (((0,), (0,)), ((), ())), preferred_element_type=f32)


def two_parts(values):
    high = values.astype(bf16)
    return high, (values - high.astype(f32)).astype(bf16)


class Plain:
    def __init__(self, mesh):
        self.pair = 1
        self.tp = mesh.shape["dp"]
        self.experts = mesh.shape["expert"]

    def labels(self):
        return jnp.arange(self.experts, dtype=jnp.int32)

    def spread(self, blocks):
        moved = lax.all_to_all(jnp.stack(blocks), "expert", 0, 0, tiled=True)
        return [lax.all_gather(one, "dp", axis=0, tiled=True) for one in moved]

    spread_small = spread

    def collect(self, parts):
        mine = [
            lax.psum_scatter(one.astype(bf16), "dp", scatter_dimension=0, tiled=True)
            for one in parts
        ]
        moved = lax.all_to_all(jnp.stack(mine), "expert", 0, 0, tiled=True)
        return [one for one in moved]

    def gather_all(self, block):
        rows = lax.all_gather(block, "expert", axis=0, tiled=False)
        return [lax.all_gather(one, "dp", axis=0, tiled=True) for one in rows]

    def reduce_all(self, parts):
        mine = [
            lax.psum_scatter(one.astype(bf16), "dp", scatter_dimension=0, tiled=True)
            for one in parts
        ]
        total = lax.psum_scatter(jnp.stack(mine), "expert", scatter_dimension=0, tiled=True)
        return total[0].astype(f32)

    def pair_gather(self, block):
        return block

    def pair_scatter(self, part):
        return part

    def column_gather(self, block):
        return lax.all_gather(block, "expert", axis=0, tiled=False)[None]

    def column_scatter(self, part):
        return lax.psum_scatter(
            part[0].astype(bf16), "expert", scatter_dimension=0, tiled=True
        )[0].astype(f32)

    def gather_vec(self, block):
        return lax.all_gather(block, ("dp", "expert"), axis=1, tiled=True)

    def sum_vec(self, vec):
        return lax.psum_scatter(vec, ("dp", "expert"), scatter_dimension=1, tiled=True)

    def max_vec(self, vec):
        return lax.pmax(vec, ("dp", "expert"))


def swap(block, mask):
    return lax.ppermute(block, "dp", [(i, i ^ mask) for i in range(8)])


def flip(block, mask):
    return lax.ppermute(block, "expert", [(i, i ^ mask) for i in range(4)])


def hop(block, pairs):
    return lax.ppermute(block, "expert", pairs)


CORE, SIDE_X, SIDE_Y = 1, 2, 4
INWARD = [(0, 1), (3, 2)]
OUTWARD = [(1, 0), (2, 3)]
MIDDLE = [(1, 2), (2, 1)]


class Paired:
    def __init__(self, mesh):
        self.pair = 2
        self.tp = 4
        self.experts = 4

    def labels(self):
        return lax.axis_index("expert") ^ jnp.arange(4, dtype=jnp.int32)

    def plane_gather(self, block):
        half = block.shape[0] // 2
        from_x = swap(block, SIDE_X)
        from_y = swap(block, SIDE_Y)
        low = swap(from_y[:half], SIDE_X)
        high = swap(from_x[half:], SIDE_Y)
        return jnp.concatenate([block, from_x, from_y, low, high], axis=0)

    def plane_reduce(self, part):
        size = part.shape[0] // 4
        half = size // 2
        own, to_x, to_y, across = (part[i * size : (i + 1) * size] for i in range(4))
        across = across.astype(bf16)
        low = swap(across[:half], SIDE_X)
        high = swap(across[half:], SIDE_Y)
        to_y = jnp.concatenate([to_y[:half] + low.astype(f32), to_y[half:]], axis=0)
        to_x = jnp.concatenate([to_x[:half], to_x[half:] + high.astype(f32)], axis=0)
        from_x = swap(to_x.astype(bf16), SIDE_X)
        from_y = swap(to_y.astype(bf16), SIDE_Y)
        return own + from_x.astype(f32) + from_y.astype(f32)

    def line_gather(self, block):
        near = flip(block, 1)
        crossed = hop(block, MIDDLE)
        second = hop(crossed, OUTWARD) + hop(near, MIDDLE)
        third = crossed + hop(second, OUTWARD)
        return [block, near, second, third]

    def line_reduce(self, parts):
        own, near, second, third = parts
        second = second + hop(third.astype(bf16), INWARD).astype(f32)
        second = second.astype(bf16)
        third = third + hop(second, INWARD).astype(f32)
        near = near + hop(second, MIDDLE).astype(f32)
        return (
            own
            + flip(near.astype(bf16), 1).astype(f32)
            + hop(third.astype(bf16), MIDDLE).astype(f32)
        )

    def reorder(self, parts):
        place = lax.axis_index("expert")
        odd = (place & 1) == 1
        parts = [jnp.where(odd, parts[i ^ 1], parts[i]) for i in range(4)]
        upper = (place & 2) == 2
        return [jnp.where(upper, parts[i ^ 2], parts[i]) for i in range(4)]

    def spread(self, blocks):
        return [
            self.plane_gather(one if r == 0 else flip(one, r)) for r, one in enumerate(blocks)
        ]

    def spread_small(self, blocks):
        moved = jnp.concatenate(
            [one if r == 0 else flip(one, r) for r, one in enumerate(blocks)], axis=0
        )
        quads = jnp.stack([moved] + [swap(moved, mask) for mask in (2, 4, 6)], axis=1)
        return [one for one in quads]

    def collect(self, parts):
        mine = [self.plane_reduce(one).astype(bf16) for one in parts]
        return [one if r == 0 else flip(one, r) for r, one in enumerate(mine)]

    def gather_all(self, block):
        return [self.plane_gather(one) for one in self.line_gather(block)]

    def reduce_all(self, parts):
        return self.line_reduce([self.plane_reduce(one) for one in parts])

    def pair_gather(self, block):
        return jnp.concatenate([block, swap(block, CORE)], axis=0)

    def pair_scatter(self, part):
        size = part.shape[0] // 2
        return part[:size] + swap(part[size:].astype(bf16), CORE).astype(f32)

    def column_gather(self, block):
        mine = jnp.stack(self.reorder(self.line_gather(block)))
        return jnp.stack([mine, swap(mine, CORE)])

    def column_scatter(self, part):
        mine = part[0] + swap(part[1].astype(bf16), CORE).astype(f32)
        return self.line_reduce(self.reorder([mine[i] for i in range(4)]))

    def butterfly(self, vec, merge):
        for mask in (CORE, SIDE_X, SIDE_Y):
            vec = merge(vec, swap(vec, mask))
        for mask in (1, 2):
            vec = merge(vec, flip(vec, mask))
        return vec

    def gather_vec(self, block):
        place = lax.axis_index("dp") * 4 + lax.axis_index("expert")
        owner = (jnp.arange(32, dtype=jnp.int32) == place)[None, :, None]
        spread = jnp.where(owner, block[:, None, :], jnp.zeros_like(block)[:, None, :])
        return self.butterfly(spread.reshape(block.shape[0], -1), jnp.add)

    def sum_vec(self, vec):
        place = lax.axis_index("dp") * 4 + lax.axis_index("expert")
        total = self.butterfly(vec, jnp.add)
        size = vec.shape[1] // 32
        return lax.dynamic_slice_in_dim(total, place * size, size, 1)

    def max_vec(self, vec):
        return self.butterfly(vec, jnp.maximum)


def turn(values, cosine, sine):
    return values * cosine + pltpu.roll(values, HD // 2, 1) * sine


def causal_mask(size):
    keys = lax.broadcasted_iota(jnp.int32, (size, size), 0)
    queries = lax.broadcasted_iota(jnp.int32, (size, size), 1)
    return keys <= queries


def slot_rows(cap, index):
    slots = lax.broadcasted_iota(jnp.int32, (cap, index.shape[1]), 0)
    return (slots == index).astype(f32).astype(bf16)


def attend_kernel(
    heads, scale, raw_ref, cos_ref, sin_ref, idx_ref, qkv_ref, mixed_ref, peak_ref
):
    size = raw_ref.shape[0]
    wide = heads * HD
    cap = mixed_ref.shape[0]
    cosine, sine = cos_ref[...], sin_ref[...]
    index = idx_ref[0]
    causal = causal_mask(size)
    mixed = []
    for h in range(heads):
        q_at = slice(h * HD, (h + 1) * HD)
        k_at = slice(wide + h * HD, wide + (h + 1) * HD)
        v_at = slice(2 * wide + h * HD, 2 * wide + (h + 1) * HD)
        query = turn(raw_ref[:, q_at], cosine, sine).astype(bf16)
        key = turn(raw_ref[:, k_at], cosine, sine).astype(bf16)
        value = raw_ref[:, v_at].astype(bf16)
        qkv_ref[:, q_at] = query
        qkv_ref[:, k_at] = key
        qkv_ref[:, v_at] = value
        scores = jnp.where(causal, dot_nt(key, query) * scale, masked_value)
        top = jnp.max(scores, axis=0, keepdims=True)
        peak_ref[0, h : h + 1, :] = jnp.where(index >= 0, top, masked_value)
        shifted = jnp.exp(scores - top)
        prob = (shifted / jnp.sum(shifted, axis=0, keepdims=True)).astype(bf16)
        mixed.append(dot_tn(prob, value).astype(bf16))
    mixed_ref[...] = dot_nn(slot_rows(cap, index), jnp.concatenate(mixed, axis=1)).astype(bf16)


def attend(raw, cosine, sine, index, cap):
    seqs, size = index.shape
    wide = raw.shape[1] // 3
    heads = wide // HD
    table = pl.BlockSpec((size, HD), lambda s: (0, 0))
    return pl.pallas_call(
        functools.partial(attend_kernel, heads, HD ** (-0.5)),
        grid=(seqs,),
        in_specs=[
            pl.BlockSpec((size, 3 * wide), lambda s: (s, 0)),
            table,
            table,
            pl.BlockSpec((1, 1, size), lambda s: (s, 0, 0)),
        ],
        out_specs=[
            pl.BlockSpec((size, 3 * wide), lambda s: (s, 0)),
            pl.BlockSpec((cap, wide), lambda s: (s, 0)),
            pl.BlockSpec((1, heads, size), lambda s: (s, 0, 0)),
        ],
        out_shape=[
            jax.ShapeDtypeStruct((seqs * size, 3 * wide), bf16),
            jax.ShapeDtypeStruct((seqs * cap, wide), bf16),
            jax.ShapeDtypeStruct((seqs, heads, size), f32),
        ],
        cost_estimate=pl.CostEstimate(
            flops=seqs * heads * size * size * HD * 6,
            bytes_accessed=seqs * size * wide * 20,
            transcendentals=seqs * heads * size * size,
        ),
        name="attend",
    )(raw, cosine, sine, index[:, None, :])


def attend_back_kernel(heads, scale, qkv_ref, gm_ref, cos_ref, sin_ref, idx_ref, out_ref):
    size = qkv_ref.shape[0]
    wide = heads * HD
    cap = gm_ref.shape[0]
    cosine, sine = cos_ref[...], -sin_ref[...]
    causal = causal_mask(size)
    grad_mixed = dot_tn(slot_rows(cap, idx_ref[0]), gm_ref[...]).astype(bf16)
    for h in range(heads):
        q_at = slice(h * HD, (h + 1) * HD)
        k_at = slice(wide + h * HD, wide + (h + 1) * HD)
        v_at = slice(2 * wide + h * HD, 2 * wide + (h + 1) * HD)
        query, key, value = qkv_ref[:, q_at], qkv_ref[:, k_at], qkv_ref[:, v_at]
        grad = grad_mixed[:, q_at]
        scores = jnp.where(causal, dot_nt(key, query) * scale, masked_value)
        top = jnp.max(scores, axis=0, keepdims=True)
        shifted = jnp.exp(scores - top)
        prob = shifted / jnp.sum(shifted, axis=0, keepdims=True)
        grad_prob = dot_nt(value, grad)
        inner = jnp.sum(prob * grad_prob, axis=0, keepdims=True)
        grad_scores = (prob * (grad_prob - inner)).astype(bf16)
        grad_query = dot_tn(grad_scores, key) * scale
        grad_key = dot_nn(grad_scores, query) * scale
        out_ref[:, q_at] = turn(grad_query, cosine, sine).astype(bf16)
        out_ref[:, k_at] = turn(grad_key, cosine, sine).astype(bf16)
        out_ref[:, v_at] = dot_nn(prob.astype(bf16), grad).astype(bf16)


def attend_back(qkv, grad_mixed, cosine, sine, index):
    seqs, size = index.shape
    cap = grad_mixed.shape[0] // seqs
    wide = qkv.shape[1] // 3
    heads = wide // HD
    table = pl.BlockSpec((size, HD), lambda s: (0, 0))
    return pl.pallas_call(
        functools.partial(attend_back_kernel, heads, HD ** (-0.5)),
        grid=(seqs,),
        in_specs=[
            pl.BlockSpec((size, 3 * wide), lambda s: (s, 0)),
            pl.BlockSpec((cap, wide), lambda s: (s, 0)),
            table,
            table,
            pl.BlockSpec((1, 1, size), lambda s: (s, 0, 0)),
        ],
        out_specs=pl.BlockSpec((size, 3 * wide), lambda s: (s, 0)),
        out_shape=jax.ShapeDtypeStruct((seqs * size, 3 * wide), bf16),
        cost_estimate=pl.CostEstimate(
            flops=seqs * heads * size * size * HD * 12,
            bytes_accessed=seqs * size * wide * 14,
            transcendentals=seqs * heads * size * size,
        ),
        name="attend_back",
    )(qkv, grad_mixed, cosine, sine, index[:, None, :])


def on_device(
    links,
    hidden_in,
    seq_lengths,
    attn_routes,
    attn_gates,
    mlp_routes,
    mlp_gates,
    attn_gain,
    mlp_gain,
    k_weight,
    v_weight,
    attn_experts,
    mlp_experts,
    logit_limit,
    out_grad,
):
    experts = links.experts
    seq_len, width = hidden_in.shape
    cap = seq_len * attn_routes.shape[1] * 3 // (2 * experts)
    shard_heads = attn_experts.shape[1] // HD
    local_heads = shard_heads * links.pair
    wide = local_heads * HD
    dp_id = lax.axis_index("dp")
    places = jnp.arange(seq_len, dtype=jnp.int32)
    live = places < seq_lengths[0]
    labels = links.labels()

    hidden_chunks = links.gather_all(hidden_in)
    gains = links.gather_vec(jnp.stack([attn_gain, mlp_gain])).astype(f32)
    gain_first, gain_second = gains[0:1], gains[1:2]
    key_value = links.column_gather(jnp.concatenate([k_weight, v_weight], axis=0))
    key_rows = k_weight.shape[0]
    k_local = key_value[:, :, :key_rows].reshape(wide, width)
    v_local = key_value[:, :, key_rows:].reshape(wide, width)
    q_local = links.pair_gather(attn_experts[0, :, 0, :])
    o_local = links.pair_gather(attn_experts[0, :, 1, :])
    qkv_w = jnp.concatenate([q_local, k_local, v_local], axis=0)
    gate_w = links.pair_gather(mlp_experts[0, :, 0, :])
    up_w = links.pair_gather(mlp_experts[0, :, 1, :])
    down_w = links.pair_gather(mlp_experts[0, :, 2, :])

    before = (places[:, None] < places[None, :]).astype(bf16)

    def slot_tables(routes, gates):
        first, second = routes[:, 0][None, :], routes[:, 1][None, :]
        names = labels[:, None]
        named = (first == names) | (second == names)
        rank = dot_nn(named.astype(bf16), before).astype(jnp.int32)
        index = jnp.where(named & live[None, :], rank, -1)
        weight = jnp.where(first == names, gates[:, 0][None, :], 0.0) + jnp.where(
            second == names, gates[:, 1][None, :], 0.0
        )
        slot_ids = jnp.arange(cap, dtype=jnp.int32)[None, :, None]
        taken = slot_ids == index[:, None, :]
        combine = jnp.where(taken, weight[:, None, :], 0.0)
        slot_gate = jnp.sum(combine, axis=2)[:, :, None]
        taken = taken.astype(bf16)
        return index, taken, slot_gate, two_parts(combine)

    attn_index, attn_taken, attn_slot_gate, attn_combine = slot_tables(attn_routes, attn_gates)
    _, mlp_taken, mlp_slot_gate, mlp_combine = slot_tables(mlp_routes, mlp_gates)
    index_chunks = links.spread_small([attn_index[r : r + 1] for r in range(experts)])

    def combine_rows(parts, rows):
        rows = jnp.concatenate(rows, axis=0)
        flat = [one.reshape(experts * cap, seq_len) for one in parts]
        return sum(dot_tn(one, rows) for one in flat)

    grad_slots = [
        (mlp_slot_gate[r] * dot_nn(mlp_taken[r], out_grad)).astype(bf16) for r in range(experts)
    ]
    grad_rows = links.spread(grad_slots)

    half = HD // 2
    freqs = rope_base ** (-jnp.arange(half, dtype=f32) / half)
    angles = places.astype(f32)[:, None] * freqs[None, :]
    cosine = jnp.concatenate([jnp.cos(angles), jnp.cos(angles)], axis=1)
    sine = jnp.concatenate([-jnp.sin(angles), jnp.sin(angles)], axis=1)

    normed, turned, mixed_rows, peaks, attn_parts = [], [], [], [], []
    for r in range(experts):
        values = hidden_chunks[r].astype(f32)
        norm_one = (values * rms_inverse(values) * gain_first).astype(bf16)
        raw = dot_nt(norm_one, qkv_w)
        qkv, mixed, peak = attend(raw, cosine, sine, index_chunks[r], cap)
        normed.append(norm_one)
        turned.append(qkv)
        mixed_rows.append(mixed)
        peaks.append(jnp.max(peak, axis=(0, 2)))
        attn_parts.append(dot_nn(mixed, o_local))
    attn_back = links.collect(attn_parts)
    hidden = hidden_in.astype(f32)
    middle = hidden + combine_rows(attn_combine, attn_back)
    norm_two = (middle * rms_inverse(middle) * gain_second).astype(bf16)
    mlp_slots = [dot_nn(mlp_taken[r], norm_two).astype(bf16) for r in range(experts)]
    mlp_rows = links.spread(mlp_slots)

    units_all, gate_all, up_all, mlp_parts, grad_parts = [], [], [], [], []
    for r in range(experts):
        grad_units = dot_nt(grad_rows[r], down_w)
        gate_pre = dot_nt(mlp_rows[r], gate_w)
        up_pre = dot_nt(mlp_rows[r], up_w)
        gate_sig = jax.nn.sigmoid(gate_pre)
        silu_val = gate_pre * gate_sig
        units = (silu_val * up_pre).astype(bf16)
        grad_gate = (grad_units * up_pre * gate_sig * (1.0 + gate_pre * (1.0 - gate_sig))).astype(
            bf16
        )
        grad_up = (grad_units * silu_val).astype(bf16)
        grad_parts.append(dot_nn(grad_gate, gate_w) + dot_nn(grad_up, up_w))
        mlp_parts.append(dot_nn(units, down_w))
        units_all.append(units)
        gate_all.append(grad_gate)
        up_all.append(grad_up)
    grad_back = links.collect(grad_parts)
    mlp_back = links.collect(mlp_parts)

    keep = live.astype(f32)[:, None]
    block_out = (keep * (middle + combine_rows(mlp_combine, mlp_back))).astype(bf16)
    grad_norm_two = combine_rows([mlp_taken], grad_back)
    grad_mid_norm, gain_two_grad = norm_back(middle, gain_second, grad_norm_two)
    grad_middle = out_grad.astype(f32) * keep + grad_mid_norm
    mid_high, mid_low = two_parts(grad_middle)
    attn_grad_slots = [
        (
            attn_slot_gate[r]
            * (dot_nn(attn_taken[r], mid_high) + dot_nn(attn_taken[r], mid_low))
        ).astype(bf16)
        for r in range(experts)
    ]
    attn_grad_rows = links.spread(attn_grad_slots)

    grads_all, norm_parts = [], []
    for r in range(experts):
        grad_mixed = dot_nt(attn_grad_rows[r], o_local).astype(bf16)
        grads = attend_back(turned[r], grad_mixed, cosine, sine, index_chunks[r])
        norm_parts.append(dot_nn(grads, qkv_w))
        grads_all.append(grads)
    grad_norm_one = links.reduce_all(norm_parts)

    def joined(parts):
        return jnp.concatenate(parts, axis=0)

    rows_all, grad_rows_all = joined(mlp_rows), joined(grad_rows)
    mlp_grad = jnp.stack(
        [
            links.pair_scatter(dot_tn(joined(gate_all), rows_all)),
            links.pair_scatter(dot_tn(joined(up_all), rows_all)),
            links.pair_scatter(dot_tn(joined(units_all), grad_rows_all)),
        ],
        axis=1,
    )[None]
    qkv_grad = dot_tn(joined(grads_all), joined(normed))
    attn_grad = jnp.stack(
        [
            links.pair_scatter(qkv_grad[:wide]),
            links.pair_scatter(dot_tn(joined(mixed_rows), joined(attn_grad_rows))),
        ],
        axis=1,
    )[None]
    column = (links.pair, experts, key_rows, width)
    kv_grad = links.column_scatter(
        jnp.concatenate(
            [qkv_grad[wide : 2 * wide].reshape(column), qkv_grad[2 * wide :].reshape(column)],
            axis=2,
        )
    )
    k_grad, v_grad = kv_grad[:key_rows], kv_grad[key_rows:]

    grad_hid_norm, gain_one_grad = norm_back(hidden, gain_first, grad_norm_one)
    grad_input = grad_middle + grad_hid_norm
    gain_grads = links.sum_vec(jnp.stack([gain_one_grad, gain_two_grad]))

    head_count = logit_limit.shape[0]
    local_peak = jnp.max(jnp.stack(peaks), axis=0)
    owners = jnp.concatenate(
        [(dp_id ^ i) * shard_heads + jnp.arange(shard_heads) for i in range(links.pair)]
    )
    spots = owners[:, None] == jnp.arange(head_count)[None, :]
    peak_vec = jnp.max(jnp.where(spots, local_peak[:, None], masked_value), axis=0)
    factors = logit_limit / jnp.maximum(links.max_vec(peak_vec), logit_limit)
    roots = jnp.sqrt(factors)

    def row_scale(first_row, count):
        rows = first_row + jnp.arange(count, dtype=jnp.int32)
        heads = (rows // HD)[:, None] == jnp.arange(head_count)[None, :]
        return jnp.sum(jnp.where(heads, roots[None, :], 0.0), axis=1, keepdims=True)

    query_count = attn_experts.shape[1]
    clipped_query = (
        attn_experts[0, :, 0, :].astype(f32) * row_scale(dp_id * query_count, query_count)
    ).astype(bf16)[None]
    device_id = dp_id * experts + lax.axis_index("expert")
    clipped_key = (
        k_weight.astype(f32) * row_scale(device_id * key_rows, key_rows)
    ).astype(bf16)
    return (
        block_out,
        grad_input,
        k_grad,
        v_grad,
        gain_grads[0],
        gain_grads[1],
        attn_grad,
        mlp_grad,
        clipped_query,
        clipped_key,
        factors,
    )


def solution(mesh):
    paired = mesh.shape["dp"] == 8 and mesh.shape["expert"] == 4
    links = Paired(mesh) if paired else Plain(mesh)
    rows = P(("dp", "expert"), None)
    vec = P(("dp", "expert"))
    weights = P("expert", "dp", None, None)
    return jax.shard_map(
        functools.partial(on_device, links),
        mesh=mesh,
        in_specs=(rows, vec, rows, rows, rows, rows, vec, vec, rows, rows)
        + (weights, weights, P(), rows),
        out_specs=(rows, rows, rows, rows, vec, vec, weights, weights)
        + (P("expert", "dp", None), rows, P()),
        check_vma=False,
    )
```

time: 2250 us -> 1190 us (0.53)
  waiting for transfers between devices: 1480 us -> 368 us
  blocking collectives: 244 us -> 0 us
  starting transfers between devices: 32.3 us -> 265 us
  Pallas kernels: 0 us -> 61.4 us
  local copies, waits for them, and re-layouts: 62.2 us -> 97.9 us
    reduce_scatter x6 -> x0, waiting for transfers between devices: 976 us -> none  [the longest x1 365 us: on_device(): lax.psum_scatter(val_w_grad, ('dp', 'expert'), scatter_dimension=0, tiled...]
    all_gather x6 -> x0, waiting for transfers between devices: 377 us -> none  [the longest x1 164 us: on_device(): lax.all_gather(mlp_experts, 'dp', axis=1, tiled=True)]
    ppermute x0 -> x199, waiting for transfers between devices: none -> 368 us  [the longest x152 206 us: swap(): return lax.ppermute(block, 'dp', [(i, i ^ mask) for i in range(8)])]
    ppermute x0 -> x199, starting transfers between devices: none -> 265 us  [the longest x152 144 us: swap(): return lax.ppermute(block, 'dp', [(i, i ^ mask) for i in range(8)])]
    unnamed x3 -> x0, blocking collectives: 138 us -> none
    all_to_all x7 -> x0, waiting for transfers between devices: 124 us -> none  [the longest x4 67.8 us: to_experts(): lax.all_to_all(slots, 'expert', split_axis=0, concat_axis=0, tiled=True)]
    pallas_call x0 -> x8, Pallas kernels: none -> 61.4 us  [the longest x4 30.8 us: attend(): pl.pallas_call(functools.partial(attend_kernel, heads, HD ** (-0.5)), gri...]
    pmax x1 -> x0, blocking collectives: 55.5 us -> none  [on_device(): global_peak = lax.pmax(local_peak, ('dp', 'expert'))]
  transfers between devices with their start and end apart: 19 -> 199, of which waited for: 12 -> 74; matrix products, arithmetic and copies ran while one was open for 17% -> 40% of each run, Pallas kernels for 0% -> 5%
where the time goes in v1:
time: 1190 us; the launch traced here: 1180 us
  waiting for transfers between devices  368 us (31%)
  matrix products  291 us (24%)
  starting transfers between devices  265 us (22%)
  local copies, waits for them, and re-layouts  97.9 us (8%)
  other arithmetic  95.9 us (8%)
  Pallas kernels  61.4 us (5%)
    ppermute x152, waiting for transfers between devices, swap(): return lax.ppermute(block, 'dp', [(i, i ^ mask) for i in range(8)])  206 us
    ppermute x152, starting transfers between devices, swap(): return lax.ppermute(block, 'dp', [(i, i ^ mask) for i in range(8)])  144 us
    dot_general x20, matrix products, dot_nt(): lax.dot_general(left, right, (((1,), (1,)), ((), ())), preferred_element_...  110 us
    dot_general x38, matrix products, dot_nn(): lax.dot_general(left, right, (((1,), (0,)), ((), ())), preferred_element_...  107 us
    ppermute x31, waiting for transfers between devices, flip(): return lax.ppermute(block, 'expert', [(i, i ^ mask) for i in range(4)])  105 us
    ppermute x31, starting transfers between devices, flip(): return lax.ppermute(block, 'expert', [(i, i ^ mask) for i in range(4)])  95.1 us
    dot_general x10, matrix products, dot_tn(): lax.dot_general(left, right, (((0,), (0,)), ((), ())), preferred_element_...  74.1 us
    ppermute x16, waiting for transfers between devices, hop(): return lax.ppermute(block, 'expert', pairs)  58 us
  transfers between devices with their start and end apart: 199, of which 74 were waited for; matrix products, arithmetic and copies ran while one was open for 40% of the time, Pallas kernels for 5%

profile of v1, /device:TPU:0, one launch (start us, length us, event | category | flops | bytes accessed | tf_op | source)
XLA Modules:
  0.0 1184.5 jit_solution(13926506333785884358)
XLA Ops:
  53.3 8.2 collective-permute-done.7
  111.8 8.8 collective-permute-start.12
  164.2 9.1 collective-permute-done.38
  176.1 10.0 collective-permute-done.11
  189.8 22.1 %collective-permute-done.14 = bf16[128,2048]{1,0:T(8,128)(2,1)S(1)} collective-permute-done((bf16[128,2048]{1,0:T(8,128)(2,1)S(1)}, bf16[128,2048]{1,0:T(8,128)(2,1)S(1)}, u32[]{:S(2)}, u32[]{:S(2)}) %collective-permute-start.14) | collective-permute-done | bytes 524320 | tf_op jit(solution)/shard_map/ppermute | solution.py:116
  215.1 8.9 collective-permute-done.40
  236.1 6.4 collective-permute-done.51
  271.2 11.4 pad_maximum_fusion
  292.9 7.5 attend.7
  301.8 7.7 attend.6
  310.8 8.5 fusion.280.raw_ref
  319.4 7.5 attend.5
  328.2 8.5 fusion.279.raw_ref
  336.8 7.9 attend.4
  391.4 13.0 %collective-permute-done.35 = bf16[96,2048]{1,0:T(8,128)(2,1)S(1)} collective-permute-done((bf16[96,2048]{1,0:T(8,128)(2,1)S(1)}, bf16[96,2048]{1,0:T(8,128)(2,1)S(1)}, u32[]{:S(2)}, u32[]{:S(2)}) %collective-permute-start.35) | collective-permute-done | bytes 393248 | tf_op jit(solution)/shard_map/ppermute | solution.py:108
  406.8 7.1 collective-permute-done.47
  432.6 8.6 collective-permute-done.36
  441.2 11.1 collective-permute-done.48
  481.7 7.6 collective-permute-done.80
  552.0 6.8 fusion.231
  558.8 7.8 multiply_convert_fusion.1
  571.8 7.1 fusion.271
  587.4 7.1 multiply_convert_fusion.3
  600.1 7.0 fusion.272
  607.9 6.8 fusion.233
  614.7 9.2 multiply_convert_fusion.5
  624.0 13.5 %fusion.18 = f32[1408,2048]{1,0:T(8,128)} fusion(bf16[1536,2048]{1,0:T(8,128)(2,1)S(1)} %bitcast.315, bf16[384,1408]{1,0:T(8,128)(2,1)S(1)} %get-tuple-element.103, bf16[384,1408]{1,0:T(8,128)(2,1)S(1)} %get-tuple-element.100, bf16[384,1408]{1,0:T(8,128)(2,1)} %get-tuple-element.97, bf16[384,1408]{1,0:T(8,128)(2,1)S(1)} %get-tuple-element.94), kind=kOutput, calls=%fused_computation.39 | convolution fusion | flops 8875671552 | bytes 22151168 | tf_op jit(solution)/shard_map/dot_general | solution.py:40
  637.5 13.0 %fusion.26 = f32[1408,2048]{1,0:T(8,128)S(1)} fusion(bf16[1536,2048]{1,0:T(8,128)(2,1)} %get-tuple-element.288, bf16[384,1408]{1,0:T(8,128)(2,1)} %copy-done.90, bf16[384,1408]{1,0:T(8,128)(2,1)} %copy-done.91, bf16[384,1408]{1,0:T(8,128)(2,1)} %get-tuple-element.98, bf16[384,1408]{1,0:T(8,128)(2,1)} %copy-done.89), kind=kOutput, calls=%fused_computation.47 | convolution fusion | flops 8875671552 | bytes 22151168 | tf_op jit(solution)/shard_map/dot_general | solution.py:40
  650.6 8.6 fusion.229
  659.2 7.3 fusion.273
  677.4 15.1 %fusion.34 = f32[1408,2048]{1,0:T(8,128)} fusion(bf16[1536,2048]{1,0:T(8,128)(2,1)} %get-tuple-element.304, bf16[384,1408]{1,0:T(8,128)(2,1)} %get-tuple-element.105, bf16[384,1408]{1,0:T(8,128)(2,1)} %get-tuple-element.102, bf16[384,1408]{1,0:T(8,128)(2,1)} %get-tuple-element.99, bf16[384,1408]{1,0:T(8,128)(2,1)} %copy-done.83), kind=kOutput, calls=%fused_computation.55 | convolution fusion | flops 8875671552 | bytes 22151168 | tf_op jit(solution)/shard_map/dot_general | solution.py:40
  776.1 12.4 %collective-permute-start.117 = (bf16[96,2048]{1,0:T(8,128)(2,1)S(1)}, bf16[96,2048]{1,0:T(8,128)(2,1)S(1)}, u32[]{:S(2)}, u32[]{:S(2)}) collective-permute-start(bf16[96,2048]{1,0:T(8,128)(2,1)S(1)} %fusion.129), channel_id=1, source_target_pairs={{0,1},{1,0},{2,3},{3,2},{4,5},{5,4},{6,7},{7,6},{8,9},{9,8},{10,11... | collective-permute-start | bytes 1179656 | tf_op jit(solution)/shard_map/ppermute | solution.py:112
  801.9 29.1 %collective-permute-done.127 = bf16[96,2048]{1,0:T(8,128)(2,1)S(1)} collective-permute-done((bf16[96,2048]{1,0:T(8,128)(2,1)S(1)}, bf16[96,2048]{1,0:T(8,128)(2,1)S(1)}, u32[]{:S(2)}, u32[]{:S(2)}) %collective-permute-start.127) | collective-permute-done | bytes 393248 | tf_op jit(solution)/shard_map/ppermute | solution.py:112
  849.3 8.4 collective-permute-done.155
  869.2 7.7 attend_back.4
  914.2 7.6 attend_back.5
  931.8 7.5 attend_back.6
  947.2 7.9 attend_back.7
  955.1 23.0 %fusion = f32[1536,2048]{1,0:T(8,128)} fusion(bf16[512,2048]{1,0:T(8,128)(2,1)} %copy-done.22, bf16[512,2048]{1,0:T(8,128)(2,1)} %copy-done.21, bf16[512,2048]{1,0:T(8,128)(2,1)} %get-tuple-element.343, bf16[512,2048]{1,0:T(8,128)(2,1)S(1)} %copy-done.20, bf16[512,1536]{1,0:T(8,128)(2,1)} %attend_back.7, bf16[512,1536]{1,0:T(8,128)(2,1)} %attend_back.6, ...), kind=kOutput, calls=%fused_computation.1 | convolution fusion | flops 12943622144 | bytes 27262976 | tf_op jit(solution)/shard_map/dot_general | solution.py:40
  985.1 7.8 fusion.277
  1038.9 8.2 collective-permute-done.172
  1065.2 7.2 fusion.16
  1072.4 10.0 maximum_bitcast_fusion
  1090.2 10.0 collective-permute-done.176
  1103.8 18.4 %collective-permute-start.175 = (bf16[128,2048]{1,0:T(8,128)(2,1)S(1)}, bf16[128,2048]{1,0:T(8,128)(2,1)S(1)}, u32[]{:S(2)}, u32[]{:S(2)}) collective-permute-start(bf16[128,2048]{1,0:T(8,128)(2,1)S(1)} %fusion.116), channel_id=1, source_target_pairs={{0,1},{1,0},{2,3},{3,2},{4,5},{5,4},{6,7},{7,6},{8,9},{9,8},{10,11... | collective-permute-start | bytes 1572872 | tf_op jit(solution)/shard_map/ppermute | solution.py:112
  1123.2 9.3 collective-permute-done.175
  1143.7 6.8 collective-permute-done.179
  1173.4 9.4 collective-permute-done.181
  (924 shorter events, 699.8 us)
Async XLA Ops:
  2.4 33.1 %collective-permute-start.18 = (s32[1,128]{1,0:T(1,128)S(1)}, s32[1,128]{1,0:T(1,128)S(1)}, u32[]{:S(2)}, u32[]{:S(2)}) collective-permute-start(s32[1,128]{1,0:T(1,128)S(1)} %get-tuple-element.359), channel_id=1, source_target_pairs={{0,3},{1,2},{2,1},{3,0},{4,7},{5,6},{6,5},{7,4},{8,11},{9,10},{10,... | collective-permute-start | bytes 1544 | tf_op jit(solution)/shard_map/ppermute | solution.py:112
  7.4 28.1 %collective-permute-start.17 = (s32[1,128]{1,0:T(1,128)S(1)}, s32[1,128]{1,0:T(1,128)S(1)}, u32[]{:S(2)}, u32[]{:S(2)}) collective-permute-start(s32[1,128]{1,0:T(1,128)S(1)} %get-tuple-element.360), channel_id=1, source_target_pairs={{0,2},{1,3},{2,0},{3,1},{4,6},{5,7},{6,4},{7,5},{8,10},{9,11},{10,... | collective-permute-start | bytes 1544 | tf_op jit(solution)/shard_map/ppermute | solution.py:112
  7.4 28.1 %collective-permute-start.16 = (s32[1,128]{1,0:T(1,128)S(1)}, s32[1,128]{1,0:T(1,128)S(1)}, u32[]{:S(2)}, u32[]{:S(2)}) collective-permute-start(s32[1,128]{1,0:T(1,128)S(1)} %get-tuple-element.361), channel_id=1, source_target_pairs={{0,1},{1,0},{2,3},{3,2},{4,5},{5,4},{6,7},{7,6},{8,9},{9,8},{10,11... | collective-permute-start | bytes 1544 | tf_op jit(solution)/shard_map/ppermute | solution.py:112
  9.1 68.5 %collective-permute-start.1 = (bf16[128,2048]{1,0:T(8,128)(2,1)}, bf16[128,2048]{1,0:T(8,128)(2,1)}, u32[]{:S(2)}, u32[]{:S(2)}) collective-permute-start(bf16[128,2048]{1,0:T(8,128)(2,1)} %param.14), channel_id=1, source_target_pairs={{0,16},{4,20},{8,24},{12,28},{16,0},{20,4},{24,8},{28,12},{1,17},{... | collective-permute-start | bytes 1572872 | tf_op jit(solution)/shard_map/ppermute | solution.py:108
  47.5 34.1 %collective-permute-start = (bf16[128,2048]{1,0:T(8,128)(2,1)}, bf16[128,2048]{1,0:T(8,128)(2,1)S(1)}, u32[]{:S(2)}, u32[]{:S(2)}) collective-permute-start(bf16[128,2048]{1,0:T(8,128)(2,1)} %param.14), channel_id=1, source_target_pairs={{0,8},{4,12},{8,0},{12,4},{16,24},{20,28},{24,16},{28,20},{1,9},{5... | collective-permute-start | bytes 1572872 | tf_op jit(solution)/shard_map/ppermute | solution.py:108
  48.8 35.9 %collective-permute-start.27 = (bf16[128,2048]{1,0:T(8,128)(2,1)}, bf16[128,2048]{1,0:T(8,128)(2,1)S(1)}, u32[]{:S(2)}, u32[]{:S(2)}) collective-permute-start(bf16[128,2048]{1,0:T(8,128)(2,1)} %param.14), channel_id=1, source_target_pairs={{0,1},{1,0},{2,3},{3,2},{4,5},{5,4},{6,7},{7,6},{8,9},{9,8},{10,11... | collective-permute-start | bytes 1572872 | tf_op jit(solution)/shard_map/ppermute | solution.py:112
  106.2 45.4 %collective-permute-start.37 = (bf16[128,2048]{1,0:T(8,128)(2,1)S(1)}, bf16[128,2048]{1,0:T(8,128)(2,1)S(1)}, u32[]{:S(2)}, u32[]{:S(2)}) collective-permute-start(bf16[128,2048]{1,0:T(8,128)(2,1)S(1)} %copy-done.7), channel_id=1, source_target_pairs={{1,2},{2,1},{5,6},{6,5},{9,10},{10,9},{13,14},{14,13},{17,18},{18,... | collective-permute-start | bytes 1572872 | tf_op jit(solution)/shard_map/ppermute | solution.py:116
  111.8 45.9 %collective-permute-start.12 = (bf16[128,2048]{1,0:T(8,128)(2,1)}, bf16[128,2048]{1,0:T(8,128)(2,1)S(1)}, u32[]{:S(2)}, u32[]{:S(2)}) collective-permute-start(bf16[128,2048]{1,0:T(8,128)(2,1)} %constant_dynamic-update-slice_fusion.5), channel_id=1, source_target_pairs={{0,1},{1,0},{2,3},{3,2},{4,5},{5,4},{6,7},{7,6},{8,9},{9,8},{10,11... | collective-permute-start | bytes 1572872 | tf_op jit(solution)/shard_map/ppermute | solution.py:112
  120.6 33.5 %collective-permute-start.29 = (bf16[128,2048]{1,0:T(8,128)(2,1)S(1)}, bf16[128,2048]{1,0:T(8,128)(2,1)S(1)}, u32[]{:S(2)}, u32[]{:S(2)}) collective-permute-start(bf16[128,2048]{1,0:T(8,128)(2,1)S(1)} %collective-permute-done.27), channel_id=1, source_target_pairs={{0,16},{4,20},{8,24},{12,28},{16,0},{20,4},{24,8},{28,12},{1,17},{... | collective-permute-start | bytes 1572872 | tf_op jit(solution)/shard_map/ppermute | solution.py:108
  122.3 30.0 %collective-permute-start.131 = (bf16[48,2048]{1,0:T(8,128)(2,1)S(1)}, bf16[48,2048]{1,0:T(8,128)(2,1)S(1)}, u32[]{:S(2)}, u32[]{:S(2)}) collective-permute-start(bf16[48,2048]{1,0:T(8,128)(2,1)S(1)} %slice.1137), channel_id=1, source_target_pairs={{0,8},{4,12},{8,0},{12,4},{16,24},{20,28},{24,16},{28,20},{1,9},{5... | collective-permute-start | bytes 589832 | tf_op jit(solution)/shard_map/ppermute | solution.py:108
  157.7 113.5 %collective-permute-start.9 = (bf16[256,2048]{1,0:T(8,128)(2,1)S(1)}, bf16[256,2048]{1,0:T(8,128)(2,1)S(1)}, u32[]{:S(2)}, u32[]{:S(2)}) collective-permute-start(bf16[256,2048]{1,0:T(8,128)(2,1)S(1)} %bitcast.299), channel_id=1, source_target_pairs={{0,4},{4,0},{8,12},{12,8},{16,20},{20,16},{24,28},{28,24},{1,5},{5... | collective-permute-start | bytes 3145736 | tf_op jit(solution)/shard_map/ppermute | solution.py:108
  176.0 171.5 %collective-permute-start.22 = (bf16[256,2048]{1,0:T(8,128)(2,1)S(1)}, bf16[256,2048]{1,0:T(8,128)(2,1)}, u32[]{:S(2)}, u32[]{:S(2)}) collective-permute-start(bf16[256,2048]{1,0:T(8,128)(2,1)S(1)} %bitcast.286), channel_id=1, source_target_pairs={{0,4},{4,0},{8,12},{12,8},{16,20},{20,16},{24,28},{28,24},{1,5},{5... | collective-permute-start | bytes 3145736 | tf_op jit(solution)/shard_map/ppermute | solution.py:108
  186.0 38.8 %collective-permute-start.49 = (bf16[128,2048]{1,0:T(8,128)(2,1)S(1)}, bf16[128,2048]{1,0:T(8,128)(2,1)S(1)}, u32[]{:S(2)}, u32[]{:S(2)}) collective-permute-start(bf16[128,2048]{1,0:T(8,128)(2,1)S(1)} %get-tuple-element.82), channel_id=1, source_target_pairs={{1,0},{2,3},{5,4},{6,7},{9,8},{10,11},{13,12},{14,15},{17,16},{18,... | collective-permute-start | bytes 1572872 | tf_op jit(solution)/shard_map/ppermute | solution.py:116
  187.5 27.5 %collective-permute-start.41 = (bf16[128,2048]{1,0:T(8,128)(2,1)S(1)}, bf16[128,2048]{1,0:T(8,128)(2,1)S(1)}, u32[]{:S(2)}, u32[]{:S(2)}) collective-permute-start(bf16[128,2048]{1,0:T(8,128)(2,1)S(1)} %get-tuple-element.82), channel_id=1, source_target_pairs={{0,16},{4,20},{8,24},{12,28},{16,0},{20,4},{24,8},{28,12},{1,17},{... | collective-permute-start | bytes 1572872 | tf_op jit(solution)/shard_map/ppermute | solution.py:108
  215.0 39.4 %collective-permute-start.65 = (bf16[704,2048]{1,0:T(8,128)(2,1)S(1)}, bf16[704,2048]{1,0:T(8,128)(2,1)S(1)}, u32[]{:S(2)}, u32[]{:S(2)}) collective-permute-start(bf16[704,2048]{1,0:T(8,128)(2,1)S(1)} %copy-done.16), channel_id=1, source_target_pairs={{0,4},{4,0},{8,12},{12,8},{16,20},{20,16},{24,28},{28,24},{1,5},{5... | collective-permute-start | bytes 8650760 | tf_op jit(solution)/shard_map/ppermute | solution.py:108
  249.0 246.5 %collective-permute-start.63 = (bf16[704,2048]{1,0:T(8,128)(2,1)}, bf16[704,2048]{1,0:T(8,128)(2,1)}, u32[]{:S(2)}, u32[]{:S(2)}) collective-permute-start(bf16[704,2048]{1,0:T(8,128)(2,1)} %get-tuple-element.92), channel_id=1, source_target_pairs={{0,4},{4,0},{8,12},{12,8},{16,20},{20,16},{24,28},{28,24},{1,5},{5... | collective-permute-start | bytes 8650760 | tf_op jit(solution)/shard_map/ppermute | solution.py:108
  250.5 230.3 %collective-permute-start.64 = (bf16[704,2048]{1,0:T(8,128)(2,1)}, bf16[704,2048]{1,0:T(8,128)(2,1)}, u32[]{:S(2)}, u32[]{:S(2)}) collective-permute-start(bf16[704,2048]{1,0:T(8,128)(2,1)} %get-tuple-element.93), channel_id=1, source_target_pairs={{0,4},{4,0},{8,12},{12,8},{16,20},{20,16},{24,28},{28,24},{1,5},{5... | collective-permute-start | bytes 8650760 | tf_op jit(solution)/shard_map/ppermute | solution.py:108
  385.7 42.8 %collective-permute-start.26 = (bf16[96,2048]{1,0:T(8,128)(2,1)S(1)}, bf16[96,2048]{1,0:T(8,128)(2,1)S(1)}, u32[]{:S(2)}, u32[]{:S(2)}) collective-permute-start(bf16[96,2048]{1,0:T(8,128)(2,1)S(1)} %pad_maximum_fusion.19), channel_id=1, source_target_pairs={{0,16},{4,20},{8,24},{12,28},{16,0},{20,4},{24,8},{28,12},{1,17},{... | collective-permute-start | bytes 1179656 | tf_op jit(solution)/shard_map/ppermute | solution.py:108
  461.7 27.5 %collective-permute-start.80 = (bf16[96,2048]{1,0:T(8,128)(2,1)S(1)}, bf16[96,2048]{1,0:T(8,128)(2,1)S(1)}, u32[]{:S(2)}, u32[]{:S(2)}) collective-permute-start(bf16[96,2048]{1,0:T(8,128)(2,1)S(1)} %convolution_convert_fusion.1), channel_id=1, source_target_pairs={{0,2},{1,3},{2,0},{3,1},{4,6},{5,7},{6,4},{7,5},{8,10},{9,11},{10,... | collective-permute-start | bytes 1179656 | tf_op jit(solution)/shard_map/ppermute | solution.py:112
  479.6 37.0 %collective-permute-start.72 = (bf16[96,2048]{1,0:T(8,128)(2,1)S(1)}, bf16[96,2048]{1,0:T(8,128)(2,1)S(1)}, u32[]{:S(2)}, u32[]{:S(2)}) collective-permute-start(bf16[96,2048]{1,0:T(8,128)(2,1)S(1)} %collective-permute-done.70), channel_id=1, source_target_pairs={{0,16},{4,20},{8,24},{12,28},{16,0},{20,4},{24,8},{28,12},{1,17},{... | collective-permute-start | bytes 1179656 | tf_op jit(solution)/shard_map/ppermute | solution.py:108
  480.8 37.8 %collective-permute-start.71 = (bf16[96,2048]{1,0:T(8,128)(2,1)S(1)}, bf16[96,2048]{1,0:T(8,128)(2,1)S(1)}, u32[]{:S(2)}, u32[]{:S(2)}) collective-permute-start(bf16[96,2048]{1,0:T(8,128)(2,1)S(1)} %collective-permute-done.70), channel_id=1, source_target_pairs={{0,8},{4,12},{8,0},{12,4},{16,24},{20,28},{24,16},{28,20},{1,9},{5... | collective-permute-start | bytes 1179656 | tf_op jit(solution)/shard_map/ppermute | solution.py:108
  489.3 30.1 %collective-permute-start.82 = (bf16[96,2048]{1,0:T(8,128)(2,1)S(1)}, bf16[96,2048]{1,0:T(8,128)(2,1)S(1)}, u32[]{:S(2)}, u32[]{:S(2)}) collective-permute-start(bf16[96,2048]{1,0:T(8,128)(2,1)S(1)} %collective-permute-done.80), channel_id=1, source_target_pairs={{0,16},{4,20},{8,24},{12,28},{16,0},{20,4},{24,8},{28,12},{1,17},{... | collective-permute-start | bytes 1179656 | tf_op jit(solution)/shard_map/ppermute | solution.py:108
  496.2 25.3 %collective-permute-start.92 = (bf16[96,2048]{1,0:T(8,128)(2,1)S(1)}, bf16[96,2048]{1,0:T(8,128)(2,1)S(1)}, u32[]{:S(2)}, u32[]{:S(2)}) collective-permute-start(bf16[96,2048]{1,0:T(8,128)(2,1)S(1)} %collective-permute-done.90), channel_id=1, source_target_pairs={{0,16},{4,20},{8,24},{12,28},{16,0},{20,4},{24,8},{28,12},{1,17},{... | collective-permute-start | bytes 1179656 | tf_op jit(solution)/shard_map/ppermute | solution.py:108
  538.2 212.4 %collective-permute-start.107 = (bf16[96,2048]{1,0:T(8,128)(2,1)S(1)}, bf16[96,2048]{1,0:T(8,128)(2,1)S(1)}, u32[]{:S(2)}, u32[]{:S(2)}) collective-permute-start(bf16[96,2048]{1,0:T(8,128)(2,1)S(1)} %pad_maximum_fusion.35), channel_id=1, source_target_pairs={{0,16},{4,20},{8,24},{12,28},{16,0},{20,4},{24,8},{28,12},{1,17},{... | collective-permute-start | bytes 1179656 | tf_op jit(solution)/shard_map/ppermute | solution.py:108
  544.8 206.5 %collective-permute-start.105 = (bf16[96,2048]{1,0:T(8,128)(2,1)S(1)}, bf16[96,2048]{1,0:T(8,128)(2,1)S(1)}, u32[]{:S(2)}, u32[]{:S(2)}) collective-permute-start(bf16[96,2048]{1,0:T(8,128)(2,1)S(1)} %pad_maximum_fusion.34), channel_id=1, source_target_pairs={{0,8},{4,12},{8,0},{12,4},{16,24},{20,28},{24,16},{28,20},{1,9},{5... | collective-permute-start | bytes 1179656 | tf_op jit(solution)/shard_map/ppermute | solution.py:108
  546.0 208.1 %collective-permute-start.69 = (bf16[96,2048]{1,0:T(8,128)(2,1)S(1)}, bf16[96,2048]{1,0:T(8,128)(2,1)S(1)}, u32[]{:S(2)}, u32[]{:S(2)}) collective-permute-start(bf16[96,2048]{1,0:T(8,128)(2,1)S(1)} %pad_maximum_fusion.27), channel_id=1, source_target_pairs={{0,16},{4,20},{8,24},{12,28},{16,0},{20,4},{24,8},{28,12},{1,17},{... | collective-permute-start | bytes 1179656 | tf_op jit(solution)/shard_map/ppermute | solution.py:108
  579.8 129.4 %collective-permute-start.135 = (bf16[48,2048]{1,0:T(8,128)(2,1)}, bf16[48,2048]{1,0:T(8,128)(2,1)}, u32[]{:S(2)}, u32[]{:S(2)}) collective-permute-start(bf16[48,2048]{1,0:T(8,128)(2,1)} %get-tuple-element.178), channel_id=1, source_target_pairs={{0,8},{4,12},{8,0},{12,4},{16,24},{20,28},{24,16},{28,20},{1,9},{5... | collective-permute-start | bytes 589832 | tf_op jit(solution)/shard_map/ppermute | solution.py:108
  580.5 129.2 %collective-permute-start.133 = (bf16[48,2048]{1,0:T(8,128)(2,1)}, bf16[48,2048]{1,0:T(8,128)(2,1)}, u32[]{:S(2)}, u32[]{:S(2)}) collective-permute-start(bf16[48,2048]{1,0:T(8,128)(2,1)} %get-tuple-element.179), channel_id=1, source_target_pairs={{0,16},{4,20},{8,24},{12,28},{16,0},{20,4},{24,8},{28,12},{1,17},{... | collective-permute-start | bytes 589832 | tf_op jit(solution)/shard_map/ppermute | solution.py:108
  769.7 25.6 %collective-permute-start.96 = (bf16[96,2048]{1,0:T(8,128)(2,1)S(1)}, bf16[96,2048]{1,0:T(8,128)(2,1)S(1)}, u32[]{:S(2)}, u32[]{:S(2)}) collective-permute-start(bf16[96,2048]{1,0:T(8,128)(2,1)S(1)} %pad_maximum_fusion.32), channel_id=1, source_target_pairs={{0,8},{4,12},{8,0},{12,4},{16,24},{20,28},{24,16},{28,20},{1,9},{5... | collective-permute-start | bytes 1179656 | tf_op jit(solution)/shard_map/ppermute | solution.py:108
  773.1 25.3 %collective-permute-start.137 = (bf16[96,2048]{1,0:T(8,128)(2,1)S(1)}, bf16[96,2048]{1,0:T(8,128)(2,1)S(1)}, u32[]{:S(2)}, u32[]{:S(2)}) collective-permute-start(bf16[96,2048]{1,0:T(8,128)(2,1)S(1)} %fusion.125), channel_id=1, source_target_pairs={{0,3},{1,2},{2,1},{3,0},{4,7},{5,6},{6,5},{7,4},{8,11},{9,10},{10,... | collective-permute-start | bytes 1179656 | tf_op jit(solution)/shard_map/ppermute | solution.py:112
  776.1 25.8 %collective-permute-start.117 = (bf16[96,2048]{1,0:T(8,128)(2,1)S(1)}, bf16[96,2048]{1,0:T(8,128)(2,1)S(1)}, u32[]{:S(2)}, u32[]{:S(2)}) collective-permute-start(bf16[96,2048]{1,0:T(8,128)(2,1)S(1)} %fusion.129), channel_id=1, source_target_pairs={{0,1},{1,0},{2,3},{3,2},{4,5},{5,4},{6,7},{7,6},{8,9},{9,8},{10,11... | collective-permute-start | bytes 1179656 | tf_op jit(solution)/shard_map/ppermute | solution.py:112
  788.5 42.6 %collective-permute-start.127 = (bf16[96,2048]{1,0:T(8,128)(2,1)S(1)}, bf16[96,2048]{1,0:T(8,128)(2,1)S(1)}, u32[]{:S(2)}, u32[]{:S(2)}) collective-permute-start(bf16[96,2048]{1,0:T(8,128)(2,1)S(1)} %fusion.127), channel_id=1, source_target_pairs={{0,2},{1,3},{2,0},{3,1},{4,6},{5,7},{6,4},{7,5},{8,10},{9,11},{10,... | collective-permute-start | bytes 1179656 | tf_op jit(solution)/shard_map/ppermute | solution.py:112
  793.3 43.9 %collective-permute-start.79 = (bf16[96,2048]{1,0:T(8,128)(2,1)S(1)}, bf16[96,2048]{1,0:T(8,128)(2,1)S(1)}, u32[]{:S(2)}, u32[]{:S(2)}) collective-permute-start(bf16[96,2048]{1,0:T(8,128)(2,1)S(1)} %fusion.137), channel_id=1, source_target_pairs={{0,1},{1,0},{2,3},{3,2},{4,5},{5,4},{6,7},{7,6},{8,9},{9,8},{10,11... | collective-permute-start | bytes 1179656 | tf_op jit(solution)/shard_map/ppermute | solution.py:112
  795.3 44.2 %collective-permute-start.89 = (bf16[96,2048]{1,0:T(8,128)(2,1)S(1)}, bf16[96,2048]{1,0:T(8,128)(2,1)S(1)}, u32[]{:S(2)}, u32[]{:S(2)}) collective-permute-start(bf16[96,2048]{1,0:T(8,128)(2,1)S(1)} %fusion.135), channel_id=1, source_target_pairs={{0,2},{1,3},{2,0},{3,1},{4,6},{5,7},{6,4},{7,5},{8,10},{9,11},{10,... | collective-permute-start | bytes 1179656 | tf_op jit(solution)/shard_map/ppermute | solution.py:112
  798.4 41.4 %collective-permute-start.99 = (bf16[96,2048]{1,0:T(8,128)(2,1)S(1)}, bf16[96,2048]{1,0:T(8,128)(2,1)S(1)}, u32[]{:S(2)}, u32[]{:S(2)}) collective-permute-start(bf16[96,2048]{1,0:T(8,128)(2,1)S(1)} %fusion.133), channel_id=1, source_target_pairs={{0,3},{1,2},{2,1},{3,0},{4,7},{5,6},{6,5},{7,4},{8,11},{9,10},{10,... | collective-permute-start | bytes 1179656 | tf_op jit(solution)/shard_map/ppermute | solution.py:112
  857.6 25.3 %collective-permute-start.157 = (bf16[96,2048]{1,0:T(8,128)(2,1)}, bf16[96,2048]{1,0:T(8,128)(2,1)S(1)}, u32[]{:S(2)}, u32[]{:S(2)}) collective-permute-start(bf16[96,2048]{1,0:T(8,128)(2,1)} %collective-permute-done.155), channel_id=1, source_target_pairs={{0,16},{4,20},{8,24},{12,28},{16,0},{20,4},{24,8},{28,12},{1,17},{... | collective-permute-start | bytes 1179656 | tf_op jit(solution)/shard_map/ppermute | solution.py:108
  861.4 28.4 %collective-permute-start.148 = (bf16[96,2048]{1,0:T(8,128)(2,1)}, bf16[96,2048]{1,0:T(8,128)(2,1)S(1)}, u32[]{:S(2)}, u32[]{:S(2)}) collective-permute-start(bf16[96,2048]{1,0:T(8,128)(2,1)} %collective-permute-done.146), channel_id=1, source_target_pairs={{0,16},{4,20},{8,24},{12,28},{16,0},{20,4},{24,8},{28,12},{1,17},{... | collective-permute-start | bytes 1179656 | tf_op jit(solution)/shard_map/ppermute | solution.py:108
  864.0 25.8 %collective-permute-start.166 = (bf16[96,2048]{1,0:T(8,128)(2,1)}, bf16[96,2048]{1,0:T(8,128)(2,1)S(1)}, u32[]{:S(2)}, u32[]{:S(2)}) collective-permute-start(bf16[96,2048]{1,0:T(8,128)(2,1)} %collective-permute-done.164), channel_id=1, source_target_pairs={{0,16},{4,20},{8,24},{12,28},{16,0},{20,4},{24,8},{28,12},{1,17},{... | collective-permute-start | bytes 1179656 | tf_op jit(solution)/shard_map/ppermute | solution.py:108
  889.8 160.4 %collective-permute-start.193 = (bf16[704,2048]{1,0:T(8,128)(2,1)}, bf16[704,2048]{1,0:T(8,128)(2,1)}, u32[]{:S(2)}, u32[]{:S(2)}) collective-permute-start(bf16[704,2048]{1,0:T(8,128)(2,1)} %slice.1495), channel_id=1, source_target_pairs={{0,4},{4,0},{8,12},{12,8},{16,20},{20,16},{24,28},{28,24},{1,5},{5... | collective-permute-start | bytes 8650760 | tf_op jit(solution)/shard_map/ppermute | solution.py:108
  889.8 164.8 %collective-permute-start.191 = (bf16[704,2048]{1,0:T(8,128)(2,1)}, bf16[704,2048]{1,0:T(8,128)(2,1)}, u32[]{:S(2)}, u32[]{:S(2)}) collective-permute-start(bf16[704,2048]{1,0:T(8,128)(2,1)} %slice.1497), channel_id=1, source_target_pairs={{0,4},{4,0},{8,12},{12,8},{16,20},{20,16},{24,28},{28,24},{1,5},{5... | collective-permute-start | bytes 8650760 | tf_op jit(solution)/shard_map/ppermute | solution.py:108
  891.0 169.3 %collective-permute-start.192 = (bf16[704,2048]{1,0:T(8,128)(2,1)}, bf16[704,2048]{1,0:T(8,128)(2,1)}, u32[]{:S(2)}, u32[]{:S(2)}) collective-permute-start(bf16[704,2048]{1,0:T(8,128)(2,1)} %slice.1496), channel_id=1, source_target_pairs={{0,4},{4,0},{8,12},{12,8},{16,20},{20,16},{24,28},{28,24},{1,5},{5... | collective-permute-start | bytes 8650760 | tf_op jit(solution)/shard_map/ppermute | solution.py:108
  893.8 31.3 %collective-permute-start.158 = (bf16[48,2048]{1,0:T(8,128)(2,1)}, bf16[48,2048]{1,0:T(8,128)(2,1)S(1)}, u32[]{:S(2)}, u32[]{:S(2)}) collective-permute-start(bf16[48,2048]{1,0:T(8,128)(2,1)} %slice.1167), channel_id=1, source_target_pairs={{0,8},{4,12},{8,0},{12,4},{16,24},{20,28},{24,16},{28,20},{1,9},{5... | collective-permute-start | bytes 589832 | tf_op jit(solution)/shard_map/ppermute | solution.py:108
  1047.2 76.0 %collective-permute-start.145 = (bf16[128,2048]{1,0:T(8,128)(2,1)}, bf16[128,2048]{1,0:T(8,128)(2,1)}, u32[]{:S(2)}, u32[]{:S(2)}) collective-permute-start(bf16[128,2048]{1,0:T(8,128)(2,1)} %pad_maximum_fusion.11), channel_id=1, source_target_pairs={{0,16},{4,20},{8,24},{12,28},{16,0},{20,4},{24,8},{28,12},{1,17},{... | collective-permute-start | bytes 1572872 | tf_op jit(solution)/shard_map/ppermute | solution.py:108
  1049.2 38.1 %collective-permute-start.190 = (bf16[256,2048]{1,0:T(8,128)(2,1)}, bf16[256,2048]{1,0:T(8,128)(2,1)}, u32[]{:S(2)}, u32[]{:S(2)}) collective-permute-start(bf16[256,2048]{1,0:T(8,128)(2,1)} %slice.1498), channel_id=1, source_target_pairs={{0,4},{4,0},{8,12},{12,8},{16,20},{20,16},{24,28},{28,24},{1,5},{5... | collective-permute-start | bytes 3145736 | tf_op jit(solution)/shard_map/ppermute | solution.py:108
  1050.2 32.2 %collective-permute-start.163 = (bf16[128,2048]{1,0:T(8,128)(2,1)}, bf16[128,2048]{1,0:T(8,128)(2,1)}, u32[]{:S(2)}, u32[]{:S(2)}) collective-permute-start(bf16[128,2048]{1,0:T(8,128)(2,1)} %pad_maximum_fusion.15), channel_id=1, source_target_pairs={{0,16},{4,20},{8,24},{12,28},{16,0},{20,4},{24,8},{28,12},{1,17},{... | collective-permute-start | bytes 1572872 | tf_op jit(solution)/shard_map/ppermute | solution.py:108
  1054.6 27.8 %collective-permute-start.161 = (bf16[128,2048]{1,0:T(8,128)(2,1)}, bf16[128,2048]{1,0:T(8,128)(2,1)}, u32[]{:S(2)}, u32[]{:S(2)}) collective-permute-start(bf16[128,2048]{1,0:T(8,128)(2,1)} %pad_maximum_fusion.14), channel_id=1, source_target_pairs={{0,8},{4,12},{8,0},{12,4},{16,24},{20,28},{24,16},{28,20},{1,9},{5... | collective-permute-start | bytes 1572872 | tf_op jit(solution)/shard_map/ppermute | solution.py:108
  1101.5 38.0 %collective-permute-start.189 = (bf16[256,2048]{1,0:T(8,128)(2,1)S(1)}, bf16[256,2048]{1,0:T(8,128)(2,1)S(1)}, u32[]{:S(2)}, u32[]{:S(2)}) collective-permute-start(bf16[256,2048]{1,0:T(8,128)(2,1)S(1)} %copy-done.29), channel_id=1, source_target_pairs={{0,4},{4,0},{8,12},{12,8},{16,20},{20,16},{24,28},{28,24},{1,5},{5... | collective-permute-start | bytes 3145736 | tf_op jit(solution)/shard_map/ppermute | solution.py:108
  1103.8 28.7 %collective-permute-start.175 = (bf16[128,2048]{1,0:T(8,128)(2,1)S(1)}, bf16[128,2048]{1,0:T(8,128)(2,1)S(1)}, u32[]{:S(2)}, u32[]{:S(2)}) collective-permute-start(bf16[128,2048]{1,0:T(8,128)(2,1)S(1)} %fusion.116), channel_id=1, source_target_pairs={{0,1},{1,0},{2,3},{3,2},{4,5},{5,4},{6,7},{7,6},{8,9},{9,8},{10,11... | collective-permute-start | bytes 1572872 | tf_op jit(solution)/shard_map/ppermute | solution.py:112
  (247 other events, 3779.6 us)

commit v2 on v1

v2 whole, which is shorter than its diff:
```python
import functools

import jax
import jax.numpy as jnp
from jax import lax
from jax.experimental import pallas as pl
from jax.experimental.pallas import tpu as pltpu
from jax.sharding import PartitionSpec as P

HD = 128
eps = 1e-06
rope_base = 10000.0
masked_value = -1e30
f32 = jnp.float32
bf16 = jnp.bfloat16


def rms_inverse(values):
    return lax.rsqrt(jnp.mean(values * values, axis=-1, keepdims=True) + eps)


def norm_back(values, gain_vec, grad_out):
    inverse = rms_inverse(values)
    scaled = grad_out * gain_vec
    inner = jnp.mean(scaled * values, axis=-1, keepdims=True)
    grad_values = inverse * scaled - values * inverse * inverse * inverse * inner
    grad_gain = jnp.sum(grad_out * values * inverse, axis=0)
    return (grad_values, grad_gain)


def dot_nt(left, right):
    return lax.dot_general(left, right, (((1,), (1,)), ((), ())), preferred_element_type=f32)


def dot_nn(left, right):
    return lax.dot_general(left, right, (((1,), (0,)), ((), ())), preferred_element_type=f32)


def dot_tn(left, right):
    return lax.dot_general(left, right, (((0,), (0,)), ((), ())), preferred_element_type=f32)


def two_parts(values):
    high = values.astype(bf16)
    return high, (values - high.astype(f32)).astype(bf16)


CORE, SIDE_X, SIDE_Y = 1, 2, 4
flows = []


def spawn(flow):
    flows.append([flow, None])


def pause(steps):
    for _ in range(steps):
        yield ()


def drive():
    while flows:
        due, going = [], []
        for entry in flows:
            try:
                values = entry[0].send(entry[1])
            except StopIteration:
                continue
            going.append((entry, len(values)))
            due.extend(values)
        flows[:] = [entry for entry, _ in going]
        if due:
            due = lax.optimization_barrier(tuple(due))
        place = 0
        for entry, count in going:
            entry[1] = tuple(due[place : place + count])
            place += count


class Plain:
    def __init__(self, mesh):
        self.pair = 1
        self.column_steps = 0
        self.tp = mesh.shape["dp"]
        self.experts = mesh.shape["expert"]

    def labels(self):
        return jnp.arange(self.experts, dtype=jnp.int32)

    def order(self):
        return list(range(self.experts))

    def exchange(self, blocks):
        moved = lax.all_to_all(jnp.stack(blocks), "expert", 0, 0, tiled=True)
        moved = yield tuple(one for one in moved)
        return moved

    def order_back(self):
        return list(range(self.experts))

    def spread(self, blocks, ready, order):
        moved = yield from self.exchange(blocks)
        for r, one in enumerate(moved):
            rows = yield from self.plane_gather(one)
            ready(r, rows)

    def collect(self, parts, r, part, last=False, slow=0):
        parts[r] = yield from self.plane_reduce(part)
        if len(parts) == self.experts:
            moved = yield from self.exchange([parts[i] for i in range(self.experts)])
            return list(moved)
        return None

    def line_gather(self, block, ready):
        rows = lax.all_gather(block, "expert", axis=0, tiled=False)
        rows = yield tuple(one for one in rows)
        for r, one in enumerate(rows):
            ready(r, one)
        return rows

    def plane_gather(self, block, axes=None):
        (rows,) = yield (lax.all_gather(block, "dp", axis=0, tiled=True),)
        return rows

    def plane_reduce(self, part):
        mine = lax.psum_scatter(part.astype(bf16), "dp", scatter_dimension=0, tiled=True)
        (mine,) = yield (mine,)
        return mine

    def share(self, index, gains):
        yield ()
        moved = lax.all_to_all(index[:, None, :], "expert", 0, 0, tiled=True)
        rows = lax.all_gather(moved, "dp", axis=1, tiled=True)
        gains = lax.all_gather(gains, ("dp", "expert"), axis=1, tiled=True)
        return [one for one in rows], gains

    def pair_gather(self, block):
        (block,) = yield (block,)
        return (block,)

    def pair_scatter(self, part):
        (part,) = yield (part,)
        return part.astype(f32)

    def column_gather(self, block):
        (rows,) = yield (lax.all_gather(block, "expert", axis=0, tiled=False),)
        return (rows,)

    def column_scatter(self, part):
        total = lax.psum_scatter(
            part[0].astype(bf16), "expert", scatter_dimension=0, tiled=True
        )
        (total,) = yield (total,)
        return total[0].astype(f32)

    def totals(self, sums, peak):
        yield ()
        sums = lax.psum_scatter(sums, ("dp", "expert"), scatter_dimension=1, tiled=True)
        return sums, lax.pmax(peak, ("dp", "expert"))


def swap(block, mask):
    return lax.ppermute(block, "dp", [(i, i ^ mask) for i in range(8)])


def flip(block, mask):
    return lax.ppermute(block, "expert", [(i, i ^ mask) for i in range(4)])


class Paired:
    def __init__(self, mesh):
        self.pair = 2
        self.column_steps = 2
        self.tp = 4
        self.experts = 4

    def labels(self):
        return lax.axis_index("expert") ^ jnp.arange(4, dtype=jnp.int32)

    def plane_gather(self, block, axes=(SIDE_X, SIDE_Y), slow=0):
        other = swap(block, axes[0])
        yield from pause(slow)
        (other,) = yield (other,)
        both = jnp.concatenate([block, other], axis=0)
        other = swap(both, axes[1])
        yield from pause(slow)
        (other,) = yield (other,)
        if axes[0] == SIDE_X:
            return jnp.concatenate([both, other], axis=0)
        size = block.shape[0]
        return jnp.concatenate([block, other[:size], both[size:], other[size:]], axis=0)

    def plane_gather_even(self, block):
        half = block.shape[0] // 2
        from_x, from_y = yield (swap(block, SIDE_X), swap(block, SIDE_Y))
        low, high = yield (swap(from_y[:half], SIDE_X), swap(from_x[half:], SIDE_Y))
        return jnp.concatenate([block, from_x, from_y, low, high], axis=0)

    def plane_reduce_even(self, part):
        size = part.shape[0] // 4
        half = size // 2
        own, to_x, to_y, across = (part[i * size : (i + 1) * size] for i in range(4))
        low, high = swap(across[:half], SIDE_X), swap(across[half:], SIDE_Y)
        own, to_x, to_y, low, high = yield (own, to_x, to_y, low, high)
        low = (to_y[:half].astype(f32) + low.astype(f32)).astype(bf16)
        high = (to_x[half:].astype(f32) + high.astype(f32)).astype(bf16)
        to_y = jnp.concatenate([low, to_y[half:]], axis=0)
        to_x = jnp.concatenate([to_x[:half], high], axis=0)
        own, from_x, from_y = yield (own, swap(to_x, SIDE_X), swap(to_y, SIDE_Y))
        return own.astype(f32) + from_x.astype(f32) + from_y.astype(f32)

    def plane_reduce(self, part, slow=0):
        size = part.shape[0] // 4
        rows = part.reshape(2, 2, size, -1)
        arrived = swap(rows[:, 1].reshape(2 * size, -1), SIDE_X)
        yield from pause(slow)
        rows, arrived = yield (rows, arrived)
        rows = rows[:, 0].astype(f32) + arrived.astype(f32).reshape(2, size, -1)
        own, arrived = rows[0], swap(rows[1].astype(bf16), SIDE_Y)
        yield from pause(slow)
        own, arrived = yield (own, arrived)
        return own + arrived.astype(f32)

    def line_gather(self, block, ready):
        ready(0, block)
        rows = [block]
        for r in (1, 2, 3):
            (moved,) = yield (flip(block, r),)
            ready(r, moved)
            rows.append(moved)
        return rows

    def line_reduce(self, parts):
        total = parts[0]
        moved = tuple(flip(parts[r].astype(bf16), r) for r in (1, 2, 3))
        moved = yield moved
        for one in moved:
            total = total + one.astype(f32)
        return total

    def reorder(self, parts):
        place = lax.axis_index("expert")
        odd = (place & 1) == 1
        parts = [jnp.where(odd, parts[i ^ 1], parts[i]) for i in range(4)]
        upper = (place & 2) == 2
        return [jnp.where(upper, parts[i ^ 2], parts[i]) for i in range(4)]

    def order(self):
        return [0, 1, 2, 3]

    def order_back(self):
        return [1, 2, 3, 0]

    def spread(self, blocks, ready, order):
        def plane(r, block, even):
            gather = self.plane_gather_even if even else self.plane_gather
            rows = yield from gather(block)
            ready(r, rows)

        for place, r in enumerate(order):
            if r:
                (moved,) = yield (flip(blocks[r], r),)
                spawn(plane(r, moved, place == 0))
            else:
                spawn(plane(0, blocks[0], place == 0))

    def spread_later(self, blocks, ready):
        def plane(r, block):
            rows = yield from self.plane_gather(block, (SIDE_Y, SIDE_X), slow=1)
            ready(r, rows)

        for r in (1, 2, 3):
            moved = flip(blocks[r], r)
            yield ()
            (moved,) = yield (moved,)
            spawn(plane(r, moved))

    def collect(self, parts, r, part, last=False, slow=0):
        if last:
            mine = yield from self.plane_reduce_even(part)
        else:
            mine = yield from self.plane_reduce(part, slow)
        mine = mine.astype(bf16)
        if r:
            mine = flip(mine, r)
            yield from pause(slow)
            (mine,) = yield (mine,)
        parts[r] = mine
        if len(parts) == self.experts:
            return [parts[i] for i in range(self.experts)]
        return None

    def pair_gather(self, block):
        block, other = yield (block, swap(block, CORE))
        return (block, other)

    def pair_scatter(self, part):
        size = part.shape[0] // 2
        (other,) = yield (swap(part[size:].astype(bf16), CORE),)
        return part[:size].astype(f32) + other.astype(f32)

    def column_gather(self, block):
        moved = tuple(flip(block, r) for r in (1, 2, 3))
        yield ()
        moved = yield moved
        rows = [block] + list(moved)
        mine = jnp.stack(self.reorder(rows))
        mine, other = yield (mine, swap(mine, CORE))
        return (mine, other)

    def column_scatter(self, part):
        (other,) = yield (swap(part[1].astype(bf16), CORE),)
        mine = part[0] + other.astype(f32)
        total = yield from self.line_reduce(self.reorder([mine[i] for i in range(4)]))
        return total

    def steps(self, block, merge):
        for move, masks in ((flip, (1, 2, 3)), (swap, (SIDE_X, SIDE_Y, 6)), (swap, (CORE,))):
            block, *others = yield (block,) + tuple(move(block, mask) for mask in masks)
            for other in others:
                block = merge(block, other)
        return block

    def share(self, index, gains):
        count, size = gains.shape
        piece = jnp.concatenate(
            [index.astype(f32), gains.reshape(1, count * size).astype(f32)]
            + [jnp.zeros((7 - index.shape[0], index.shape[1]), f32)]
        )
        rows = yield from self.steps(piece[None], lambda a, b: jnp.concatenate([a, b]))
        rows = rows.reshape(2, 4, 4, 8, -1)
        index = rows[0].astype(jnp.int32)
        here = lax.axis_index("dp") * 4 + lax.axis_index("expert")
        spots = jnp.arange(32, dtype=jnp.int32)
        core, plane, line = spots // 16, spots // 4 % 4, spots % 4
        relative = plane * 8 + core * 4 + line
        moved = (spots[:, None] ^ here) == relative[None, :]
        gains = rows.reshape(32, 8, -1)[:, 4].astype(bf16)
        gains = jnp.dot(moved.astype(bf16), gains, preferred_element_type=f32)
        gains = gains.reshape(32, count, size).transpose(1, 0, 2).reshape(count, 32 * size)
        return [index[:, r, r] for r in range(4)], gains

    def totals(self, sums, peak):
        width = sums.shape[1]
        peak = jnp.pad(peak[None, :], ((0, 0), (0, width - peak.shape[0])))
        both = jnp.concatenate([sums, peak])
        is_peak = (jnp.arange(both.shape[0]) == sums.shape[0])[:, None]
        both = yield from self.steps(both, lambda a, b: jnp.where(is_peak, jnp.maximum(a, b), a + b))
        place = lax.axis_index("dp") * 4 + lax.axis_index("expert")
        size = width // 32
        mine = lax.dynamic_slice_in_dim(both, place * size, size, 1)
        return mine[:-1], both[-1]


def turn(values, cosine, sine):
    return values * cosine + pltpu.roll(values, HD // 2, 1) * sine


def causal_mask(size):
    keys = lax.broadcasted_iota(jnp.int32, (size, size), 0)
    queries = lax.broadcasted_iota(jnp.int32, (size, size), 1)
    return keys <= queries


def slot_rows(cap, index):
    slots = lax.broadcasted_iota(jnp.int32, (cap, index.shape[1]), 0)
    return (slots == index).astype(f32).astype(bf16)


def assemble_kernel(pair, *refs):
    queries, blocks, out = refs[:pair], refs[pair : 2 * pair], refs[-1]
    count = queries[0].shape[0]
    places, rows = blocks[0].shape[0], blocks[0].shape[1] // 2
    for p in range(pair):
        out[p * count : (p + 1) * count, :] = queries[p][...]
        for z in range(places):
            for kind in range(2):
                first = (kind + 1) * pair * count + p * count + z * rows
                out[first : first + rows, :] = blocks[p][z, kind * rows : (kind + 1) * rows, :]


def assemble(queries, blocks):
    pair = len(queries)
    count, width = queries[0].shape
    places, rows, _ = blocks[0].shape
    part = width // 4
    return pl.pallas_call(
        functools.partial(assemble_kernel, pair),
        grid=(4,),
        in_specs=[pl.BlockSpec((count, part), lambda i: (0, i))] * pair
        + [pl.BlockSpec((places, rows, part), lambda i: (0, 0, i))] * pair,
        out_specs=pl.BlockSpec((3 * pair * count, part), lambda i: (0, i)),
        out_shape=jax.ShapeDtypeStruct((3 * pair * count, width), bf16),
        cost_estimate=pl.CostEstimate(
            flops=0, bytes_accessed=12 * pair * count * width, transcendentals=0
        ),
        compiler_params=pltpu.CompilerParams(vmem_limit_bytes=32 << 20),
        name="assemble",
    )(*queries, *blocks)


def weave_kernel(first_ref, second_ref, out_ref):
    out_ref[:, 0, :] = first_ref[...]
    out_ref[:, 1, :] = second_ref[...]


def weave(first, second):
    count, width = first.shape
    step = 32
    rows = pl.BlockSpec((step, width), lambda i: (i, 0))
    return pl.pallas_call(
        weave_kernel,
        grid=(count // step,),
        in_specs=[rows, rows],
        out_specs=pl.BlockSpec((step, 2, width), lambda i: (i, 0, 0)),
        out_shape=jax.ShapeDtypeStruct((count, 2, width), first.dtype),
        cost_estimate=pl.CostEstimate(
            flops=0, bytes_accessed=16 * count * width, transcendentals=0
        ),
        name="weave",
    )(first, second)


def attend_kernel(
    heads, scale, raw_ref, cos_ref, sin_ref, idx_ref, qkv_ref, mixed_ref, peak_ref
):
    size = cos_ref.shape[0]
    wide = heads * HD
    seqs = raw_ref.shape[0] // size
    cap = mixed_ref.shape[0] // seqs
    cosine, sine = cos_ref[...], sin_ref[...]
    causal = causal_mask(size)
    pairs = [(s, h) for s in range(seqs) for h in range(heads)]
    scores, values = [], []
    for s, h in pairs:
        rows = slice(s * size, (s + 1) * size)
        q_at = slice(h * HD, (h + 1) * HD)
        k_at = slice(wide + h * HD, wide + (h + 1) * HD)
        v_at = slice(2 * wide + h * HD, 2 * wide + (h + 1) * HD)
        query = turn(raw_ref[rows, q_at], cosine, sine).astype(bf16)
        key = turn(raw_ref[rows, k_at], cosine, sine).astype(bf16)
        value = raw_ref[rows, v_at].astype(bf16)
        qkv_ref[rows, q_at] = query
        qkv_ref[rows, k_at] = key
        qkv_ref[rows, v_at] = value
        scores.append(dot_nt(key, query))
        values.append(value)
    scores = [jnp.where(causal, one * scale, masked_value) for one in scores]
    tops = [jnp.max(one, axis=0, keepdims=True) for one in scores]
    shifted = [jnp.exp(one - top) for one, top in zip(scores, tops)]
    totals = [jnp.sum(one, axis=0, keepdims=True) for one in shifted]
    probs = [(one * (1.0 / total)).astype(bf16) for one, total in zip(shifted, totals)]
    mixed = [dot_tn(prob, value).astype(bf16) for prob, value in zip(probs, values)]
    for s in range(seqs):
        index = idx_ref[s]
        for h in range(heads):
            peak_ref[s, h : h + 1, :] = jnp.where(index >= 0, tops[s * heads + h], masked_value)
        joined = jnp.concatenate(mixed[s * heads : (s + 1) * heads], axis=1)
        mixed_ref[s * cap : (s + 1) * cap, :] = dot_nn(slot_rows(cap, index), joined).astype(bf16)


GROUP = 1


def attend(raw, cosine, sine, index, cap):
    seqs, size = index.shape
    wide = raw.shape[1] // 3
    heads = wide // HD
    table = pl.BlockSpec((size, HD), lambda s: (0, 0))
    return pl.pallas_call(
        functools.partial(attend_kernel, heads, HD ** (-0.5)),
        grid=(seqs // GROUP,),
        in_specs=[
            pl.BlockSpec((GROUP * size, 3 * wide), lambda s: (s, 0)),
            table,
            table,
            pl.BlockSpec((GROUP, 1, size), lambda s: (s, 0, 0)),
        ],
        out_specs=[
            pl.BlockSpec((GROUP * size, 3 * wide), lambda s: (s, 0)),
            pl.BlockSpec((GROUP * cap, wide), lambda s: (s, 0)),
            pl.BlockSpec((GROUP, heads, size), lambda s: (s, 0, 0)),
        ],
        out_shape=[
            jax.ShapeDtypeStruct((seqs * size, 3 * wide), bf16),
            jax.ShapeDtypeStruct((seqs * cap, wide), bf16),
            jax.ShapeDtypeStruct((seqs, heads, size), f32),
        ],
        cost_estimate=pl.CostEstimate(
            flops=seqs * heads * size * size * HD * 6,
            bytes_accessed=seqs * size * wide * 20,
            transcendentals=seqs * heads * size * size,
        ),
        compiler_params=pltpu.CompilerParams(vmem_limit_bytes=32 << 20),
        name="attend",
    )(raw, cosine, sine, index[:, None, :])


def attend_back_kernel(heads, scale, qkv_ref, gm_ref, cos_ref, sin_ref, idx_ref, out_ref):
    size = cos_ref.shape[0]
    wide = heads * HD
    seqs = qkv_ref.shape[0] // size
    cap = gm_ref.shape[0] // seqs
    cosine, sine = cos_ref[...], -sin_ref[...]
    causal = causal_mask(size)
    places, operands, scores, grad_probs = [], [], [], []
    for s in range(seqs):
        rows = slice(s * size, (s + 1) * size)
        slots = gm_ref[s * cap : (s + 1) * cap, :]
        grad_mixed = dot_tn(slot_rows(cap, idx_ref[s]), slots).astype(bf16)
        for h in range(heads):
            q_at = slice(h * HD, (h + 1) * HD)
            k_at = slice(wide + h * HD, wide + (h + 1) * HD)
            v_at = slice(2 * wide + h * HD, 2 * wide + (h + 1) * HD)
            query, key, value = qkv_ref[rows, q_at], qkv_ref[rows, k_at], qkv_ref[rows, v_at]
            grad = grad_mixed[:, q_at]
            places.append((rows, q_at, k_at, v_at))
            operands.append((query, key, grad))
            scores.append(dot_nt(key, query))
            grad_probs.append(dot_nt(value, grad))
    scores = [jnp.where(causal, one * scale, masked_value) for one in scores]
    tops = [jnp.max(one, axis=0, keepdims=True) for one in scores]
    shifted = [jnp.exp(one - top) for one, top in zip(scores, tops)]
    totals = [jnp.sum(one, axis=0, keepdims=True) for one in shifted]
    probs = [one * (1.0 / total) for one, total in zip(shifted, totals)]
    inners = [jnp.sum(p * g, axis=0, keepdims=True) for p, g in zip(probs, grad_probs)]
    grads = [(p * (g - i)).astype(bf16) for p, g, i in zip(probs, grad_probs, inners)]
    for place, (query, key, grad), prob, grad_scores in zip(places, operands, probs, grads):
        rows, q_at, k_at, v_at = place
        grad_query = dot_tn(grad_scores, key) * scale
        grad_key = dot_nn(grad_scores, query) * scale
        out_ref[rows, q_at] = turn(grad_query, cosine, sine).astype(bf16)
        out_ref[rows, k_at] = turn(grad_key, cosine, sine).astype(bf16)
        out_ref[rows, v_at] = dot_nn(prob.astype(bf16), grad).astype(bf16)


def attend_back(qkv, grad_mixed, cosine, sine, index):
    seqs, size = index.shape
    cap = grad_mixed.shape[0] // seqs
    wide = qkv.shape[1] // 3
    heads = wide // HD
    table = pl.BlockSpec((size, HD), lambda s: (0, 0))
    return pl.pallas_call(
        functools.partial(attend_back_kernel, heads, HD ** (-0.5)),
        grid=(seqs // GROUP,),
        in_specs=[
            pl.BlockSpec((GROUP * size, 3 * wide), lambda s: (s, 0)),
            pl.BlockSpec((GROUP * cap, wide), lambda s: (s, 0)),
            table,
            table,
            pl.BlockSpec((GROUP, 1, size), lambda s: (s, 0, 0)),
        ],
        out_specs=pl.BlockSpec((GROUP * size, 3 * wide), lambda s: (s, 0)),
        out_shape=jax.ShapeDtypeStruct((seqs * size, 3 * wide), bf16),
        cost_estimate=pl.CostEstimate(
            flops=seqs * heads * size * size * HD * 12,
            bytes_accessed=seqs * size * wide * 14,
            transcendentals=seqs * heads * size * size,
        ),
        compiler_params=pltpu.CompilerParams(vmem_limit_bytes=32 << 20),
        name="attend_back",
    )(qkv, grad_mixed, cosine, sine, index[:, None, :])


def on_device(
    links,
    hidden_in,
    seq_lengths,
    attn_routes,
    attn_gates,
    mlp_routes,
    mlp_gates,
    attn_gain,
    mlp_gain,
    k_weight,
    v_weight,
    attn_experts,
    mlp_experts,
    logit_limit,
    out_grad,
):
    experts = links.experts
    seq_len, width = hidden_in.shape
    cap = seq_len * attn_routes.shape[1] * 3 // (2 * experts)
    shard_heads = attn_experts.shape[1] // HD
    local_heads = shard_heads * links.pair
    wide = local_heads * HD
    dp_id = lax.axis_index("dp")
    places = jnp.arange(seq_len, dtype=jnp.int32)
    live = places < seq_lengths[0]
    labels = links.labels()

    before = (places[:, None] < places[None, :]).astype(bf16)

    def slot_tables(routes, gates):
        first, second = routes[:, 0][None, :], routes[:, 1][None, :]
        names = labels[:, None]
        named = (first == names) | (second == names)
        rank = dot_nn(named.astype(bf16), before).astype(jnp.int32)
        index = jnp.where(named & live[None, :], rank, -1)
        weight = jnp.where(first == names, gates[:, 0][None, :], 0.0) + jnp.where(
            second == names, gates[:, 1][None, :], 0.0
        )
        slot_ids = jnp.arange(cap, dtype=jnp.int32)[None, :, None]
        taken = slot_ids == index[:, None, :]
        combine = jnp.where(taken, weight[:, None, :], 0.0)
        slot_gate = jnp.sum(combine, axis=2)[:, :, None]
        taken = taken.astype(bf16)
        return index, taken, slot_gate, two_parts(combine)

    key_rows = k_weight.shape[0]
    attn_index, attn_taken, attn_slot_gate, attn_combine = slot_tables(attn_routes, attn_gates)
    _, mlp_taken, mlp_slot_gate, mlp_combine = slot_tables(mlp_routes, mlp_gates)
    def combine_rows(parts, rows):
        rows = jnp.concatenate(rows, axis=0)
        flat = [one.reshape(experts * cap, seq_len) for one in parts]
        return sum(dot_tn(one, rows) for one in flat)

    half = HD // 2
    freqs = rope_base ** (-jnp.arange(half, dtype=f32) / half)
    angles = places.astype(f32)[:, None] * freqs[None, :]
    cosine = jnp.concatenate([jnp.cos(angles), jnp.cos(angles)], axis=1)
    sine = jnp.concatenate([-jnp.sin(angles), jnp.sin(angles)], axis=1)

    head_count = logit_limit.shape[0]
    hidden = hidden_in.astype(f32)
    keep = live.astype(f32)[:, None]
    box = {}

    def wait(*names):
        while any(name not in box for name in names):
            yield ()

    def put(name):
        def ready(r, value):
            box[name, r] = value

        return ready

    def gated(values, *names):
        names = [name for name in names if name in box]
        values = yield tuple(values) + tuple(box[name] for name in names)
        for place, name in enumerate(names):
            box[name] = values[len(values) - len(names) + place]
        return values[: len(values) - len(names)]

    def following(order, r):
        place = order.index(r) + 1
        return order[place] if place < len(order) else None

    def hidden_plane(r, block):
        rows = yield from links.plane_gather(block)
        box["hidden", r] = rows

    def fetch_small():
        index, gains = yield from links.share(attn_index, jnp.stack([attn_gain, mlp_gain]))
        gains = gains.astype(f32)
        box["gain_one"], box["gain_two"] = gains[0:1], gains[1:2]
        box["index"] = index

    def fetch_key_value():
        block = jnp.concatenate([k_weight, v_weight], axis=0)
        key_values = yield from links.column_gather(block)
        yield from wait("q_parts")
        box["qkv_w"] = assemble(box["q_parts"], key_values)

    def fetch_hidden():
        spawn(hidden_plane(0, hidden_in))
        for _ in range(links.column_steps):
            yield ()
        yield from links.line_gather(
            hidden_in, lambda r, block: spawn(hidden_plane(r, block)) if r else None
        )
        box["line"] = True

    def fetch_pair(name, block, after=None):
        parts = yield from links.pair_gather(block)
        if after is not None:
            yield from wait(after)
            parts = yield parts
        (box[name],) = yield (jnp.concatenate(parts, axis=0),)

    def fetch_queries():
        box["q_parts"] = yield from links.pair_gather(attn_experts[0, :, 0, :])

    def fetch_grads():
        slots = [
            (mlp_slot_gate[r] * dot_nn(mlp_taken[r], out_grad)).astype(bf16)
            for r in range(experts)
        ]
        if links.pair == 2:
            spawn(grads_plane(slots[0]))
        slots = yield slots
        if links.pair == 1:
            yield from links.spread(slots, put("grad_rows"), links.order())
        else:
            yield from wait("line")
            yield from links.spread_later(slots, put("grad_rows"))

    def grads_plane(block):
        rows = yield from links.plane_gather(block, (SIDE_Y, SIDE_X))
        box["grad_rows", 0] = rows

    def attention():
        parts = {}
        for r in range(experts):
            yield from wait("qkv_w", "o_w", "index", ("hidden", r))
            values = box["hidden", r].astype(f32)
            norm_one = (values * rms_inverse(values) * box["gain_one"]).astype(bf16)
            box["normed", r] = norm_one
            raw = dot_nt(norm_one, box["qkv_w"])
            qkv, mixed, peak = attend(raw, cosine, sine, box["index"][r], cap)
            part = dot_nn(mixed, box["o_w"]).astype(bf16)
            qkv, mixed, peak, part = yield from gated(
                (qkv, mixed, peak, part), ("hidden", r + 1), ("hidden", r + 2)
            )
            box["turned", r], box["mixed", r] = qkv, mixed
            box["started"] = True
            box["peak", r] = peak
            if r == experts - 1:
                box["attended"] = True
            spawn(gather_middle(parts, r, part))

    def gather_middle(parts, r, part):
        rows = yield from links.collect(parts, r, part, r == experts - 1)
        if rows is None:
            return
        middle = hidden + combine_rows(attn_combine, rows)
        norm_two = (middle * rms_inverse(middle) * box["gain_two"]).astype(bf16)
        slots = [dot_nn(mlp_taken[r], norm_two).astype(bf16) for r in range(experts)]
        *slots, box["middle"] = yield slots + [middle]
        spawn(links.spread(slots, put("mlp_rows"), links.order()))

    def unit_grads():
        for r in links.order():
            yield from wait("down_w", ("grad_rows", r))
            later = following(links.order(), r)
            (box["grad_units", r],) = yield from gated(
                (dot_nt(box["grad_rows", r], box["down_w"]),), ("grad_rows", later)
            )

    def feed_forward():
        grad_parts = {}
        for r in links.order():
            yield from wait(("mlp_rows", r), ("grad_units", r))
            rows, grad_units = box["mlp_rows", r], box["grad_units", r]
            gate_pre = dot_nt(rows, box["gate_w"])
            up_pre = dot_nt(rows, box["up_w"])
            gate_sig = jax.nn.sigmoid(gate_pre)
            silu_val = gate_pre * gate_sig
            units = (silu_val * up_pre).astype(bf16)
            grad_gate = grad_units * up_pre * gate_sig * (1.0 + gate_pre * (1.0 - gate_sig))
            grad_gate = grad_gate.astype(bf16)
            grad_up = (grad_units * silu_val).astype(bf16)
            box["units", r], box["grad_gate", r], box["grad_up", r] = units, grad_gate, grad_up
            grad_part = dot_nn(grad_gate, box["gate_w"]) + dot_nn(grad_up, box["up_w"])
            grad_part = grad_part.astype(bf16)
            out_part = dot_nn(units, box["down_w"]).astype(bf16)
            later = following(links.order(), r)
            grad_part, out_part = yield from gated(
                (grad_part, out_part), ("mlp_rows", later), ("grad_units", later)
            )
            spawn(gather_grads(grad_parts, r, grad_part))
            box["out_part", r] = out_part

    def gather_outs():
        parts = {}
        for r in links.order_back():
            (part,) = yield (box["out_part", r],)
            spawn(gather_out(parts, r, part))

    def gather_out(parts, r, part):
        rows = yield from links.collect(parts, r, part)
        if rows is None:
            return
        total = box["middle"] + combine_rows(mlp_combine, rows)
        box["block_out"] = (keep * total).astype(bf16)

    def gather_grads(parts, r, part):
        rows = yield from links.collect(parts, r, part, r == links.order()[-1])
        if rows is None:
            return
        grad_norm_two = combine_rows([mlp_taken], rows)
        grad_mid_norm, box["gain_two_grad"] = norm_back(
            box["middle"], box["gain_two"], grad_norm_two
        )
        grad_middle = out_grad.astype(f32) * keep + grad_mid_norm
        high, low = two_parts(grad_middle)
        slots = [
            (attn_slot_gate[r] * (dot_nn(attn_taken[r], high) + dot_nn(attn_taken[r], low)))
            .astype(bf16)
            for r in range(experts)
        ]
        *slots, box["grad_middle"] = yield slots + [grad_middle]
        spawn(links.spread(slots, put("attn_grad_rows"), links.order_back()))
        spawn(gather_outs())
        spawn(expert_grads())

    def joined(name):
        return jnp.concatenate([box[name, r] for r in range(experts)], axis=0)

    def expert_grads():
        rows, grads = joined("mlp_rows"), joined("grad_rows")
        pieces = []
        for name, other in (("grad_gate", rows), ("grad_up", rows), ("units", grads)):
            (whole,) = yield (dot_tn(joined(name), other).astype(bf16),)
            piece = yield from links.pair_scatter(whole)
            pieces.append(piece)
        box["mlp_grad"] = jnp.stack(pieces).transpose(1, 0, 2)[None]

    def attention_back():
        parts = {}
        *early, last = links.order_back()

        def early_rows(start, stop):
            grads = jnp.concatenate([box["grads", r][:, start:stop] for r in early], axis=0)
            return grads, jnp.concatenate([box["normed", r] for r in early], axis=0)

        for r in links.order_back():
            yield from wait(("attn_grad_rows", r))
            grad_mixed = dot_nt(box["attn_grad_rows", r], box["o_w"]).astype(bf16)
            grads = attend_back(box["turned", r], grad_mixed, cosine, sine, box["index"][r])
            later = following(links.order_back(), r)
            part = dot_nn(grads, box["qkv_w"]).astype(bf16)
            box["grads", r], part = yield from gated((grads, part), ("attn_grad_rows", later))
            spawn(gather_input(parts, r, part))
            if r == early[-1]:
                kv_sum = dot_tn(*early_rows(wide, None))
                q_sum = dot_tn(*early_rows(0, wide))
                kv_sum, q_sum = yield (kv_sum, q_sum)
        grads, rows = box["grads", last], box["normed", last]
        kv_grad = kv_sum + dot_tn(grads[:, wide:], rows)
        gain_one = jnp.sum(kv_grad * box["qkv_w"][wide:].astype(f32), axis=0, keepdims=True)
        kv_grad, grads, rows = yield (kv_grad, grads, rows)
        spawn(project_grads(kv_grad))
        q_grad = q_sum + dot_tn(grads[:, :wide], rows)
        more = jnp.sum(q_grad * box["qkv_w"][:wide].astype(f32), axis=0, keepdims=True)
        (q_grad,) = yield (q_grad,)
        box["gain_one_grad"] = (gain_one + more) / box["gain_one"]
        spawn(gather_totals())
        query_grad = yield from links.pair_scatter(q_grad)
        out_grads = dot_tn(joined("mixed"), joined("attn_grad_rows"))
        (out_grads,) = yield (out_grads,)
        out_grads = yield from links.pair_scatter(out_grads)
        box["attn_grad"] = weave(query_grad, out_grads)[None]

    def gather_totals():
        local_peak = jnp.max(jnp.stack([box["peak", r] for r in range(experts)]), axis=(0, 1, 3))
        owners = jnp.concatenate(
            [(dp_id ^ i) * shard_heads + jnp.arange(shard_heads) for i in range(links.pair)]
        )
        spots = owners[:, None] == jnp.arange(head_count)[None, :]
        peak_vec = jnp.max(jnp.where(spots, local_peak[:, None], masked_value), axis=0)
        gain_sums = jnp.concatenate([box["gain_one_grad"], box["gain_two_grad"][None]])
        box["gains"], box["peaks"] = yield from links.totals(gain_sums, peak_vec)

    def project_grads(part):
        column = (links.pair, experts, key_rows, width)
        part = jnp.concatenate(
            [part[:wide].reshape(column), part[wide:].reshape(column)], axis=2
        )
        total = yield from links.column_scatter(part)
        box["k_grad"], box["v_grad"] = total[:key_rows], total[key_rows:]

    def gather_input(parts, r, part):
        rows = yield from links.collect(parts, r, part, r == links.order_back()[-1])
        if rows is None:
            return
        grad_norm_one = sum(one.astype(f32) for one in rows)
        grad_hid_norm, _ = norm_back(hidden, box["gain_one"], grad_norm_one)
        box["grad_input"] = box["grad_middle"] + grad_hid_norm

    spawn(fetch_key_value())
    spawn(fetch_hidden())
    spawn(fetch_small())
    spawn(fetch_queries())
    spawn(fetch_pair("o_w", attn_experts[0, :, 1, :]))
    spawn(fetch_pair("down_w", mlp_experts[0, :, 2, :], "started"))
    spawn(fetch_pair("gate_w", mlp_experts[0, :, 0, :], "started"))
    spawn(fetch_pair("up_w", mlp_experts[0, :, 1, :], "started"))
    spawn(fetch_grads())
    spawn(attention())
    spawn(unit_grads())
    spawn(feed_forward())
    spawn(attention_back())
    drive()

    factors = logit_limit / jnp.maximum(box["peaks"][:head_count], logit_limit)
    roots = jnp.sqrt(factors)

    def row_scale(first_row, count):
        rows = first_row + jnp.arange(count, dtype=jnp.int32)
        heads = (rows // HD)[:, None] == jnp.arange(head_count)[None, :]
        return jnp.sum(jnp.where(heads, roots[None, :], 0.0), axis=1, keepdims=True)

    query_count = attn_experts.shape[1]
    clipped_query = (
        attn_experts[0, :, 0, :].astype(f32) * row_scale(dp_id * query_count, query_count)
    ).astype(bf16)[None]
    device_id = dp_id * experts + lax.axis_index("expert")
    clipped_key = (
        k_weight.astype(f32) * row_scale(device_id * key_rows, key_rows)
    ).astype(bf16)
    return (
        box["block_out"],
        box["grad_input"],
        box["k_grad"],
        box["v_grad"],
        box["gains"][0],
        box["gains"][1],
        box["attn_grad"],
        box["mlp_grad"],
        clipped_query,
        clipped_key,
        factors,
    )


def solution(mesh):
    paired = mesh.shape["dp"] == 8 and mesh.shape["expert"] == 4
    links = Paired(mesh) if paired else Plain(mesh)
    rows = P(("dp", "expert"), None)
    vec = P(("dp", "expert"))
    weights = P("expert", "dp", None, None)
    return jax.shard_map(
        functools.partial(on_device, links),
        mesh=mesh,
        in_specs=(rows, vec, rows, rows, rows, rows, vec, vec, rows, rows)
        + (weights, weights, P(), rows),
        out_specs=(rows, rows, rows, rows, vec, vec, weights, weights)
        + (P("expert", "dp", None), rows, P()),
        check_vma=False,
    )
```

time: 1190 us -> 1000 us (0.84)
  starting transfers between devices: 265 us -> 150 us
  matrix products: 291 us -> 236 us
  other arithmetic: 95.9 us -> 133 us
  Pallas kernels: 61.4 us -> 33.3 us
  waiting for transfers between devices: 368 us -> 342 us
    ppermute x16 -> x0, waiting for transfers between devices: 58 us -> none  [hop(): return lax.ppermute(block, 'expert', pairs)]
    ppermute x152 -> x94, starting transfers between devices: 144 us -> 86.7 us  [swap(): return lax.ppermute(block, 'dp', [(i, i ^ mask) for i in range(8)])]
    dot_general x38, matrix products: 107 us -> 70.9 us  [dot_nn(): lax.dot_general(left, right, (((1,), (0,)), ((), ())), preferred_element_...]
    ppermute x31 -> x36, starting transfers between devices: 95.1 us -> 63.6 us  [flip(): return lax.ppermute(block, 'expert', [(i, i ^ mask) for i in range(4)])]
    ppermute x31 -> x36, waiting for transfers between devices: 105 us -> 131 us  [flip(): return lax.ppermute(block, 'expert', [(i, i ^ mask) for i in range(4)])]
    ppermute x16 -> x0, starting transfers between devices: 25.6 us -> none  [hop(): return lax.ppermute(block, 'expert', pairs)]
    dot_general x20, matrix products: 110 us -> 87.8 us  [dot_nt(): lax.dot_general(left, right, (((1,), (1,)), ((), ())), preferred_element_...]
    concatenate x35 -> x28, other arithmetic: 18.4 us -> 36.7 us  [the longest x4 20.2 us: fetch_pair(): box[name], = (yield (jnp.concatenate(parts, axis=0),))]
  transfers between devices with their start and end apart: 199 -> 130, of which waited for: 74 -> 47; matrix products, arithmetic and copies ran while one was open for 40% -> 39% of each run, Pallas kernels for 5% -> 3%
where the time goes in v2:
time: 1000 us; the launch traced here: 994 us
  waiting for transfers between devices  342 us (34%)
  matrix products  236 us (24%)
  starting transfers between devices  150 us (15%)
  other arithmetic  133 us (13%)
  local copies, waits for them, and re-layouts  93.7 us (9%)
  Pallas kernels  33.3 us (3%)
    ppermute x94, waiting for transfers between devices, swap(): return lax.ppermute(block, 'dp', [(i, i ^ mask) for i in range(8)])  211 us
    ppermute x36, waiting for transfers between devices, flip(): return lax.ppermute(block, 'expert', [(i, i ^ mask) for i in range(4)])  131 us
    dot_general x20, matrix products, dot_nt(): lax.dot_general(left, right, (((1,), (1,)), ((), ())), preferred_element_...  87.8 us
    ppermute x94, starting transfers between devices, swap(): return lax.ppermute(block, 'dp', [(i, i ^ mask) for i in range(8)])  86.7 us
    dot_general x13, matrix products, dot_tn(): lax.dot_general(left, right, (((0,), (0,)), ((), ())), preferred_element_...  77.3 us
    dot_general x38, matrix products, dot_nn(): lax.dot_general(left, right, (((1,), (0,)), ((), ())), preferred_element_...  70.9 us
    ppermute x36, starting transfers between devices, flip(): return lax.ppermute(block, 'expert', [(i, i ^ mask) for i in range(4)])  63.6 us
    unnamed x434, local copies, waits for them, and re-layouts  58.8 us
  transfers between devices with their start and end apart: 130, of which 47 were waited for; matrix products, arithmetic and copies ran while one was open for 39% of the time, Pallas kernels for 3%

profile of v2, /device:TPU:0, one launch (start us, length us, event | category | flops | bytes accessed | tf_op | source)
XLA Modules:
  0.0 994.0 jit_solution(2610458118992440639)
XLA Ops:
  3.7 5.1 collective-permute-start.2
  8.8 6.1 slice_bitcast_fusion
  52.4 6.5 collective-permute-done.13
  61.4 29.7 %collective-permute-done.12 = bf16[128,2048]{1,0:T(8,128)(2,1)S(1)} collective-permute-done((bf16[128,2048]{1,0:T(8,128)(2,1)S(1)}, bf16[128,2048]{1,0:T(8,128)(2,1)S(1)}, u32[]{:S(2)}, u32[]{:S(2)}) %collective-permute-start.12) | collective-permute-done | bytes 524320 | tf_op jit(solution)/shard_map/ppermute | solution.py:167
  106.3 12.8 %collective-permute-done.20 = bf16[128,2048]{1,0:T(8,128)(2,1)S(1)} collective-permute-done((bf16[128,2048]{1,0:T(8,128)(2,1)}, bf16[128,2048]{1,0:T(8,128)(2,1)S(1)}, u32[]{:S(2)}, u32[]{:S(2)}) %collective-permute-start.20) | collective-permute-done | bytes 524320 | tf_op jit(solution)/shard_map/ppermute | solution.py:167
  146.4 18.7 %collective-permute-done.25 = bf16[128,2048]{1,0:T(8,128)(2,1)S(1)} collective-permute-done((bf16[128,2048]{1,0:T(8,128)(2,1)}, bf16[128,2048]{1,0:T(8,128)(2,1)S(1)}, u32[]{:S(2)}, u32[]{:S(2)}) %collective-permute-start.25) | collective-permute-done | bytes 524320 | tf_op jit(solution)/shard_map/ppermute | solution.py:163
  171.9 27.3 %collective-permute-done.28 = bf16[96,2048]{1,0:T(8,128)(2,1)S(1)} collective-permute-done((bf16[96,2048]{1,0:T(8,128)(2,1)S(1)}, bf16[96,2048]{1,0:T(8,128)(2,1)S(1)}, u32[]{:S(2)}, u32[]{:S(2)}) %collective-permute-start.28) | collective-permute-done | bytes 393248 | tf_op jit(solution)/shard_map/ppermute | solution.py:163
  204.0 5.4 fusion.32
  216.3 6.1 pad_maximum_fusion.1
  227.0 6.3 pad_maximum_fusion.2
  233.2 6.3 pad_maximum_fusion.3
  261.9 5.3 fusion.66
  272.7 6.7 collective-permute-done.36
  279.4 5.9 collective-permute-done.37
  292.7 11.8 %collective-permute-done.42 = bf16[48,2048]{1,0:T(8,128)(2,1)S(1)} collective-permute-done((bf16[48,2048]{1,0:T(8,128)(2,1)S(1)}, bf16[48,2048]{1,0:T(8,128)(2,1)S(1)}, u32[]{:S(2)}, u32[]{:S(2)}) %collective-permute-start.42) | collective-permute-done | bytes 196640 | tf_op jit(solution)/shard_map/ppermute | solution.py:163
  318.6 5.1 collective-permute-done.45
  323.7 6.6 collective-permute-done.43
  338.6 6.8 fusion.74
  352.0 5.6 collective-permute-done.47
  366.8 5.9 fusion.82
  398.6 6.9 multiply_convert_fusion.9
  440.0 7.7 multiply_convert_fusion.6
  474.7 6.9 multiply_convert_fusion.3
  490.7 7.4 multiply_convert_fusion
  511.7 6.0 collective-permute-done.67
  537.3 7.5 collective-permute-done.73
  546.4 8.3 collective-permute-done.76
  564.7 11.5 %convolution_convert_fusion.2 = bf16[1408,2048]{1,0:T(8,128)(2,1)S(1)} fusion(bf16[1536,2048]{1,0:T(8,128)(2,1)} %get-tuple-element.614, bf16[384,1408]{1,0:T(8,128)(2,1)S(1)} %copy-done.170, bf16[384,1408]{1,0:T(8,128)(2,1)S(1)} %copy-done.169, bf16[384,1408]{1,0:T(8,128)(2,1)S(1)} %copy-done.167, bf16[384,1408]{1,0:T(8,128)(2,1)S(1)} %copy-done.165), kind=kOutput, calls=%fused_computation.6 | convolution fusion | flops 8878555136 | bytes 16384000 | tf_op jit(solution)/shard_map/dot_general | solution.py:40
  579.3 12.4 %convolution_convert_fusion.1 = bf16[1408,2048]{1,0:T(8,128)(2,1)S(1)} fusion(bf16[1536,2048]{1,0:T(8,128)(2,1)} %get-tuple-element.614, bf16[384,1408]{1,0:T(8,128)(2,1)} %copy-done.163, bf16[384,1408]{1,0:T(8,128)(2,1)} %copy-done.162, bf16[384,1408]{1,0:T(8,128)(2,1)S(1)} %copy-done.161, bf16[384,1408]{1,0:T(8,128)(2,1)S(1)} %copy-done.159), kind=kOutput, calls=%fused_computation.5 | convolution fusion | flops 8878555136 | bytes 16384000 | tf_op jit(solution)/shard_map/dot_general | solution.py:40
  595.1 13.7 %convolution_convert_fusion = bf16[1408,2048]{1,0:T(8,128)(2,1)} fusion(bf16[1536,2048]{1,0:T(8,128)(2,1)} %get-tuple-element.602, bf16[384,1408]{1,0:T(8,128)(2,1)} %get-tuple-element.564, bf16[384,1408]{1,0:T(8,128)(2,1)S(1)} %copy-done.175, bf16[384,1408]{1,0:T(8,128)(2,1)S(1)} %copy-done.173, bf16[384,1408]{1,0:T(8,128)(2,1)S(1)} %copy-done.172), kind=kOutput, calls=%fused_computation.4 | convolution fusion | flops 8878555136 | bytes 16384000 | tf_op jit(solution)/shard_map/dot_general | solution.py:40
  613.6 6.7 collective-permute-done.82
  635.8 23.1 %collective-permute-done.84 = bf16[48,2048]{1,0:T(8,128)(2,1)S(1)} collective-permute-done((bf16[48,2048]{1,0:T(8,128)(2,1)S(1)}, bf16[48,2048]{1,0:T(8,128)(2,1)S(1)}, u32[]{:S(2)}, u32[]{:S(2)}) %collective-permute-start.84) | collective-permute-done | bytes 196640 | tf_op jit(solution)/shard_map/ppermute | solution.py:163
  679.0 11.1 %collective-permute-done.93 = bf16[96,2048]{1,0:T(8,128)(2,1)S(1)} collective-permute-done((bf16[96,2048]{1,0:T(8,128)(2,1)S(1)}, bf16[96,2048]{1,0:T(8,128)(2,1)S(1)}, u32[]{:S(2)}, u32[]{:S(2)}) %collective-permute-start.93) | collective-permute-done | bytes 393248 | tf_op jit(solution)/shard_map/ppermute | solution.py:163
  716.0 28.7 %collective-permute-done.99 = bf16[96,2048]{1,0:T(8,128)(2,1)S(1)} collective-permute-done((bf16[96,2048]{1,0:T(8,128)(2,1)S(1)}, bf16[96,2048]{1,0:T(8,128)(2,1)S(1)}, u32[]{:S(2)}, u32[]{:S(2)}) %collective-permute-start.99) | collective-permute-done | bytes 393248 | tf_op jit(solution)/shard_map/ppermute | solution.py:163
  764.2 9.4 collective-permute-done.103
  773.6 6.4 add_bitcast_fusion
  785.6 6.4 maximum_bitcast_fusion
  797.4 8.9 collective-permute-done.106
  828.4 5.7 fusion.43
  834.1 10.4 %fusion.37 = f32[1024,2048]{1,0:T(8,128)} fusion(bf16[512,1024]{1,0:T(8,128)(2,1)S(1)} %slice-done.11, bf16[512,1024]{1,0:T(8,128)(2,1)S(1)} %slice-done.7, bf16[512,1024]{1,0:T(8,128)(2,1)S(1)} %slice-done.9, bf16[512,2048]{1,0:T(8,128)(2,1)} %copy-done.65, bf16[512,2048]{1,0:T(8,128)(2,1)S(1)} %copy-done.56, bf16[512,2048]{1,0:T(8,128)(2,1)S(1)} %copy-done.58), kind=kOutput, calls=%fused_computation.61 | convolution fusion | flops 6470762496 | bytes 17825792 | tf_op jit(solution)/shard_map/dot_general | solution.py:40
  854.0 7.9 fusion.123
  861.9 10.9 %collective-permute-done.110 = bf16[128,2048]{1,0:T(8,128)(2,1)S(1)} collective-permute-done((bf16[128,2048]{1,0:T(8,128)(2,1)S(1)}, bf16[128,2048]{1,0:T(8,128)(2,1)S(1)}, u32[]{:S(2)}, u32[]{:S(2)}) %collective-permute-start.110) | collective-permute-done | bytes 524320 | tf_op jit(solution)/shard_map/ppermute | solution.py:167
  876.9 5.7 fusion.148
  882.5 9.6 multiply_reduce_fusion
  930.1 9.8 collective-permute-done.121
  939.9 11.6 %collective-permute-done.119 = bf16[128,2048]{1,0:T(8,128)(2,1)S(1)} collective-permute-done((bf16[128,2048]{1,0:T(8,128)(2,1)S(1)}, bf16[128,2048]{1,0:T(8,128)(2,1)S(1)}, u32[]{:S(2)}, u32[]{:S(2)}) %collective-permute-start.119) | collective-permute-done | bytes 524320 | tf_op jit(solution)/shard_map/ppermute | solution.py:167
  951.5 20.0 %collective-permute-done.120 = bf16[128,2048]{1,0:T(8,128)(2,1)S(1)} collective-permute-done((bf16[128,2048]{1,0:T(8,128)(2,1)S(1)}, bf16[128,2048]{1,0:T(8,128)(2,1)S(1)}, u32[]{:S(2)}, u32[]{:S(2)}) %collective-permute-start.120) | collective-permute-done | bytes 524320 | tf_op jit(solution)/shard_map/ppermute | solution.py:167
  986.8 6.7 weave.1
  (971 shorter events, 511.6 us)
Async XLA Ops:
  14.9 31.0 %collective-permute-start.7 = (bf16[704,2048]{1,0:T(8,128)(2,1)}, bf16[704,2048]{1,0:T(8,128)(2,1)}, u32[]{:S(2)}, u32[]{:S(2)}) collective-permute-start(bf16[704,2048]{1,0:T(8,128)(2,1)} %get-tuple-element.322), channel_id=1, source_target_pairs={{0,4},{4,0},{8,12},{12,8},{16,20},{20,16},{24,28},{28,24},{1,5},{5... | collective-permute-start | bytes 8650760 | tf_op jit(solution)/shard_map/ppermute | solution.py:163
  14.9 31.6 %collective-permute-start.5 = (bf16[704,2048]{1,0:T(8,128)(2,1)}, bf16[704,2048]{1,0:T(8,128)(2,1)}, u32[]{:S(2)}, u32[]{:S(2)}) collective-permute-start(bf16[704,2048]{1,0:T(8,128)(2,1)} %get-tuple-element.318), channel_id=1, source_target_pairs={{0,4},{4,0},{8,12},{12,8},{16,20},{20,16},{24,28},{28,24},{1,5},{5... | collective-permute-start | bytes 8650760 | tf_op jit(solution)/shard_map/ppermute | solution.py:163
  15.4 31.1 %collective-permute-start.6 = (bf16[704,2048]{1,0:T(8,128)(2,1)}, bf16[704,2048]{1,0:T(8,128)(2,1)}, u32[]{:S(2)}, u32[]{:S(2)}) collective-permute-start(bf16[704,2048]{1,0:T(8,128)(2,1)} %get-tuple-element.320), channel_id=1, source_target_pairs={{0,4},{4,0},{8,12},{12,8},{16,20},{20,16},{24,28},{28,24},{1,5},{5... | collective-permute-start | bytes 8650760 | tf_op jit(solution)/shard_map/ppermute | solution.py:163
  45.9 45.2 %collective-permute-start.12 = (bf16[128,2048]{1,0:T(8,128)(2,1)S(1)}, bf16[128,2048]{1,0:T(8,128)(2,1)S(1)}, u32[]{:S(2)}, u32[]{:S(2)}) collective-permute-start(bf16[128,2048]{1,0:T(8,128)(2,1)S(1)} %constant_dynamic-update-slice_fusion), channel_id=1, source_target_pairs={{0,2},{1,3},{2,0},{3,1},{4,6},{5,7},{6,4},{7,5},{8,10},{9,11},{10,... | collective-permute-start | bytes 1572872 | tf_op jit(solution)/shard_map/ppermute | solution.py:167
  45.9 46.7 %collective-permute-start.11 = (bf16[128,2048]{1,0:T(8,128)(2,1)S(1)}, bf16[128,2048]{1,0:T(8,128)(2,1)S(1)}, u32[]{:S(2)}, u32[]{:S(2)}) collective-permute-start(bf16[128,2048]{1,0:T(8,128)(2,1)S(1)} %constant_dynamic-update-slice_fusion), channel_id=1, source_target_pairs={{0,1},{1,0},{2,3},{3,2},{4,5},{5,4},{6,7},{7,6},{8,9},{9,8},{10,11... | collective-permute-start | bytes 1572872 | tf_op jit(solution)/shard_map/ppermute | solution.py:167
  47.9 52.2 %collective-permute-start.17 = (bf16[256,2048]{1,0:T(8,128)(2,1)S(1)}, bf16[256,2048]{1,0:T(8,128)(2,1)S(1)}, u32[]{:S(2)}, u32[]{:S(2)}) collective-permute-start(bf16[256,2048]{1,0:T(8,128)(2,1)S(1)} %pad_maximum_fusion.16), channel_id=1, source_target_pairs={{0,16},{4,20},{8,24},{12,28},{16,0},{20,4},{24,8},{28,12},{1,17},{... | collective-permute-start | bytes 3145736 | tf_op jit(solution)/shard_map/ppermute | solution.py:163
  50.8 49.3 %collective-permute-start.18 = (bf16[192,2048]{1,0:T(8,128)(2,1)S(1)}, bf16[192,2048]{1,0:T(8,128)(2,1)S(1)}, u32[]{:S(2)}, u32[]{:S(2)}) collective-permute-start(bf16[192,2048]{1,0:T(8,128)(2,1)S(1)} %pad_maximum_fusion.20), channel_id=1, source_target_pairs={{0,8},{4,12},{8,0},{12,4},{16,24},{20,28},{24,16},{28,20},{1,9},{5... | collective-permute-start | bytes 2359304 | tf_op jit(solution)/shard_map/ppermute | solution.py:163
  58.9 36.8 %collective-permute-start.16 = (f32[4,8,128]{2,1,0:T(8,128)S(1)}, f32[4,8,128]{2,1,0:T(8,128)S(1)}, u32[]{:S(2)}, u32[]{:S(2)}) collective-permute-start(f32[4,8,128]{2,1,0:T(8,128)S(1)} %constant_dynamic-update-slice_fusion.2), channel_id=1, source_target_pairs={{0,24},{4,28},{8,16},{12,20},{16,8},{20,12},{24,0},{28,4},{1,25},{... | collective-permute-start | bytes 49160 | tf_op jit(solution)/shard_map/ppermute | solution.py:163
  95.7 39.0 %collective-permute-start.10 = (bf16[128,2048]{1,0:T(8,128)(2,1)}, bf16[128,2048]{1,0:T(8,128)(2,1)}, u32[]{:S(2)}, u32[]{:S(2)}) collective-permute-start(bf16[128,2048]{1,0:T(8,128)(2,1)} %param.14), channel_id=1, source_target_pairs={{0,2},{1,3},{2,0},{3,1},{4,6},{5,7},{6,4},{7,5},{8,10},{9,11},{10,... | collective-permute-start | bytes 1572872 | tf_op jit(solution)/shard_map/ppermute | solution.py:167
  98.9 44.9 %collective-permute-start.23 = (bf16[128,2048]{1,0:T(8,128)(2,1)}, bf16[128,2048]{1,0:T(8,128)(2,1)}, u32[]{:S(2)}, u32[]{:S(2)}) collective-permute-start(bf16[128,2048]{1,0:T(8,128)(2,1)} %param.14), channel_id=1, source_target_pairs={{0,3},{1,2},{2,1},{3,0},{4,7},{5,6},{6,5},{7,4},{8,11},{9,10},{10,... | collective-permute-start | bytes 1572872 | tf_op jit(solution)/shard_map/ppermute | solution.py:167
  119.1 128.5 %collective-permute-start.30 = (bf16[96,2048]{1,0:T(8,128)(2,1)}, bf16[96,2048]{1,0:T(8,128)(2,1)}, u32[]{:S(2)}, u32[]{:S(2)}) collective-permute-start(bf16[96,2048]{1,0:T(8,128)(2,1)} %fusion.53), channel_id=1, source_target_pairs={{0,1},{1,0},{2,3},{3,2},{4,5},{5,4},{6,7},{7,6},{8,9},{9,8},{10,11... | collective-permute-start | bytes 1179656 | tf_op jit(solution)/shard_map/ppermute | solution.py:167
  135.7 29.4 %collective-permute-start.26 = (bf16[192,2048]{1,0:T(8,128)(2,1)}, bf16[192,2048]{1,0:T(8,128)(2,1)}, u32[]{:S(2)}, u32[]{:S(2)}) collective-permute-start(bf16[192,2048]{1,0:T(8,128)(2,1)} %bitcast.33), channel_id=1, source_target_pairs={{0,8},{4,12},{8,0},{12,4},{16,24},{20,28},{24,16},{28,20},{1,9},{5... | collective-permute-start | bytes 2359304 | tf_op jit(solution)/shard_map/ppermute | solution.py:163
  137.9 27.2 %collective-permute-start.24 = (bf16[256,2048]{1,0:T(8,128)(2,1)}, bf16[256,2048]{1,0:T(8,128)(2,1)S(1)}, u32[]{:S(2)}, u32[]{:S(2)}) collective-permute-start(bf16[256,2048]{1,0:T(8,128)(2,1)} %pad_maximum_fusion.17), channel_id=1, source_target_pairs={{0,16},{4,20},{8,24},{12,28},{16,0},{20,4},{24,8},{28,12},{1,17},{... | collective-permute-start | bytes 3145736 | tf_op jit(solution)/shard_map/ppermute | solution.py:163
  139.2 25.8 %collective-permute-start.25 = (bf16[128,2048]{1,0:T(8,128)(2,1)}, bf16[128,2048]{1,0:T(8,128)(2,1)S(1)}, u32[]{:S(2)}, u32[]{:S(2)}) collective-permute-start(bf16[128,2048]{1,0:T(8,128)(2,1)} %collective-permute-done.10), channel_id=1, source_target_pairs={{0,8},{4,12},{8,0},{12,4},{16,24},{20,28},{24,16},{28,20},{1,9},{5... | collective-permute-start | bytes 1572872 | tf_op jit(solution)/shard_map/ppermute | solution.py:163
  143.8 167.3 %collective-permute-start.32 = (bf16[96,2048]{1,0:T(8,128)(2,1)}, bf16[96,2048]{1,0:T(8,128)(2,1)}, u32[]{:S(2)}, u32[]{:S(2)}) collective-permute-start(bf16[96,2048]{1,0:T(8,128)(2,1)} %fusion.55), channel_id=1, source_target_pairs={{0,3},{1,2},{2,1},{3,0},{4,7},{5,6},{6,5},{7,4},{8,11},{9,10},{10,... | collective-permute-start | bytes 1179656 | tf_op jit(solution)/shard_map/ppermute | solution.py:167
  165.6 34.8 %collective-permute-start.29 = (bf16[128,2048]{1,0:T(8,128)(2,1)}, bf16[128,2048]{1,0:T(8,128)(2,1)S(1)}, u32[]{:S(2)}, u32[]{:S(2)}) collective-permute-start(bf16[128,2048]{1,0:T(8,128)(2,1)} %collective-permute-done.23), channel_id=1, source_target_pairs={{0,8},{4,12},{8,0},{12,4},{16,24},{20,28},{24,16},{28,20},{1,9},{5... | collective-permute-start | bytes 1572872 | tf_op jit(solution)/shard_map/ppermute | solution.py:163
  168.2 32.3 %collective-permute-start.27 = (bf16[256,2048]{1,0:T(8,128)(2,1)S(1)}, bf16[256,2048]{1,0:T(8,128)(2,1)S(1)}, u32[]{:S(2)}, u32[]{:S(2)}) collective-permute-start(bf16[256,2048]{1,0:T(8,128)(2,1)S(1)} %pad_maximum_fusion.18), channel_id=1, source_target_pairs={{0,16},{4,20},{8,24},{12,28},{16,0},{20,4},{24,8},{28,12},{1,17},{... | collective-permute-start | bytes 3145736 | tf_op jit(solution)/shard_map/ppermute | solution.py:163
  170.2 29.1 %collective-permute-start.28 = (bf16[96,2048]{1,0:T(8,128)(2,1)S(1)}, bf16[96,2048]{1,0:T(8,128)(2,1)S(1)}, u32[]{:S(2)}, u32[]{:S(2)}) collective-permute-start(bf16[96,2048]{1,0:T(8,128)(2,1)S(1)} %fusion.158), channel_id=1, source_target_pairs={{0,16},{4,20},{8,24},{12,28},{16,0},{20,4},{24,8},{28,12},{1,17},{... | collective-permute-start | bytes 1179656 | tf_op jit(solution)/shard_map/ppermute | solution.py:163
  199.2 73.4 %collective-permute-start.33 = (bf16[96,2048]{1,0:T(8,128)(2,1)}, bf16[96,2048]{1,0:T(8,128)(2,1)}, u32[]{:S(2)}, u32[]{:S(2)}) collective-permute-start(bf16[96,2048]{1,0:T(8,128)(2,1)} %fusion.54), channel_id=1, source_target_pairs={{0,2},{1,3},{2,0},{3,1},{4,6},{5,7},{6,4},{7,5},{8,10},{9,11},{10,... | collective-permute-start | bytes 1179656 | tf_op jit(solution)/shard_map/ppermute | solution.py:167
  203.4 44.3 %collective-permute-start.31 = (bf16[256,2048]{1,0:T(8,128)(2,1)S(1)}, bf16[256,2048]{1,0:T(8,128)(2,1)}, u32[]{:S(2)}, u32[]{:S(2)}) collective-permute-start(bf16[256,2048]{1,0:T(8,128)(2,1)S(1)} %pad_maximum_fusion.19), channel_id=1, source_target_pairs={{0,16},{4,20},{8,24},{12,28},{16,0},{20,4},{24,8},{28,12},{1,17},{... | collective-permute-start | bytes 3145736 | tf_op jit(solution)/shard_map/ppermute | solution.py:163
  380.2 41.4 %collective-permute-start.58 = (bf16[96,2048]{1,0:T(8,128)(2,1)S(1)}, bf16[96,2048]{1,0:T(8,128)(2,1)S(1)}, u32[]{:S(2)}, u32[]{:S(2)}) collective-permute-start(bf16[96,2048]{1,0:T(8,128)(2,1)S(1)} %convolution_convert_fusion.15), channel_id=1, source_target_pairs={{0,3},{1,2},{2,1},{3,0},{4,7},{5,6},{6,5},{7,4},{8,11},{9,10},{10,... | collective-permute-start | bytes 1179656 | tf_op jit(solution)/shard_map/ppermute | solution.py:167
  390.9 30.8 %collective-permute-start.60 = (bf16[96,2048]{1,0:T(8,128)(2,1)S(1)}, bf16[96,2048]{1,0:T(8,128)(2,1)S(1)}, u32[]{:S(2)}, u32[]{:S(2)}) collective-permute-start(bf16[96,2048]{1,0:T(8,128)(2,1)S(1)} %collective-permute-done.51), channel_id=1, source_target_pairs={{0,8},{4,12},{8,0},{12,4},{16,24},{20,28},{24,16},{28,20},{1,9},{5... | collective-permute-start | bytes 1179656 | tf_op jit(solution)/shard_map/ppermute | solution.py:163
  391.9 29.7 %collective-permute-start.59 = (bf16[192,2048]{1,0:T(8,128)(2,1)S(1)}, bf16[192,2048]{1,0:T(8,128)(2,1)S(1)}, u32[]{:S(2)}, u32[]{:S(2)}) collective-permute-start(bf16[192,2048]{1,0:T(8,128)(2,1)S(1)} %pad_maximum_fusion.24), channel_id=1, source_target_pairs={{0,16},{4,20},{8,24},{12,28},{16,0},{20,4},{24,8},{28,12},{1,17},{... | collective-permute-start | bytes 2359304 | tf_op jit(solution)/shard_map/ppermute | solution.py:163
  434.7 28.7 %collective-permute-start.63 = (bf16[192,2048]{1,0:T(8,128)(2,1)S(1)}, bf16[192,2048]{1,0:T(8,128)(2,1)}, u32[]{:S(2)}, u32[]{:S(2)}) collective-permute-start(bf16[192,2048]{1,0:T(8,128)(2,1)S(1)} %pad_maximum_fusion.26), channel_id=1, source_target_pairs={{0,16},{4,20},{8,24},{12,28},{16,0},{20,4},{24,8},{28,12},{1,17},{... | collective-permute-start | bytes 2359304 | tf_op jit(solution)/shard_map/ppermute | solution.py:163
  436.8 26.6 %collective-permute-start.64 = (bf16[192,2048]{1,0:T(8,128)(2,1)S(1)}, bf16[192,2048]{1,0:T(8,128)(2,1)}, u32[]{:S(2)}, u32[]{:S(2)}) collective-permute-start(bf16[192,2048]{1,0:T(8,128)(2,1)S(1)} %bitcast.524), channel_id=1, source_target_pairs={{0,8},{4,12},{8,0},{12,4},{16,24},{20,28},{24,16},{28,20},{1,9},{5... | collective-permute-start | bytes 2359304 | tf_op jit(solution)/shard_map/ppermute | solution.py:163
  463.5 27.2 %collective-permute-start.66 = (bf16[192,2048]{1,0:T(8,128)(2,1)S(1)}, bf16[192,2048]{1,0:T(8,128)(2,1)}, u32[]{:S(2)}, u32[]{:S(2)}) collective-permute-start(bf16[192,2048]{1,0:T(8,128)(2,1)S(1)} %bitcast.525), channel_id=1, source_target_pairs={{0,8},{4,12},{8,0},{12,4},{16,24},{20,28},{24,16},{28,20},{1,9},{5... | collective-permute-start | bytes 2359304 | tf_op jit(solution)/shard_map/ppermute | solution.py:163
  578.8 41.4 %collective-permute-start.79 = (bf16[704,2048]{1,0:T(8,128)(2,1)S(1)}, bf16[704,2048]{1,0:T(8,128)(2,1)}, u32[]{:S(2)}, u32[]{:S(2)}) collective-permute-start(bf16[704,2048]{1,0:T(8,128)(2,1)S(1)} %slice.625), channel_id=1, source_target_pairs={{0,4},{4,0},{8,12},{12,8},{16,20},{20,16},{24,28},{28,24},{1,5},{5... | collective-permute-start | bytes 8650760 | tf_op jit(solution)/shard_map/ppermute | solution.py:163
  594.4 25.9 %collective-permute-start.82 = (bf16[192,2048]{1,0:T(8,128)(2,1)S(1)}, bf16[192,2048]{1,0:T(8,128)(2,1)S(1)}, u32[]{:S(2)}, u32[]{:S(2)}) collective-permute-start(bf16[192,2048]{1,0:T(8,128)(2,1)S(1)} %bitcast.526), channel_id=1, source_target_pairs={{0,8},{4,12},{8,0},{12,4},{16,24},{20,28},{24,16},{28,20},{1,9},{5... | collective-permute-start | bytes 2359304 | tf_op jit(solution)/shard_map/ppermute | solution.py:163
  625.7 33.2 %collective-permute-start.88 = (bf16[192,2048]{1,0:T(8,128)(2,1)S(1)}, bf16[192,2048]{1,0:T(8,128)(2,1)S(1)}, u32[]{:S(2)}, u32[]{:S(2)}) collective-permute-start(bf16[192,2048]{1,0:T(8,128)(2,1)S(1)} %bitcast.523), channel_id=1, source_target_pairs={{0,8},{4,12},{8,0},{12,4},{16,24},{20,28},{24,16},{28,20},{1,9},{5... | collective-permute-start | bytes 2359304 | tf_op jit(solution)/shard_map/ppermute | solution.py:163
  628.0 30.9 %collective-permute-start.86 = (bf16[96,2048]{1,0:T(8,128)(2,1)S(1)}, bf16[96,2048]{1,0:T(8,128)(2,1)S(1)}, u32[]{:S(2)}, u32[]{:S(2)}) collective-permute-start(bf16[96,2048]{1,0:T(8,128)(2,1)S(1)} %fusion.164), channel_id=1, source_target_pairs={{0,16},{4,20},{8,24},{12,28},{16,0},{20,4},{24,8},{28,12},{1,17},{... | collective-permute-start | bytes 1179656 | tf_op jit(solution)/shard_map/ppermute | solution.py:163
  629.3 29.5 %collective-permute-start.87 = (bf16[96,2048]{1,0:T(8,128)(2,1)S(1)}, bf16[96,2048]{1,0:T(8,128)(2,1)S(1)}, u32[]{:S(2)}, u32[]{:S(2)}) collective-permute-start(bf16[96,2048]{1,0:T(8,128)(2,1)S(1)} %collective-permute-done.77), channel_id=1, source_target_pairs={{0,8},{4,12},{8,0},{12,4},{16,24},{20,28},{24,16},{28,20},{1,9},{5... | collective-permute-start | bytes 1179656 | tf_op jit(solution)/shard_map/ppermute | solution.py:163
  630.0 28.8 %collective-permute-start.84 = (bf16[48,2048]{1,0:T(8,128)(2,1)S(1)}, bf16[48,2048]{1,0:T(8,128)(2,1)S(1)}, u32[]{:S(2)}, u32[]{:S(2)}) collective-permute-start(bf16[48,2048]{1,0:T(8,128)(2,1)S(1)} %slice.627), channel_id=1, source_target_pairs={{0,8},{4,12},{8,0},{12,4},{16,24},{20,28},{24,16},{28,20},{1,9},{5... | collective-permute-start | bytes 589832 | tf_op jit(solution)/shard_map/ppermute | solution.py:163
  635.1 41.6 %collective-permute-start.94 = (bf16[96,2048]{1,0:T(8,128)(2,1)S(1)}, bf16[96,2048]{1,0:T(8,128)(2,1)S(1)}, u32[]{:S(2)}, u32[]{:S(2)}) collective-permute-start(bf16[96,2048]{1,0:T(8,128)(2,1)S(1)} %fusion.56), channel_id=1, source_target_pairs={{0,8},{4,12},{8,0},{12,4},{16,24},{20,28},{24,16},{28,20},{1,9},{5... | collective-permute-start | bytes 1179656 | tf_op jit(solution)/shard_map/ppermute | solution.py:163
  663.4 26.6 %collective-permute-start.91 = (bf16[192,2048]{1,0:T(8,128)(2,1)}, bf16[192,2048]{1,0:T(8,128)(2,1)}, u32[]{:S(2)}, u32[]{:S(2)}) collective-permute-start(bf16[192,2048]{1,0:T(8,128)(2,1)} %pad_maximum_fusion.27), channel_id=1, source_target_pairs={{0,16},{4,20},{8,24},{12,28},{16,0},{20,4},{24,8},{28,12},{1,17},{... | collective-permute-start | bytes 2359304 | tf_op jit(solution)/shard_map/ppermute | solution.py:163
  664.9 25.2 %collective-permute-start.95 = (bf16[192,2048]{1,0:T(8,128)(2,1)}, bf16[192,2048]{1,0:T(8,128)(2,1)}, u32[]{:S(2)}, u32[]{:S(2)}) collective-permute-start(bf16[192,2048]{1,0:T(8,128)(2,1)} %bitcast.98), channel_id=1, source_target_pairs={{0,8},{4,12},{8,0},{12,4},{16,24},{20,28},{24,16},{28,20},{1,9},{5... | collective-permute-start | bytes 2359304 | tf_op jit(solution)/shard_map/ppermute | solution.py:163
  665.8 24.3 %collective-permute-start.89 = (bf16[704,2048]{1,0:T(8,128)(2,1)S(1)}, bf16[704,2048]{1,0:T(8,128)(2,1)S(1)}, u32[]{:S(2)}, u32[]{:S(2)}) collective-permute-start(bf16[704,2048]{1,0:T(8,128)(2,1)S(1)} %slice.633), channel_id=1, source_target_pairs={{0,4},{4,0},{8,12},{12,8},{16,20},{20,16},{24,28},{28,24},{1,5},{5... | collective-permute-start | bytes 8650760 | tf_op jit(solution)/shard_map/ppermute | solution.py:163
  702.4 42.3 %collective-permute-start.97 = (bf16[192,2048]{1,0:T(8,128)(2,1)}, bf16[192,2048]{1,0:T(8,128)(2,1)S(1)}, u32[]{:S(2)}, u32[]{:S(2)}) collective-permute-start(bf16[192,2048]{1,0:T(8,128)(2,1)} %pad_maximum_fusion.28), channel_id=1, source_target_pairs={{0,16},{4,20},{8,24},{12,28},{16,0},{20,4},{24,8},{28,12},{1,17},{... | collective-permute-start | bytes 2359304 | tf_op jit(solution)/shard_map/ppermute | solution.py:163
  703.7 41.0 %collective-permute-start.98 = (bf16[192,2048]{1,0:T(8,128)(2,1)}, bf16[192,2048]{1,0:T(8,128)(2,1)}, u32[]{:S(2)}, u32[]{:S(2)}) collective-permute-start(bf16[192,2048]{1,0:T(8,128)(2,1)} %pad_maximum_fusion.29), channel_id=1, source_target_pairs={{0,16},{4,20},{8,24},{12,28},{16,0},{20,4},{24,8},{28,12},{1,17},{... | collective-permute-start | bytes 2359304 | tf_op jit(solution)/shard_map/ppermute | solution.py:163
  704.4 40.3 %collective-permute-start.100 = (bf16[192,2048]{1,0:T(8,128)(2,1)}, bf16[192,2048]{1,0:T(8,128)(2,1)}, u32[]{:S(2)}, u32[]{:S(2)}) collective-permute-start(bf16[192,2048]{1,0:T(8,128)(2,1)} %bitcast.104), channel_id=1, source_target_pairs={{0,8},{4,12},{8,0},{12,4},{16,24},{20,28},{24,16},{28,20},{1,9},{5... | collective-permute-start | bytes 2359304 | tf_op jit(solution)/shard_map/ppermute | solution.py:163
  714.6 30.1 %collective-permute-start.99 = (bf16[96,2048]{1,0:T(8,128)(2,1)S(1)}, bf16[96,2048]{1,0:T(8,128)(2,1)S(1)}, u32[]{:S(2)}, u32[]{:S(2)}) collective-permute-start(bf16[96,2048]{1,0:T(8,128)(2,1)S(1)} %fusion.166), channel_id=1, source_target_pairs={{0,16},{4,20},{8,24},{12,28},{16,0},{20,4},{24,8},{28,12},{1,17},{... | collective-permute-start | bytes 1179656 | tf_op jit(solution)/shard_map/ppermute | solution.py:163
  747.2 26.4 %collective-permute-start.104 = (bf16[256,2048]{1,0:T(8,128)(2,1)S(1)}, bf16[256,2048]{1,0:T(8,128)(2,1)}, u32[]{:S(2)}, u32[]{:S(2)}) collective-permute-start(bf16[256,2048]{1,0:T(8,128)(2,1)S(1)} %bitcast.521), channel_id=1, source_target_pairs={{0,8},{4,12},{8,0},{12,4},{16,24},{20,28},{24,16},{28,20},{1,9},{5... | collective-permute-start | bytes 3145736 | tf_op jit(solution)/shard_map/ppermute | solution.py:163
  781.5 24.8 %collective-permute-start.106 = (bf16[256,2048]{1,0:T(8,128)(2,1)S(1)}, bf16[256,2048]{1,0:T(8,128)(2,1)S(1)}, u32[]{:S(2)}, u32[]{:S(2)}) collective-permute-start(bf16[256,2048]{1,0:T(8,128)(2,1)S(1)} %bitcast.520), channel_id=1, source_target_pairs={{0,8},{4,12},{8,0},{12,4},{16,24},{20,28},{24,16},{28,20},{1,9},{5... | collective-permute-start | bytes 3145736 | tf_op jit(solution)/shard_map/ppermute | solution.py:163
  809.5 37.7 %collective-permute-start.107 = (bf16[128,2048]{1,0:T(8,128)(2,1)}, bf16[128,2048]{1,0:T(8,128)(2,1)}, u32[]{:S(2)}, u32[]{:S(2)}) collective-permute-start(bf16[128,2048]{1,0:T(8,128)(2,1)} %add_convert_fusion.7), channel_id=1, source_target_pairs={{0,1},{1,0},{2,3},{3,2},{4,5},{5,4},{6,7},{7,6},{8,9},{9,8},{10,11... | collective-permute-start | bytes 1572872 | tf_op jit(solution)/shard_map/ppermute | solution.py:167
  810.5 36.7 %collective-permute-start.109 = (bf16[256,2048]{1,0:T(8,128)(2,1)}, bf16[256,2048]{1,0:T(8,128)(2,1)}, u32[]{:S(2)}, u32[]{:S(2)}) collective-permute-start(bf16[256,2048]{1,0:T(8,128)(2,1)} %bitcast.122), channel_id=1, source_target_pairs={{0,8},{4,12},{8,0},{12,4},{16,24},{20,28},{24,16},{28,20},{1,9},{5... | collective-permute-start | bytes 3145736 | tf_op jit(solution)/shard_map/ppermute | solution.py:163
  812.5 34.7 %collective-permute-start.108 = (bf16[128,2048]{1,0:T(8,128)(2,1)}, bf16[128,2048]{1,0:T(8,128)(2,1)}, u32[]{:S(2)}, u32[]{:S(2)}) collective-permute-start(bf16[128,2048]{1,0:T(8,128)(2,1)} %fusion.154), channel_id=1, source_target_pairs={{0,16},{4,20},{8,24},{12,28},{16,0},{20,4},{24,8},{28,12},{1,17},{... | collective-permute-start | bytes 1572872 | tf_op jit(solution)/shard_map/ppermute | solution.py:163
  920.2 51.3 %collective-permute-start.118 = (bf16[256,2048]{1,0:T(8,128)(2,1)S(1)}, bf16[256,2048]{1,0:T(8,128)(2,1)S(1)}, u32[]{:S(2)}, u32[]{:S(2)}) collective-permute-start(bf16[256,2048]{1,0:T(8,128)(2,1)S(1)} %slice.998), channel_id=1, source_target_pairs={{0,4},{4,0},{8,12},{12,8},{16,20},{20,16},{24,28},{28,24},{1,5},{5... | collective-permute-start | bytes 3145736 | tf_op jit(solution)/shard_map/ppermute | solution.py:163
  925.3 26.2 %collective-permute-start.119 = (bf16[128,2048]{1,0:T(8,128)(2,1)S(1)}, bf16[128,2048]{1,0:T(8,128)(2,1)S(1)}, u32[]{:S(2)}, u32[]{:S(2)}) collective-permute-start(bf16[128,2048]{1,0:T(8,128)(2,1)S(1)} %get-tuple-element.577), channel_id=1, source_target_pairs={{0,1},{1,0},{2,3},{3,2},{4,5},{5,4},{6,7},{7,6},{8,9},{9,8},{10,11... | collective-permute-start | bytes 1572872 | tf_op jit(solution)/shard_map/ppermute | solution.py:167
  925.3 46.2 %collective-permute-start.120 = (bf16[128,2048]{1,0:T(8,128)(2,1)S(1)}, bf16[128,2048]{1,0:T(8,128)(2,1)S(1)}, u32[]{:S(2)}, u32[]{:S(2)}) collective-permute-start(bf16[128,2048]{1,0:T(8,128)(2,1)S(1)} %get-tuple-element.578), channel_id=1, source_target_pairs={{0,2},{1,3},{2,0},{3,1},{4,6},{5,7},{6,4},{7,5},{8,10},{9,11},{10,... | collective-permute-start | bytes 1572872 | tf_op jit(solution)/shard_map/ppermute | solution.py:167
  (279 other events, 3571.6 us)

commit v3 on v2

--- a/solution.py
+++ b/solution.py
@@ -147,11 +147,10 @@
         return (rows,)
 
     def column_scatter(self, part):
-        total = lax.psum_scatter(
-            part[0].astype(bf16), "expert", scatter_dimension=0, tiled=True
-        )
+        part = part[:, 0].reshape(2, self.experts, -1, part.shape[-1]).astype(bf16)
+        total = lax.psum_scatter(part, "expert", scatter_dimension=1, tiled=True)
         (total,) = yield (total,)
-        return total[0].astype(f32)
+        return total.reshape(-1, part.shape[-1]).astype(f32)
 
     def totals(self, sums, peak):
         yield ()
@@ -309,9 +308,16 @@
         return (mine, other)
 
     def column_scatter(self, part):
-        (other,) = yield (swap(part[1].astype(bf16), CORE),)
-        mine = part[0] + other.astype(f32)
-        total = yield from self.line_reduce(self.reorder([mine[i] for i in range(4)]))
+        size, width = part.shape[2] // 4, part.shape[3]
+        other = swap(part[:, 1].astype(bf16).reshape(-1, width), CORE)
+        own, other = yield (part[:, 0], other)
+        mine = own + other.astype(f32).reshape(2, -1, width)
+        place = lax.axis_index("expert")
+        blocks = [
+            lax.dynamic_slice_in_dim(mine, (place ^ r) * size, size, 1).reshape(-1, width)
+            for r in range(4)
+        ]
+        total = yield from self.line_reduce(blocks)
         return total
 
     def steps(self, block, merge):
@@ -824,19 +830,16 @@
             part = dot_nn(grads, box["qkv_w"]).astype(bf16)
             box["grads", r], part = yield from gated((grads, part), ("attn_grad_rows", later))
             spawn(gather_input(parts, r, part))
-            if r == early[-1]:
-                kv_sum = dot_tn(*early_rows(wide, None))
-                q_sum = dot_tn(*early_rows(0, wide))
-                kv_sum, q_sum = yield (kv_sum, q_sum)
+        kv_sum, q_sum = (dot_tn(*early_rows(*span)) for span in ((wide, None), (0, wide)))
         grads, rows = box["grads", last], box["normed", last]
         kv_grad = kv_sum + dot_tn(grads[:, wide:], rows)
-        gain_one = jnp.sum(kv_grad * box["qkv_w"][wide:].astype(f32), axis=0, keepdims=True)
         kv_grad, grads, rows = yield (kv_grad, grads, rows)
         spawn(project_grads(kv_grad))
         q_grad = q_sum + dot_tn(grads[:, :wide], rows)
-        more = jnp.sum(q_grad * box["qkv_w"][:wide].astype(f32), axis=0, keepdims=True)
-        (q_grad,) = yield (q_grad,)
-        box["gain_one_grad"] = (gain_one + more) / box["gain_one"]
+        kv_grad, q_grad = yield (kv_grad, q_grad)
+        both = jnp.concatenate([q_grad, kv_grad], axis=0)
+        gain_one = jnp.sum(both * box["qkv_w"].astype(f32), axis=0, keepdims=True)
+        box["gain_one_grad"] = gain_one / box["gain_one"]
         spawn(gather_totals())
         query_grad = yield from links.pair_scatter(q_grad)
         out_grads = dot_tn(joined("mixed"), joined("attn_grad_rows"))
@@ -855,11 +858,7 @@
         box["gains"], box["peaks"] = yield from links.totals(gain_sums, peak_vec)
 
     def project_grads(part):
-        column = (links.pair, experts, key_rows, width)
-        part = jnp.concatenate(
-            [part[:wide].reshape(column), part[wide:].reshape(column)], axis=2
-        )
-        total = yield from links.column_scatter(part)
+        total = yield from links.column_scatter(part.reshape(2, links.pair, wide // links.pair, -1))
         box["k_grad"], box["v_grad"] = total[:key_rows], total[key_rows:]
 
     def gather_input(parts, r, part):

time: 1000 us -> 1010 us (1.010); the launches traced: 994 us -> 994 us
    unnamed x434 -> x442, local copies, waits for them, and re-layouts: 58.8 us -> 63.1 us
where the time goes in v3:
time: 1010 us; the launch traced here: 994 us
  waiting for transfers between devices  343 us (34%)
  matrix products  235 us (23%)
  starting transfers between devices  146 us (14%)
  other arithmetic  129 us (13%)
  local copies, waits for them, and re-layouts  101 us (10%)
  Pallas kernels  33.4 us (3%)
    ppermute x94, waiting for transfers between devices, swap(): return lax.ppermute(block, 'dp', [(i, i ^ mask) for i in range(8)])  212 us
    ppermute x36, waiting for transfers between devices, flip(): return lax.ppermute(block, 'expert', [(i, i ^ mask) for i in range(4)])  131 us
    dot_general x20, matrix products, dot_nt(): lax.dot_general(left, right, (((1,), (1,)), ((), ())), preferred_element_...  89.6 us
    ppermute x94, starting transfers between devices, swap(): return lax.ppermute(block, 'dp', [(i, i ^ mask) for i in range(8)])  87.5 us
    dot_general x38, matrix products, dot_nn(): lax.dot_general(left, right, (((1,), (0,)), ((), ())), preferred_element_...  73.2 us
    dot_general x13, matrix products, dot_tn(): lax.dot_general(left, right, (((0,), (0,)), ((), ())), preferred_element_...  72.4 us
    unnamed x442, local copies, waits for them, and re-layouts  63.1 us
    ppermute x36, starting transfers between devices, flip(): return lax.ppermute(block, 'expert', [(i, i ^ mask) for i in range(4)])  58.8 us
  transfers between devices with their start and end apart: 130, of which 47 were waited for; matrix products, arithmetic and copies ran while one was open for 39% of the time, Pallas kernels for 3%

profile of v3, /device:TPU:0, one launch (start us, length us, event | category | flops | bytes accessed | tf_op | source)
XLA Modules:
  0.0 993.7 jit_solution(16672304433066697989)
XLA Ops:
  3.7 5.1 collective-permute-start.2
  8.8 6.1 slice_bitcast_fusion.1
  52.4 6.5 collective-permute-done.13
  61.4 29.7 %collective-permute-done.12 = bf16[128,2048]{1,0:T(8,128)(2,1)S(1)} collective-permute-done((bf16[128,2048]{1,0:T(8,128)(2,1)S(1)}, bf16[128,2048]{1,0:T(8,128)(2,1)S(1)}, u32[]{:S(2)}, u32[]{:S(2)}) %collective-permute-start.12) | collective-permute-done | bytes 524320 | tf_op jit(solution)/shard_map/ppermute | solution.py:166
  106.2 12.9 %collective-permute-done.20 = bf16[128,2048]{1,0:T(8,128)(2,1)S(1)} collective-permute-done((bf16[128,2048]{1,0:T(8,128)(2,1)}, bf16[128,2048]{1,0:T(8,128)(2,1)S(1)}, u32[]{:S(2)}, u32[]{:S(2)}) %collective-permute-start.20) | collective-permute-done | bytes 524320 | tf_op jit(solution)/shard_map/ppermute | solution.py:166
  146.5 18.8 %collective-permute-done.25 = bf16[128,2048]{1,0:T(8,128)(2,1)S(1)} collective-permute-done((bf16[128,2048]{1,0:T(8,128)(2,1)}, bf16[128,2048]{1,0:T(8,128)(2,1)S(1)}, u32[]{:S(2)}, u32[]{:S(2)}) %collective-permute-start.25) | collective-permute-done | bytes 524320 | tf_op jit(solution)/shard_map/ppermute | solution.py:162
  171.9 27.3 %collective-permute-done.28 = bf16[96,2048]{1,0:T(8,128)(2,1)S(1)} collective-permute-done((bf16[96,2048]{1,0:T(8,128)(2,1)S(1)}, bf16[96,2048]{1,0:T(8,128)(2,1)S(1)}, u32[]{:S(2)}, u32[]{:S(2)}) %collective-permute-start.28) | collective-permute-done | bytes 393248 | tf_op jit(solution)/shard_map/ppermute | solution.py:162
  204.0 5.3 fusion.33
  216.3 6.2 pad_maximum_fusion.1
  227.0 6.4 pad_maximum_fusion.2
  233.4 6.3 pad_maximum_fusion.3
  262.2 5.3 fusion.62
  273.0 6.9 collective-permute-done.36
  279.9 5.4 collective-permute-done.37
  292.8 11.9 %collective-permute-done.42 = bf16[48,2048]{1,0:T(8,128)(2,1)S(1)} collective-permute-done((bf16[48,2048]{1,0:T(8,128)(2,1)S(1)}, bf16[48,2048]{1,0:T(8,128)(2,1)S(1)}, u32[]{:S(2)}, u32[]{:S(2)}) %collective-permute-start.42) | collective-permute-done | bytes 196640 | tf_op jit(solution)/shard_map/ppermute | solution.py:162
  317.7 6.3 collective-permute-done.45
  324.0 6.2 collective-permute-done.43
  339.0 6.8 fusion.70
  352.4 5.1 collective-permute-done.47
  366.9 5.5 fusion.78
  398.3 7.0 multiply_convert_fusion.9
  408.0 5.1 fusion.86
  440.2 7.7 multiply_convert_fusion.6
  447.9 5.2 convolution_convert_fusion.9
  475.4 7.1 multiply_convert_fusion.3
  491.7 7.4 multiply_convert_fusion
  511.9 6.7 collective-permute-done.67
  538.0 8.5 collective-permute-done.73
  548.5 7.9 collective-permute-done.76
  565.3 11.5 %convolution_convert_fusion.2 = bf16[1408,2048]{1,0:T(8,128)(2,1)S(1)} fusion(bf16[1536,2048]{1,0:T(8,128)(2,1)} %get-tuple-element.608, bf16[384,1408]{1,0:T(8,128)(2,1)S(1)} %copy-done.171, bf16[384,1408]{1,0:T(8,128)(2,1)S(1)} %copy-done.170, bf16[384,1408]{1,0:T(8,128)(2,1)S(1)} %copy-done.168, bf16[384,1408]{1,0:T(8,128)(2,1)S(1)} %copy-done.166), kind=kOutput, calls=%fused_computation.5 | convolution fusion | flops 8878555136 | bytes 16384000 | tf_op jit(solution)/shard_map/dot_general | solution.py:40
  579.2 12.7 %convolution_convert_fusion.1 = bf16[1408,2048]{1,0:T(8,128)(2,1)S(1)} fusion(bf16[1536,2048]{1,0:T(8,128)(2,1)} %get-tuple-element.608, bf16[384,1408]{1,0:T(8,128)(2,1)} %copy-done.164, bf16[384,1408]{1,0:T(8,128)(2,1)} %copy-done.163, bf16[384,1408]{1,0:T(8,128)(2,1)} %get-tuple-element.566, bf16[384,1408]{1,0:T(8,128)(2,1)S(1)} %copy-done.161), kind=kOutput, calls=%fused_computation.4 | convolution fusion | flops 8878555136 | bytes 16384000 | tf_op jit(solution)/shard_map/dot_general | solution.py:40
  596.1 13.4 %convolution_convert_fusion = bf16[1408,2048]{1,0:T(8,128)(2,1)} fusion(bf16[1536,2048]{1,0:T(8,128)(2,1)} %get-tuple-element.596, bf16[384,1408]{1,0:T(8,128)(2,1)S(1)} %copy-done.178, bf16[384,1408]{1,0:T(8,128)(2,1)S(1)} %copy-done.176, bf16[384,1408]{1,0:T(8,128)(2,1)S(1)} %copy-done.174, bf16[384,1408]{1,0:T(8,128)(2,1)S(1)} %copy-done.173), kind=kOutput, calls=%fused_computation.3 | convolution fusion | flops 8878555136 | bytes 16384000 | tf_op jit(solution)/shard_map/dot_general | solution.py:40
  614.0 8.0 collective-permute-done.82
  637.4 23.1 %collective-permute-done.84 = bf16[48,2048]{1,0:T(8,128)(2,1)S(1)} collective-permute-done((bf16[48,2048]{1,0:T(8,128)(2,1)S(1)}, bf16[48,2048]{1,0:T(8,128)(2,1)S(1)}, u32[]{:S(2)}, u32[]{:S(2)}) %collective-permute-start.84) | collective-permute-done | bytes 196640 | tf_op jit(solution)/shard_map/ppermute | solution.py:162
  682.9 9.7 collective-permute-done.93
  720.1 28.3 %collective-permute-done.99 = bf16[96,2048]{1,0:T(8,128)(2,1)S(1)} collective-permute-done((bf16[96,2048]{1,0:T(8,128)(2,1)S(1)}, bf16[96,2048]{1,0:T(8,128)(2,1)S(1)}, u32[]{:S(2)}, u32[]{:S(2)}) %collective-permute-start.99) | collective-permute-done | bytes 393248 | tf_op jit(solution)/shard_map/ppermute | solution.py:162
  769.9 8.6 collective-permute-done.103
  779.3 5.4 add_bitcast_fusion
  790.2 6.4 maximum_bitcast_fusion
  802.1 8.8 collective-permute-done.106
  823.9 4.7 convolution_convert_fusion.3
  840.1 8.6 fusion.34
  848.8 8.2 fusion.119
  873.6 15.1 %collective-permute-done.110 = bf16[128,2048]{1,0:T(8,128)(2,1)S(1)} collective-permute-done((bf16[128,2048]{1,0:T(8,128)(2,1)S(1)}, bf16[128,2048]{1,0:T(8,128)(2,1)S(1)}, u32[]{:S(2)}, u32[]{:S(2)}) %collective-permute-start.110) | collective-permute-done | bytes 524320 | tf_op jit(solution)/shard_map/ppermute | solution.py:166
  908.2 8.4 fusion
  918.5 6.1 collective-permute-start.123
  939.1 32.5 %collective-permute-done.122 = f32[3,2048]{1,0:T(4,128)S(1)} collective-permute-done((f32[3,2048]{1,0:T(4,128)S(1)}, f32[3,2048]{1,0:T(4,128)S(1)}, u32[]{:S(2)}, u32[]{:S(2)}) %collective-permute-start.122) | collective-permute-done | bytes 24608 | tf_op jit(solution)/shard_map/ppermute | solution.py:166
  986.6 6.7 weave.1
  (979 shorter events, 510.3 us)
Async XLA Ops:
  14.9 31.0 %collective-permute-start.7 = (bf16[704,2048]{1,0:T(8,128)(2,1)}, bf16[704,2048]{1,0:T(8,128)(2,1)}, u32[]{:S(2)}, u32[]{:S(2)}) collective-permute-start(bf16[704,2048]{1,0:T(8,128)(2,1)} %get-tuple-element.322), channel_id=1, source_target_pairs={{0,4},{4,0},{8,12},{12,8},{16,20},{20,16},{24,28},{28,24},{1,5},{5... | collective-permute-start | bytes 8650760 | tf_op jit(solution)/shard_map/ppermute | solution.py:162
  14.9 31.7 %collective-permute-start.5 = (bf16[704,2048]{1,0:T(8,128)(2,1)}, bf16[704,2048]{1,0:T(8,128)(2,1)}, u32[]{:S(2)}, u32[]{:S(2)}) collective-permute-start(bf16[704,2048]{1,0:T(8,128)(2,1)} %get-tuple-element.318), channel_id=1, source_target_pairs={{0,4},{4,0},{8,12},{12,8},{16,20},{20,16},{24,28},{28,24},{1,5},{5... | collective-permute-start | bytes 8650760 | tf_op jit(solution)/shard_map/ppermute | solution.py:162
  15.4 31.2 %collective-permute-start.6 = (bf16[704,2048]{1,0:T(8,128)(2,1)}, bf16[704,2048]{1,0:T(8,128)(2,1)}, u32[]{:S(2)}, u32[]{:S(2)}) collective-permute-start(bf16[704,2048]{1,0:T(8,128)(2,1)} %get-tuple-element.320), channel_id=1, source_target_pairs={{0,4},{4,0},{8,12},{12,8},{16,20},{20,16},{24,28},{28,24},{1,5},{5... | collective-permute-start | bytes 8650760 | tf_op jit(solution)/shard_map/ppermute | solution.py:162
  45.9 45.2 %collective-permute-start.12 = (bf16[128,2048]{1,0:T(8,128)(2,1)S(1)}, bf16[128,2048]{1,0:T(8,128)(2,1)S(1)}, u32[]{:S(2)}, u32[]{:S(2)}) collective-permute-start(bf16[128,2048]{1,0:T(8,128)(2,1)S(1)} %constant_dynamic-update-slice_fusion), channel_id=1, source_target_pairs={{0,2},{1,3},{2,0},{3,1},{4,6},{5,7},{6,4},{7,5},{8,10},{9,11},{10,... | collective-permute-start | bytes 1572872 | tf_op jit(solution)/shard_map/ppermute | solution.py:166
  45.9 46.7 %collective-permute-start.11 = (bf16[128,2048]{1,0:T(8,128)(2,1)S(1)}, bf16[128,2048]{1,0:T(8,128)(2,1)S(1)}, u32[]{:S(2)}, u32[]{:S(2)}) collective-permute-start(bf16[128,2048]{1,0:T(8,128)(2,1)S(1)} %constant_dynamic-update-slice_fusion), channel_id=1, source_target_pairs={{0,1},{1,0},{2,3},{3,2},{4,5},{5,4},{6,7},{7,6},{8,9},{9,8},{10,11... | collective-permute-start | bytes 1572872 | tf_op jit(solution)/shard_map/ppermute | solution.py:166
  47.9 52.2 %collective-permute-start.17 = (bf16[256,2048]{1,0:T(8,128)(2,1)S(1)}, bf16[256,2048]{1,0:T(8,128)(2,1)S(1)}, u32[]{:S(2)}, u32[]{:S(2)}) collective-permute-start(bf16[256,2048]{1,0:T(8,128)(2,1)S(1)} %pad_maximum_fusion.15), channel_id=1, source_target_pairs={{0,16},{4,20},{8,24},{12,28},{16,0},{20,4},{24,8},{28,12},{1,17},{... | collective-permute-start | bytes 3145736 | tf_op jit(solution)/shard_map/ppermute | solution.py:162
  50.8 49.3 %collective-permute-start.18 = (bf16[192,2048]{1,0:T(8,128)(2,1)S(1)}, bf16[192,2048]{1,0:T(8,128)(2,1)S(1)}, u32[]{:S(2)}, u32[]{:S(2)}) collective-permute-start(bf16[192,2048]{1,0:T(8,128)(2,1)S(1)} %pad_maximum_fusion.19), channel_id=1, source_target_pairs={{0,8},{4,12},{8,0},{12,4},{16,24},{20,28},{24,16},{28,20},{1,9},{5... | collective-permute-start | bytes 2359304 | tf_op jit(solution)/shard_map/ppermute | solution.py:162
  58.9 36.8 %collective-permute-start.16 = (f32[4,8,128]{2,1,0:T(8,128)S(1)}, f32[4,8,128]{2,1,0:T(8,128)S(1)}, u32[]{:S(2)}, u32[]{:S(2)}) collective-permute-start(f32[4,8,128]{2,1,0:T(8,128)S(1)} %constant_dynamic-update-slice_fusion.2), channel_id=1, source_target_pairs={{0,24},{4,28},{8,16},{12,20},{16,8},{20,12},{24,0},{28,4},{1,25},{... | collective-permute-start | bytes 49160 | tf_op jit(solution)/shard_map/ppermute | solution.py:162
  95.7 39.1 %collective-permute-start.10 = (bf16[128,2048]{1,0:T(8,128)(2,1)}, bf16[128,2048]{1,0:T(8,128)(2,1)}, u32[]{:S(2)}, u32[]{:S(2)}) collective-permute-start(bf16[128,2048]{1,0:T(8,128)(2,1)} %param.14), channel_id=1, source_target_pairs={{0,2},{1,3},{2,0},{3,1},{4,6},{5,7},{6,4},{7,5},{8,10},{9,11},{10,... | collective-permute-start | bytes 1572872 | tf_op jit(solution)/shard_map/ppermute | solution.py:166
  98.9 45.0 %collective-permute-start.23 = (bf16[128,2048]{1,0:T(8,128)(2,1)}, bf16[128,2048]{1,0:T(8,128)(2,1)}, u32[]{:S(2)}, u32[]{:S(2)}) collective-permute-start(bf16[128,2048]{1,0:T(8,128)(2,1)} %param.14), channel_id=1, source_target_pairs={{0,3},{1,2},{2,1},{3,0},{4,7},{5,6},{6,5},{7,4},{8,11},{9,10},{10,... | collective-permute-start | bytes 1572872 | tf_op jit(solution)/shard_map/ppermute | solution.py:166
  119.1 128.7 %collective-permute-start.30 = (bf16[96,2048]{1,0:T(8,128)(2,1)}, bf16[96,2048]{1,0:T(8,128)(2,1)}, u32[]{:S(2)}, u32[]{:S(2)}) collective-permute-start(bf16[96,2048]{1,0:T(8,128)(2,1)} %fusion.50), channel_id=1, source_target_pairs={{0,1},{1,0},{2,3},{3,2},{4,5},{5,4},{6,7},{7,6},{8,9},{9,8},{10,11... | collective-permute-start | bytes 1179656 | tf_op jit(solution)/shard_map/ppermute | solution.py:166
  135.8 29.5 %collective-permute-start.26 = (bf16[192,2048]{1,0:T(8,128)(2,1)}, bf16[192,2048]{1,0:T(8,128)(2,1)}, u32[]{:S(2)}, u32[]{:S(2)}) collective-permute-start(bf16[192,2048]{1,0:T(8,128)(2,1)} %bitcast.33), channel_id=1, source_target_pairs={{0,8},{4,12},{8,0},{12,4},{16,24},{20,28},{24,16},{28,20},{1,9},{5... | collective-permute-start | bytes 2359304 | tf_op jit(solution)/shard_map/ppermute | solution.py:162
  137.9 27.4 %collective-permute-start.24 = (bf16[256,2048]{1,0:T(8,128)(2,1)}, bf16[256,2048]{1,0:T(8,128)(2,1)S(1)}, u32[]{:S(2)}, u32[]{:S(2)}) collective-permute-start(bf16[256,2048]{1,0:T(8,128)(2,1)} %pad_maximum_fusion.16), channel_id=1, source_target_pairs={{0,16},{4,20},{8,24},{12,28},{16,0},{20,4},{24,8},{28,12},{1,17},{... | collective-permute-start | bytes 3145736 | tf_op jit(solution)/shard_map/ppermute | solution.py:162
  139.3 26.0 %collective-permute-start.25 = (bf16[128,2048]{1,0:T(8,128)(2,1)}, bf16[128,2048]{1,0:T(8,128)(2,1)S(1)}, u32[]{:S(2)}, u32[]{:S(2)}) collective-permute-start(bf16[128,2048]{1,0:T(8,128)(2,1)} %collective-permute-done.10), channel_id=1, source_target_pairs={{0,8},{4,12},{8,0},{12,4},{16,24},{20,28},{24,16},{28,20},{1,9},{5... | collective-permute-start | bytes 1572872 | tf_op jit(solution)/shard_map/ppermute | solution.py:162
  143.9 167.4 %collective-permute-start.32 = (bf16[96,2048]{1,0:T(8,128)(2,1)}, bf16[96,2048]{1,0:T(8,128)(2,1)}, u32[]{:S(2)}, u32[]{:S(2)}) collective-permute-start(bf16[96,2048]{1,0:T(8,128)(2,1)} %fusion.52), channel_id=1, source_target_pairs={{0,3},{1,2},{2,1},{3,0},{4,7},{5,6},{6,5},{7,4},{8,11},{9,10},{10,... | collective-permute-start | bytes 1179656 | tf_op jit(solution)/shard_map/ppermute | solution.py:166
  165.8 34.6 %collective-permute-start.29 = (bf16[128,2048]{1,0:T(8,128)(2,1)}, bf16[128,2048]{1,0:T(8,128)(2,1)S(1)}, u32[]{:S(2)}, u32[]{:S(2)}) collective-permute-start(bf16[128,2048]{1,0:T(8,128)(2,1)} %collective-permute-done.23), channel_id=1, source_target_pairs={{0,8},{4,12},{8,0},{12,4},{16,24},{20,28},{24,16},{28,20},{1,9},{5... | collective-permute-start | bytes 1572872 | tf_op jit(solution)/shard_map/ppermute | solution.py:162
  168.1 32.3 %collective-permute-start.27 = (bf16[256,2048]{1,0:T(8,128)(2,1)S(1)}, bf16[256,2048]{1,0:T(8,128)(2,1)S(1)}, u32[]{:S(2)}, u32[]{:S(2)}) collective-permute-start(bf16[256,2048]{1,0:T(8,128)(2,1)S(1)} %pad_maximum_fusion.17), channel_id=1, source_target_pairs={{0,16},{4,20},{8,24},{12,28},{16,0},{20,4},{24,8},{28,12},{1,17},{... | collective-permute-start | bytes 3145736 | tf_op jit(solution)/shard_map/ppermute | solution.py:162
  170.3 28.9 %collective-permute-start.28 = (bf16[96,2048]{1,0:T(8,128)(2,1)S(1)}, bf16[96,2048]{1,0:T(8,128)(2,1)S(1)}, u32[]{:S(2)}, u32[]{:S(2)}) collective-permute-start(bf16[96,2048]{1,0:T(8,128)(2,1)S(1)} %fusion.149), channel_id=1, source_target_pairs={{0,16},{4,20},{8,24},{12,28},{16,0},{20,4},{24,8},{28,12},{1,17},{... | collective-permute-start | bytes 1179656 | tf_op jit(solution)/shard_map/ppermute | solution.py:162
  199.2 73.8 %collective-permute-start.33 = (bf16[96,2048]{1,0:T(8,128)(2,1)}, bf16[96,2048]{1,0:T(8,128)(2,1)}, u32[]{:S(2)}, u32[]{:S(2)}) collective-permute-start(bf16[96,2048]{1,0:T(8,128)(2,1)} %fusion.51), channel_id=1, source_target_pairs={{0,2},{1,3},{2,0},{3,1},{4,6},{5,7},{6,4},{7,5},{8,10},{9,11},{10,... | collective-permute-start | bytes 1179656 | tf_op jit(solution)/shard_map/ppermute | solution.py:166
  203.4 44.4 %collective-permute-start.31 = (bf16[256,2048]{1,0:T(8,128)(2,1)S(1)}, bf16[256,2048]{1,0:T(8,128)(2,1)}, u32[]{:S(2)}, u32[]{:S(2)}) collective-permute-start(bf16[256,2048]{1,0:T(8,128)(2,1)S(1)} %pad_maximum_fusion.18), channel_id=1, source_target_pairs={{0,16},{4,20},{8,24},{12,28},{16,0},{20,4},{24,8},{28,12},{1,17},{... | collective-permute-start | bytes 3145736 | tf_op jit(solution)/shard_map/ppermute | solution.py:162
  379.8 41.8 %collective-permute-start.58 = (bf16[96,2048]{1,0:T(8,128)(2,1)S(1)}, bf16[96,2048]{1,0:T(8,128)(2,1)S(1)}, u32[]{:S(2)}, u32[]{:S(2)}) collective-permute-start(bf16[96,2048]{1,0:T(8,128)(2,1)S(1)} %convolution_convert_fusion.15), channel_id=1, source_target_pairs={{0,3},{1,2},{2,1},{3,0},{4,7},{5,6},{6,5},{7,4},{8,11},{9,10},{10,... | collective-permute-start | bytes 1179656 | tf_op jit(solution)/shard_map/ppermute | solution.py:166
  390.5 31.0 %collective-permute-start.60 = (bf16[96,2048]{1,0:T(8,128)(2,1)S(1)}, bf16[96,2048]{1,0:T(8,128)(2,1)S(1)}, u32[]{:S(2)}, u32[]{:S(2)}) collective-permute-start(bf16[96,2048]{1,0:T(8,128)(2,1)S(1)} %collective-permute-done.51), channel_id=1, source_target_pairs={{0,8},{4,12},{8,0},{12,4},{16,24},{20,28},{24,16},{28,20},{1,9},{5... | collective-permute-start | bytes 1179656 | tf_op jit(solution)/shard_map/ppermute | solution.py:162
  392.0 29.6 %collective-permute-start.59 = (bf16[192,2048]{1,0:T(8,128)(2,1)S(1)}, bf16[192,2048]{1,0:T(8,128)(2,1)S(1)}, u32[]{:S(2)}, u32[]{:S(2)}) collective-permute-start(bf16[192,2048]{1,0:T(8,128)(2,1)S(1)} %pad_maximum_fusion.23), channel_id=1, source_target_pairs={{0,16},{4,20},{8,24},{12,28},{16,0},{20,4},{24,8},{28,12},{1,17},{... | collective-permute-start | bytes 2359304 | tf_op jit(solution)/shard_map/ppermute | solution.py:162
  435.3 29.2 %collective-permute-start.63 = (bf16[192,2048]{1,0:T(8,128)(2,1)S(1)}, bf16[192,2048]{1,0:T(8,128)(2,1)S(1)}, u32[]{:S(2)}, u32[]{:S(2)}) collective-permute-start(bf16[192,2048]{1,0:T(8,128)(2,1)S(1)} %pad_maximum_fusion.25), channel_id=1, source_target_pairs={{0,16},{4,20},{8,24},{12,28},{16,0},{20,4},{24,8},{28,12},{1,17},{... | collective-permute-start | bytes 2359304 | tf_op jit(solution)/shard_map/ppermute | solution.py:162
  436.6 27.8 %collective-permute-start.64 = (bf16[192,2048]{1,0:T(8,128)(2,1)S(1)}, bf16[192,2048]{1,0:T(8,128)(2,1)S(1)}, u32[]{:S(2)}, u32[]{:S(2)}) collective-permute-start(bf16[192,2048]{1,0:T(8,128)(2,1)S(1)} %bitcast.518), channel_id=1, source_target_pairs={{0,8},{4,12},{8,0},{12,4},{16,24},{20,28},{24,16},{28,20},{1,9},{5... | collective-permute-start | bytes 2359304 | tf_op jit(solution)/shard_map/ppermute | solution.py:162
  465.4 26.3 %collective-permute-start.66 = (bf16[192,2048]{1,0:T(8,128)(2,1)S(1)}, bf16[192,2048]{1,0:T(8,128)(2,1)}, u32[]{:S(2)}, u32[]{:S(2)}) collective-permute-start(bf16[192,2048]{1,0:T(8,128)(2,1)S(1)} %bitcast.519), channel_id=1, source_target_pairs={{0,8},{4,12},{8,0},{12,4},{16,24},{20,28},{24,16},{28,20},{1,9},{5... | collective-permute-start | bytes 2359304 | tf_op jit(solution)/shard_map/ppermute | solution.py:162
  579.2 42.8 %collective-permute-start.79 = (bf16[704,2048]{1,0:T(8,128)(2,1)S(1)}, bf16[704,2048]{1,0:T(8,128)(2,1)}, u32[]{:S(2)}, u32[]{:S(2)}) collective-permute-start(bf16[704,2048]{1,0:T(8,128)(2,1)S(1)} %slice.601), channel_id=1, source_target_pairs={{0,4},{4,0},{8,12},{12,8},{16,20},{20,16},{24,28},{28,24},{1,5},{5... | collective-permute-start | bytes 8650760 | tf_op jit(solution)/shard_map/ppermute | solution.py:162
  595.3 26.6 %collective-permute-start.82 = (bf16[192,2048]{1,0:T(8,128)(2,1)S(1)}, bf16[192,2048]{1,0:T(8,128)(2,1)S(1)}, u32[]{:S(2)}, u32[]{:S(2)}) collective-permute-start(bf16[192,2048]{1,0:T(8,128)(2,1)S(1)} %bitcast.520), channel_id=1, source_target_pairs={{0,8},{4,12},{8,0},{12,4},{16,24},{20,28},{24,16},{28,20},{1,9},{5... | collective-permute-start | bytes 2359304 | tf_op jit(solution)/shard_map/ppermute | solution.py:162
  627.3 33.2 %collective-permute-start.88 = (bf16[192,2048]{1,0:T(8,128)(2,1)S(1)}, bf16[192,2048]{1,0:T(8,128)(2,1)S(1)}, u32[]{:S(2)}, u32[]{:S(2)}) collective-permute-start(bf16[192,2048]{1,0:T(8,128)(2,1)S(1)} %bitcast.517), channel_id=1, source_target_pairs={{0,8},{4,12},{8,0},{12,4},{16,24},{20,28},{24,16},{28,20},{1,9},{5... | collective-permute-start | bytes 2359304 | tf_op jit(solution)/shard_map/ppermute | solution.py:162
  629.1 31.4 %collective-permute-start.86 = (bf16[96,2048]{1,0:T(8,128)(2,1)S(1)}, bf16[96,2048]{1,0:T(8,128)(2,1)S(1)}, u32[]{:S(2)}, u32[]{:S(2)}) collective-permute-start(bf16[96,2048]{1,0:T(8,128)(2,1)S(1)} %fusion.155), channel_id=1, source_target_pairs={{0,16},{4,20},{8,24},{12,28},{16,0},{20,4},{24,8},{28,12},{1,17},{... | collective-permute-start | bytes 1179656 | tf_op jit(solution)/shard_map/ppermute | solution.py:162
  630.7 29.8 %collective-permute-start.87 = (bf16[96,2048]{1,0:T(8,128)(2,1)S(1)}, bf16[96,2048]{1,0:T(8,128)(2,1)S(1)}, u32[]{:S(2)}, u32[]{:S(2)}) collective-permute-start(bf16[96,2048]{1,0:T(8,128)(2,1)S(1)} %collective-permute-done.77), channel_id=1, source_target_pairs={{0,8},{4,12},{8,0},{12,4},{16,24},{20,28},{24,16},{28,20},{1,9},{5... | collective-permute-start | bytes 1179656 | tf_op jit(solution)/shard_map/ppermute | solution.py:162
  632.4 28.1 %collective-permute-start.84 = (bf16[48,2048]{1,0:T(8,128)(2,1)S(1)}, bf16[48,2048]{1,0:T(8,128)(2,1)S(1)}, u32[]{:S(2)}, u32[]{:S(2)}) collective-permute-start(bf16[48,2048]{1,0:T(8,128)(2,1)S(1)} %slice.603), channel_id=1, source_target_pairs={{0,8},{4,12},{8,0},{12,4},{16,24},{20,28},{24,16},{28,20},{1,9},{5... | collective-permute-start | bytes 589832 | tf_op jit(solution)/shard_map/ppermute | solution.py:162
  636.5 44.0 %collective-permute-start.94 = (bf16[96,2048]{1,0:T(8,128)(2,1)S(1)}, bf16[96,2048]{1,0:T(8,128)(2,1)S(1)}, u32[]{:S(2)}, u32[]{:S(2)}) collective-permute-start(bf16[96,2048]{1,0:T(8,128)(2,1)S(1)} %fusion.53), channel_id=1, source_target_pairs={{0,8},{4,12},{8,0},{12,4},{16,24},{20,28},{24,16},{28,20},{1,9},{5... | collective-permute-start | bytes 1179656 | tf_op jit(solution)/shard_map/ppermute | solution.py:162
  664.8 27.8 %collective-permute-start.91 = (bf16[192,2048]{1,0:T(8,128)(2,1)}, bf16[192,2048]{1,0:T(8,128)(2,1)}, u32[]{:S(2)}, u32[]{:S(2)}) collective-permute-start(bf16[192,2048]{1,0:T(8,128)(2,1)} %pad_maximum_fusion.26), channel_id=1, source_target_pairs={{0,16},{4,20},{8,24},{12,28},{16,0},{20,4},{24,8},{28,12},{1,17},{... | collective-permute-start | bytes 2359304 | tf_op jit(solution)/shard_map/ppermute | solution.py:162
  665.0 27.5 %collective-permute-start.95 = (bf16[192,2048]{1,0:T(8,128)(2,1)}, bf16[192,2048]{1,0:T(8,128)(2,1)}, u32[]{:S(2)}, u32[]{:S(2)}) collective-permute-start(bf16[192,2048]{1,0:T(8,128)(2,1)} %bitcast.98), channel_id=1, source_target_pairs={{0,8},{4,12},{8,0},{12,4},{16,24},{20,28},{24,16},{28,20},{1,9},{5... | collective-permute-start | bytes 2359304 | tf_op jit(solution)/shard_map/ppermute | solution.py:162
  704.9 43.6 %collective-permute-start.97 = (bf16[192,2048]{1,0:T(8,128)(2,1)}, bf16[192,2048]{1,0:T(8,128)(2,1)}, u32[]{:S(2)}, u32[]{:S(2)}) collective-permute-start(bf16[192,2048]{1,0:T(8,128)(2,1)} %pad_maximum_fusion.27), channel_id=1, source_target_pairs={{0,16},{4,20},{8,24},{12,28},{16,0},{20,4},{24,8},{28,12},{1,17},{... | collective-permute-start | bytes 2359304 | tf_op jit(solution)/shard_map/ppermute | solution.py:162
  705.7 42.8 %collective-permute-start.98 = (bf16[192,2048]{1,0:T(8,128)(2,1)}, bf16[192,2048]{1,0:T(8,128)(2,1)}, u32[]{:S(2)}, u32[]{:S(2)}) collective-permute-start(bf16[192,2048]{1,0:T(8,128)(2,1)} %pad_maximum_fusion.28), channel_id=1, source_target_pairs={{0,16},{4,20},{8,24},{12,28},{16,0},{20,4},{24,8},{28,12},{1,17},{... | collective-permute-start | bytes 2359304 | tf_op jit(solution)/shard_map/ppermute | solution.py:162
  706.9 41.6 %collective-permute-start.100 = (bf16[192,2048]{1,0:T(8,128)(2,1)}, bf16[192,2048]{1,0:T(8,128)(2,1)}, u32[]{:S(2)}, u32[]{:S(2)}) collective-permute-start(bf16[192,2048]{1,0:T(8,128)(2,1)} %bitcast.104), channel_id=1, source_target_pairs={{0,8},{4,12},{8,0},{12,4},{16,24},{20,28},{24,16},{28,20},{1,9},{5... | collective-permute-start | bytes 2359304 | tf_op jit(solution)/shard_map/ppermute | solution.py:162
  716.8 31.7 %collective-permute-start.99 = (bf16[96,2048]{1,0:T(8,128)(2,1)S(1)}, bf16[96,2048]{1,0:T(8,128)(2,1)S(1)}, u32[]{:S(2)}, u32[]{:S(2)}) collective-permute-start(bf16[96,2048]{1,0:T(8,128)(2,1)S(1)} %fusion.157), channel_id=1, source_target_pairs={{0,16},{4,20},{8,24},{12,28},{16,0},{20,4},{24,8},{28,12},{1,17},{... | collective-permute-start | bytes 1179656 | tf_op jit(solution)/shard_map/ppermute | solution.py:162
  751.9 27.4 %collective-permute-start.104 = (bf16[256,2048]{1,0:T(8,128)(2,1)}, bf16[256,2048]{1,0:T(8,128)(2,1)}, u32[]{:S(2)}, u32[]{:S(2)}) collective-permute-start(bf16[256,2048]{1,0:T(8,128)(2,1)} %bitcast.110), channel_id=1, source_target_pairs={{0,8},{4,12},{8,0},{12,4},{16,24},{20,28},{24,16},{28,20},{1,9},{5... | collective-permute-start | bytes 3145736 | tf_op jit(solution)/shard_map/ppermute | solution.py:162
  814.0 46.6 %collective-permute-start.107 = (bf16[128,2048]{1,0:T(8,128)(2,1)}, bf16[128,2048]{1,0:T(8,128)(2,1)}, u32[]{:S(2)}, u32[]{:S(2)}) collective-permute-start(bf16[128,2048]{1,0:T(8,128)(2,1)} %add_convert_fusion.7), channel_id=1, source_target_pairs={{0,1},{1,0},{2,3},{3,2},{4,5},{5,4},{6,7},{7,6},{8,9},{9,8},{10,11... | collective-permute-start | bytes 1572872 | tf_op jit(solution)/shard_map/ppermute | solution.py:166
  815.7 45.0 %collective-permute-start.109 = (bf16[256,2048]{1,0:T(8,128)(2,1)}, bf16[256,2048]{1,0:T(8,128)(2,1)}, u32[]{:S(2)}, u32[]{:S(2)}) collective-permute-start(bf16[256,2048]{1,0:T(8,128)(2,1)} %bitcast.122), channel_id=1, source_target_pairs={{0,8},{4,12},{8,0},{12,4},{16,24},{20,28},{24,16},{28,20},{1,9},{5... | collective-permute-start | bytes 3145736 | tf_op jit(solution)/shard_map/ppermute | solution.py:162
  819.4 41.3 %collective-permute-start.108 = (bf16[128,2048]{1,0:T(8,128)(2,1)}, bf16[128,2048]{1,0:T(8,128)(2,1)}, u32[]{:S(2)}, u32[]{:S(2)}) collective-permute-start(bf16[128,2048]{1,0:T(8,128)(2,1)} %fusion.146), channel_id=1, source_target_pairs={{0,16},{4,20},{8,24},{12,28},{16,0},{20,4},{24,8},{28,12},{1,17},{... | collective-permute-start | bytes 1572872 | tf_op jit(solution)/shard_map/ppermute | solution.py:162
  926.4 45.2 %collective-permute-start.118 = (bf16[256,2048]{1,0:T(8,128)(2,1)S(1)}, bf16[256,2048]{1,0:T(8,128)(2,1)S(1)}, u32[]{:S(2)}, u32[]{:S(2)}) collective-permute-start(bf16[256,2048]{1,0:T(8,128)(2,1)S(1)} %slice.909), channel_id=1, source_target_pairs={{0,4},{4,0},{8,12},{12,8},{16,20},{20,16},{24,28},{28,24},{1,5},{5... | collective-permute-start | bytes 3145736 | tf_op jit(solution)/shard_map/ppermute | solution.py:162
  932.9 38.7 %collective-permute-start.120 = (bf16[128,2048]{1,0:T(8,128)(2,1)S(1)}, bf16[128,2048]{1,0:T(8,128)(2,1)S(1)}, u32[]{:S(2)}, u32[]{:S(2)}) collective-permute-start(bf16[128,2048]{1,0:T(8,128)(2,1)S(1)} %bitcast.532), channel_id=1, source_target_pairs={{0,2},{1,3},{2,0},{3,1},{4,6},{5,7},{6,4},{7,5},{8,10},{9,11},{10,... | collective-permute-start | bytes 1572872 | tf_op jit(solution)/shard_map/ppermute | solution.py:166
  933.0 38.7 %collective-permute-start.121 = (bf16[128,2048]{1,0:T(8,128)(2,1)S(1)}, bf16[128,2048]{1,0:T(8,128)(2,1)S(1)}, u32[]{:S(2)}, u32[]{:S(2)}) collective-permute-start(bf16[128,2048]{1,0:T(8,128)(2,1)S(1)} %bitcast.531), channel_id=1, source_target_pairs={{0,3},{1,2},{2,1},{3,0},{4,7},{5,6},{6,5},{7,4},{8,11},{9,10},{10,... | collective-permute-start | bytes 1572872 | tf_op jit(solution)/shard_map/ppermute | solution.py:166
  934.3 37.3 %collective-permute-start.119 = (bf16[128,2048]{1,0:T(8,128)(2,1)S(1)}, bf16[128,2048]{1,0:T(8,128)(2,1)S(1)}, u32[]{:S(2)}, u32[]{:S(2)}) collective-permute-start(bf16[128,2048]{1,0:T(8,128)(2,1)S(1)} %bitcast.530), channel_id=1, source_target_pairs={{0,1},{1,0},{2,3},{3,2},{4,5},{5,4},{6,7},{7,6},{8,9},{9,8},{10,11... | collective-permute-start | bytes 1572872 | tf_op jit(solution)/shard_map/ppermute | solution.py:166
  939.0 32.6 %collective-permute-start.122 = (f32[3,2048]{1,0:T(4,128)S(1)}, f32[3,2048]{1,0:T(4,128)S(1)}, u32[]{:S(2)}, u32[]{:S(2)}) collective-permute-start(f32[3,2048]{1,0:T(4,128)S(1)} %select_maximum_fusion), channel_id=1, source_target_pairs={{0,1},{1,0},{2,3},{3,2},{4,5},{5,4},{6,7},{7,6},{8,9},{9,8},{10,11... | collective-permute-start | bytes 73736 | tf_op jit(solution)/shard_map/ppermute | solution.py:166
  (283 other events, 3778.6 us)

commit v4 on v2

--- a/solution.py
+++ b/solution.py
@@ -142,6 +142,10 @@
         (part,) = yield (part,)
         return part.astype(f32)
 
+    def pair_send(self, part):
+        (part,) = yield (part,)
+        return (part,)
+
     def column_gather(self, block):
         (rows,) = yield (lax.all_gather(block, "expert", axis=0, tiled=False),)
         return (rows,)
@@ -293,6 +297,10 @@
     def pair_gather(self, block):
         block, other = yield (block, swap(block, CORE))
         return (block, other)
+
+    def pair_send(self, part):
+        part, other = yield (part, swap(part[part.shape[0] // 2 :], CORE))
+        return (part, other)
 
     def pair_scatter(self, part):
         size = part.shape[0] // 2
@@ -397,6 +405,33 @@
         compiler_params=pltpu.CompilerParams(vmem_limit_bytes=32 << 20),
         name="assemble",
     )(*queries, *blocks)
+
+
+def pair_totals_kernel(pair, *refs):
+    out = refs[-1]
+    for i in range(out.shape[0]):
+        total = refs[i * pair][...].astype(f32)
+        for other in refs[i * pair + 1 : (i + 1) * pair]:
+            total = total + other[...].astype(f32)
+        out[i] = total
+
+
+def pair_totals(pieces, pair):
+    count, width = pieces[0].shape[0] // pair, pieces[0].shape[1]
+    step = max(i for i in range(16, 177, 16) if count % i == 0)
+    kinds = len(pieces) // pair
+    return pl.pallas_call(
+        functools.partial(pair_totals_kernel, pair),
+        grid=(count // step,),
+        in_specs=[pl.BlockSpec((step, width), lambda i: (i, 0))] * len(pieces),
+        out_specs=pl.BlockSpec((kinds, step, width), lambda i: (0, i, 0)),
+        out_shape=jax.ShapeDtypeStruct((kinds, count, width), f32),
+        cost_estimate=pl.CostEstimate(
+            flops=kinds * count * width, bytes_accessed=8 * kinds * count * width, transcendentals=0
+        ),
+        compiler_params=pltpu.CompilerParams(vmem_limit_bytes=40 << 20),
+        name="pair_totals",
+    )(*pieces)
 
 
 def weave_kernel(first_ref, second_ref, out_ref):
@@ -804,9 +839,9 @@
         pieces = []
         for name, other in (("grad_gate", rows), ("grad_up", rows), ("units", grads)):
             (whole,) = yield (dot_tn(joined(name), other).astype(bf16),)
-            piece = yield from links.pair_scatter(whole)
-            pieces.append(piece)
-        box["mlp_grad"] = jnp.stack(pieces).transpose(1, 0, 2)[None]
+            piece = yield from links.pair_send(whole)
+            pieces.extend(piece)
+        box["mlp_grad"] = pair_totals(pieces, links.pair).transpose(1, 0, 2)[None]
 
     def attention_back():
         parts = {}

time: 1000 us -> 1030 us (1.030); the launches traced: 994 us -> 1010 us
  starting transfers between devices: 150 us -> 204 us
  other arithmetic: 133 us -> 103 us
  Pallas kernels: 33.3 us -> 53.6 us
  waiting for transfers between devices: 342 us -> 329 us
    ppermute x36, starting transfers between devices: 63.6 us -> 103 us  [flip(): return lax.ppermute(block, 'expert', [(i, i ^ mask) for i in range(4)])]
    ppermute x94, starting transfers between devices: 86.7 us -> 101 us  [swap(): return lax.ppermute(block, 'dp', [(i, i ^ mask) for i in range(8)])]
    another operation x3 -> x0, other arithmetic: 13.3 us -> none  [expert_grads(): box['mlp_grad'] = jnp.stack(pieces).transpose(1, 0, 2)[None]]
    pallas_call x4, Pallas kernels: 12.5 us -> 24.1 us  [attend(): pl.pallas_call(functools.partial(attend_kernel, heads, HD ** (-0.5)), gri...]
    unnamed x434 -> x464, local copies, waits for them, and re-layouts: 58.8 us -> 52.4 us
  transfers between devices with their start and end apart: 130 -> 130, of which waited for: 47 -> 43; matrix products, arithmetic and copies ran while one was open for 39% -> 31% of each run, Pallas kernels for 3% -> 4%
where the time goes in v4:
time: 1030 us; the launch traced here: 1010 us
  waiting for transfers between devices  329 us (32%)
  matrix products  230 us (22%)
  starting transfers between devices  204 us (20%)
  other arithmetic  103 us (10%)
  local copies, waits for them, and re-layouts  86.2 us (8%)
  Pallas kernels  53.6 us (5%)
    ppermute x94, waiting for transfers between devices, swap(): return lax.ppermute(block, 'dp', [(i, i ^ mask) for i in range(8)])  204 us
    ppermute x36, waiting for transfers between devices, flip(): return lax.ppermute(block, 'expert', [(i, i ^ mask) for i in range(4)])  125 us
    ppermute x36, starting transfers between devices, flip(): return lax.ppermute(block, 'expert', [(i, i ^ mask) for i in range(4)])  103 us
    ppermute x94, starting transfers between devices, swap(): return lax.ppermute(block, 'dp', [(i, i ^ mask) for i in range(8)])  101 us
    dot_general x20, matrix products, dot_nt(): lax.dot_general(left, right, (((1,), (1,)), ((), ())), preferred_element_...  83.8 us
    dot_general x13, matrix products, dot_tn(): lax.dot_general(left, right, (((0,), (0,)), ((), ())), preferred_element_...  80.1 us
    dot_general x38, matrix products, dot_nn(): lax.dot_general(left, right, (((1,), (0,)), ((), ())), preferred_element_...  66.4 us
    unnamed x464, local copies, waits for them, and re-layouts  52.4 us
  transfers between devices with their start and end apart: 130, of which 43 were waited for; matrix products, arithmetic and copies ran while one was open for 31% of the time, Pallas kernels for 4%

profile of v4, /device:TPU:0, one launch (start us, length us, event | category | flops | bytes accessed | tf_op | source)
XLA Modules:
  0.0 1011.5 jit_solution(294703589055736788)
XLA Ops:
  9.3 6.1 slice_bitcast_fusion
  54.5 13.7 %collective-permute-done.11 = bf16[128,2048]{1,0:T(8,128)(2,1)S(1)} collective-permute-done((bf16[128,2048]{1,0:T(8,128)(2,1)S(1)}, bf16[128,2048]{1,0:T(8,128)(2,1)S(1)}, u32[]{:S(2)}, u32[]{:S(2)}) %collective-permute-start.11) | collective-permute-done | bytes 524320 | tf_op jit(solution)/shard_map/ppermute | solution.py:171
  69.7 12.4 %collective-permute-done.12 = bf16[128,2048]{1,0:T(8,128)(2,1)S(1)} collective-permute-done((bf16[128,2048]{1,0:T(8,128)(2,1)S(1)}, bf16[128,2048]{1,0:T(8,128)(2,1)S(1)}, u32[]{:S(2)}, u32[]{:S(2)}) %collective-permute-start.12) | collective-permute-done | bytes 524320 | tf_op jit(solution)/shard_map/ppermute | solution.py:171
  88.1 21.5 %collective-permute-start.10 = (bf16[128,2048]{1,0:T(8,128)(2,1)}, bf16[128,2048]{1,0:T(8,128)(2,1)}, u32[]{:S(2)}, u32[]{:S(2)}) collective-permute-start(bf16[128,2048]{1,0:T(8,128)(2,1)} %param.14), channel_id=1, source_target_pairs={{0,2},{1,3},{2,0},{3,1},{4,6},{5,7},{6,4},{7,5},{8,10},{9,11},{10,... | collective-permute-start | bytes 1572872 | tf_op jit(solution)/shard_map/ppermute | solution.py:171
  115.8 15.4 %collective-permute-done.20 = bf16[128,2048]{1,0:T(8,128)(2,1)S(1)} collective-permute-done((bf16[128,2048]{1,0:T(8,128)(2,1)}, bf16[128,2048]{1,0:T(8,128)(2,1)S(1)}, u32[]{:S(2)}, u32[]{:S(2)}) %collective-permute-start.20) | collective-permute-done | bytes 524320 | tf_op jit(solution)/shard_map/ppermute | solution.py:171
  160.3 18.6 %collective-permute-done.25 = bf16[128,2048]{1,0:T(8,128)(2,1)S(1)} collective-permute-done((bf16[128,2048]{1,0:T(8,128)(2,1)}, bf16[128,2048]{1,0:T(8,128)(2,1)S(1)}, u32[]{:S(2)}, u32[]{:S(2)}) %collective-permute-start.25) | collective-permute-done | bytes 524320 | tf_op jit(solution)/shard_map/ppermute | solution.py:167
  186.9 23.1 %collective-permute-done.28 = bf16[96,2048]{1,0:T(8,128)(2,1)S(1)} collective-permute-done((bf16[96,2048]{1,0:T(8,128)(2,1)S(1)}, bf16[96,2048]{1,0:T(8,128)(2,1)S(1)}, u32[]{:S(2)}, u32[]{:S(2)}) %collective-permute-start.28) | collective-permute-done | bytes 393248 | tf_op jit(solution)/shard_map/ppermute | solution.py:167
  230.4 6.1 pad_maximum_fusion.1
  236.6 6.1 pad_maximum_fusion.2
  242.7 6.2 pad_maximum_fusion.3
  253.9 15.1 %attend.7 = (bf16[512,1536]{1,0:T(8,128)(2,1)S(1)}, bf16[384,512]{1,0:T(8,128)(2,1)S(1)}, f32[4,4,128]{2,1,0:T(4,128)S(1)}) custom-call(f32[512,1536]{1,0:T(8,128)S(1)} %fusion.233.raw_ref, f32[128,128]{1,0:T(8,128)S(1)} %get-tuple-element.700.cos_ref, f32[128,128]{1,0:T(8,128)S(1)} %get-tuple-element.701.sin_ref, s32[4,1,128]{2,1,0:T(1,128)S(1)} %get-tuple-element.648.idx_ref), custom_call_target="tpu_custom_call" | custom-call | flops 201326592 | bytes 5242880 | tf_op jit(solution)/shard_map/attend/pallas_call | solution.py:505
  285.1 7.0 fusion.66
  300.2 7.3 collective-permute-done.36
  322.9 6.4 collective-permute-done.42
  337.9 6.8 collective-permute-done.43
  348.3 7.1 collective-permute-start.47
  361.5 6.8 fusion.74
  439.0 5.8 collective-permute-done.60
  460.0 6.8 multiply_convert_fusion.6
  491.2 6.9 multiply_convert_fusion.3
  510.0 5.9 collective-permute-done.65
  515.9 7.5 multiply_convert_fusion
  535.4 6.3 collective-permute-done.67
  555.9 6.7 collective-permute-start.73
  566.8 5.9 collective-permute-done.73
  576.8 5.7 collective-permute-done.76
  591.2 11.5 %convolution_convert_fusion.2.refs_0_ = bf16[1408,2048]{1,0:T(8,128)(2,1)S(1)} fusion(bf16[1536,2048]{1,0:T(8,128)(2,1)} %get-tuple-element.620, bf16[384,1408]{1,0:T(8,128)(2,1)S(1)} %copy-done.185, bf16[384,1408]{1,0:T(8,128)(2,1)S(1)} %copy-done.183, bf16[384,1408]{1,0:T(8,128)(2,1)S(1)} %copy-done.181, bf16[384,1408]{1,0:T(8,128)(2,1)S(1)} %copy-done.179), kind=kOutput, calls=%fused_computation.5 | convolution fusion | flops 8878555136 | bytes 16384000 | tf_op jit(solution)/shard_map/dot_general | solution.py:40
  605.2 12.4 %convolution_convert_fusion.1.refs_2_ = bf16[1408,2048]{1,0:T(8,128)(2,1)S(1)} fusion(bf16[1536,2048]{1,0:T(8,128)(2,1)} %get-tuple-element.620, bf16[384,1408]{1,0:T(8,128)(2,1)} %copy-done.177, bf16[384,1408]{1,0:T(8,128)(2,1)} %copy-done.176, bf16[384,1408]{1,0:T(8,128)(2,1)} %copy-done.175, bf16[384,1408]{1,0:T(8,128)(2,1)S(1)} %copy-done.174), kind=kOutput, calls=%fused_computation.4 | convolution fusion | flops 8878555136 | bytes 16384000 | tf_op jit(solution)/shard_map/dot_general | solution.py:40
  622.3 14.4 %convolution_convert_fusion.refs_4_ = bf16[1408,2048]{1,0:T(8,128)(2,1)} fusion(bf16[1536,2048]{1,0:T(8,128)(2,1)} %get-tuple-element.608, bf16[384,1408]{1,0:T(8,128)(2,1)} %get-tuple-element.570, bf16[384,1408]{1,0:T(8,128)(2,1)} %get-tuple-element.573, bf16[384,1408]{1,0:T(8,128)(2,1)} %copy-done.187, bf16[384,1408]{1,0:T(8,128)(2,1)} %get-tuple-element.579), kind=kOutput, calls=%fused_computation.3 | convolution fusion | flops 8878555136 | bytes 16384000 | tf_op jit(solution)/shard_map/dot_general | solution.py:40
  640.1 6.5 collective-permute-done.82
  654.4 19.0 %collective-permute-done.84 = bf16[48,2048]{1,0:T(8,128)(2,1)S(1)} collective-permute-done((bf16[48,2048]{1,0:T(8,128)(2,1)S(1)}, bf16[48,2048]{1,0:T(8,128)(2,1)S(1)}, u32[]{:S(2)}, u32[]{:S(2)}) %collective-permute-start.84) | collective-permute-done | bytes 196640 | tf_op jit(solution)/shard_map/ppermute | solution.py:167
  674.7 7.2 collective-permute-done.87
  696.9 15.0 %collective-permute-done.92 = bf16[96,2048]{1,0:T(8,128)(2,1)S(1)} collective-permute-done((bf16[96,2048]{1,0:T(8,128)(2,1)S(1)}, bf16[96,2048]{1,0:T(8,128)(2,1)S(1)}, u32[]{:S(2)}, u32[]{:S(2)}) %collective-permute-start.92) | collective-permute-done | bytes 393248 | tf_op jit(solution)/shard_map/ppermute | solution.py:167
  730.3 12.9 %collective-permute-done.96 = bf16[96,2048]{1,0:T(8,128)(2,1)S(1)} collective-permute-done((bf16[96,2048]{1,0:T(8,128)(2,1)S(1)}, bf16[96,2048]{1,0:T(8,128)(2,1)S(1)}, u32[]{:S(2)}, u32[]{:S(2)}) %collective-permute-start.96) | collective-permute-done | bytes 393248 | tf_op jit(solution)/shard_map/ppermute | solution.py:171
  743.2 26.4 %collective-permute-done.99 = bf16[96,2048]{1,0:T(8,128)(2,1)S(1)} collective-permute-done((bf16[96,2048]{1,0:T(8,128)(2,1)S(1)}, bf16[96,2048]{1,0:T(8,128)(2,1)S(1)}, u32[]{:S(2)}, u32[]{:S(2)}) %collective-permute-start.99) | collective-permute-done | bytes 393248 | tf_op jit(solution)/shard_map/ppermute | solution.py:167
  783.9 8.6 collective-permute-done.103
  808.1 8.7 pair_totals.1
  818.2 6.5 collective-permute-done.106
  848.2 10.5 %fusion.37 = f32[1024,2048]{1,0:T(8,128)} fusion(bf16[512,1024]{1,0:T(8,128)(2,1)S(1)} %slice-done.10, bf16[512,1024]{1,0:T(8,128)(2,1)S(1)} %slice-done.6, bf16[512,1024]{1,0:T(8,128)(2,1)S(1)} %slice-done.8, bf16[512,2048]{1,0:T(8,128)(2,1)} %copy-done.79, bf16[512,2048]{1,0:T(8,128)(2,1)S(1)} %copy-done.72, bf16[512,2048]{1,0:T(8,128)(2,1)S(1)} %copy-done.74), kind=kOutput, calls=%fused_computation.57 | convolution fusion | flops 6470762496 | bytes 17825792 | tf_op jit(solution)/shard_map/dot_general | solution.py:40
  858.7 7.3 fusion.43
  875.6 7.8 fusion.123
  883.5 9.8 collective-permute-done.110
  903.7 7.7 multiply_reduce_fusion
  928.1 8.6 collective-permute-start.122
  945.2 5.7 collective-permute-start.119
  955.8 18.2 %collective-permute-done.119 = bf16[128,2048]{1,0:T(8,128)(2,1)S(1)} collective-permute-done((bf16[128,2048]{1,0:T(8,128)(2,1)S(1)}, bf16[128,2048]{1,0:T(8,128)(2,1)S(1)}, u32[]{:S(2)}, u32[]{:S(2)}) %collective-permute-start.119) | collective-permute-done | bytes 524320 | tf_op jit(solution)/shard_map/ppermute | solution.py:171
  974.0 15.1 %collective-permute-done.120 = bf16[128,2048]{1,0:T(8,128)(2,1)S(1)} collective-permute-done((bf16[128,2048]{1,0:T(8,128)(2,1)S(1)}, bf16[128,2048]{1,0:T(8,128)(2,1)S(1)}, u32[]{:S(2)}, u32[]{:S(2)}) %collective-permute-start.120) | collective-permute-done | bytes 524320 | tf_op jit(solution)/shard_map/ppermute | solution.py:171
  1004.6 6.7 weave.1
  (999 shorter events, 516.5 us)
Async XLA Ops:
  15.5 30.6 %collective-permute-start.5 = (bf16[704,2048]{1,0:T(8,128)(2,1)}, bf16[704,2048]{1,0:T(8,128)(2,1)}, u32[]{:S(2)}, u32[]{:S(2)}) collective-permute-start(bf16[704,2048]{1,0:T(8,128)(2,1)} %get-tuple-element.321), channel_id=1, source_target_pairs={{0,4},{4,0},{8,12},{12,8},{16,20},{20,16},{24,28},{28,24},{1,5},{5... | collective-permute-start | bytes 8650760 | tf_op jit(solution)/shard_map/ppermute | solution.py:167
  15.5 32.8 %collective-permute-start.6 = (bf16[704,2048]{1,0:T(8,128)(2,1)}, bf16[704,2048]{1,0:T(8,128)(2,1)}, u32[]{:S(2)}, u32[]{:S(2)}) collective-permute-start(bf16[704,2048]{1,0:T(8,128)(2,1)} %get-tuple-element.323), channel_id=1, source_target_pairs={{0,4},{4,0},{8,12},{12,8},{16,20},{20,16},{24,28},{28,24},{1,5},{5... | collective-permute-start | bytes 8650760 | tf_op jit(solution)/shard_map/ppermute | solution.py:167
  16.0 32.3 %collective-permute-start.7 = (bf16[704,2048]{1,0:T(8,128)(2,1)}, bf16[704,2048]{1,0:T(8,128)(2,1)}, u32[]{:S(2)}, u32[]{:S(2)}) collective-permute-start(bf16[704,2048]{1,0:T(8,128)(2,1)} %get-tuple-element.325), channel_id=1, source_target_pairs={{0,4},{4,0},{8,12},{12,8},{16,20},{20,16},{24,28},{28,24},{1,5},{5... | collective-permute-start | bytes 8650760 | tf_op jit(solution)/shard_map/ppermute | solution.py:167
  43.9 24.3 %collective-permute-start.11 = (bf16[128,2048]{1,0:T(8,128)(2,1)S(1)}, bf16[128,2048]{1,0:T(8,128)(2,1)S(1)}, u32[]{:S(2)}, u32[]{:S(2)}) collective-permute-start(bf16[128,2048]{1,0:T(8,128)(2,1)S(1)} %constant_dynamic-update-slice_fusion), channel_id=1, source_target_pairs={{0,1},{1,0},{2,3},{3,2},{4,5},{5,4},{6,7},{7,6},{8,9},{9,8},{10,11... | collective-permute-start | bytes 1572872 | tf_op jit(solution)/shard_map/ppermute | solution.py:171
  43.9 38.2 %collective-permute-start.12 = (bf16[128,2048]{1,0:T(8,128)(2,1)S(1)}, bf16[128,2048]{1,0:T(8,128)(2,1)S(1)}, u32[]{:S(2)}, u32[]{:S(2)}) collective-permute-start(bf16[128,2048]{1,0:T(8,128)(2,1)S(1)} %constant_dynamic-update-slice_fusion), channel_id=1, source_target_pairs={{0,2},{1,3},{2,0},{3,1},{4,6},{5,7},{6,4},{7,5},{8,10},{9,11},{10,... | collective-permute-start | bytes 1572872 | tf_op jit(solution)/shard_map/ppermute | solution.py:171
  46.1 37.6 %collective-permute-start.13 = (bf16[128,2048]{1,0:T(8,128)(2,1)S(1)}, bf16[128,2048]{1,0:T(8,128)(2,1)S(1)}, u32[]{:S(2)}, u32[]{:S(2)}) collective-permute-start(bf16[128,2048]{1,0:T(8,128)(2,1)S(1)} %constant_dynamic-update-slice_fusion), channel_id=1, source_target_pairs={{0,3},{1,2},{2,1},{3,0},{4,7},{5,6},{6,5},{7,4},{8,11},{9,10},{10,... | collective-permute-start | bytes 1572872 | tf_op jit(solution)/shard_map/ppermute | solution.py:171
  49.6 60.0 %collective-permute-start.17 = (bf16[256,2048]{1,0:T(8,128)(2,1)S(1)}, bf16[256,2048]{1,0:T(8,128)(2,1)S(1)}, u32[]{:S(2)}, u32[]{:S(2)}) collective-permute-start(bf16[256,2048]{1,0:T(8,128)(2,1)S(1)} %pad_maximum_fusion.16), channel_id=1, source_target_pairs={{0,16},{4,20},{8,24},{12,28},{16,0},{20,4},{24,8},{28,12},{1,17},{... | collective-permute-start | bytes 3145736 | tf_op jit(solution)/shard_map/ppermute | solution.py:167
  52.4 57.3 %collective-permute-start.18 = (bf16[192,2048]{1,0:T(8,128)(2,1)S(1)}, bf16[192,2048]{1,0:T(8,128)(2,1)S(1)}, u32[]{:S(2)}, u32[]{:S(2)}) collective-permute-start(bf16[192,2048]{1,0:T(8,128)(2,1)S(1)} %pad_maximum_fusion.20), channel_id=1, source_target_pairs={{0,8},{4,12},{8,0},{12,4},{16,24},{20,28},{24,16},{28,20},{1,9},{5... | collective-permute-start | bytes 2359304 | tf_op jit(solution)/shard_map/ppermute | solution.py:167
  83.6 26.0 %collective-permute-start.16 = (f32[4,8,128]{2,1,0:T(8,128)S(1)}, f32[4,8,128]{2,1,0:T(8,128)S(1)}, u32[]{:S(2)}, u32[]{:S(2)}) collective-permute-start(f32[4,8,128]{2,1,0:T(8,128)S(1)} %constant_dynamic-update-slice_fusion.2), channel_id=1, source_target_pairs={{0,24},{4,28},{8,16},{12,20},{16,8},{20,12},{24,0},{28,4},{1,25},{... | collective-permute-start | bytes 49160 | tf_op jit(solution)/shard_map/ppermute | solution.py:167
  86.6 71.1 %collective-permute-start.23 = (bf16[128,2048]{1,0:T(8,128)(2,1)}, bf16[128,2048]{1,0:T(8,128)(2,1)}, u32[]{:S(2)}, u32[]{:S(2)}) collective-permute-start(bf16[128,2048]{1,0:T(8,128)(2,1)} %param.14), channel_id=1, source_target_pairs={{0,3},{1,2},{2,1},{3,0},{4,7},{5,6},{6,5},{7,4},{8,11},{9,10},{10,... | collective-permute-start | bytes 1572872 | tf_op jit(solution)/shard_map/ppermute | solution.py:171
  88.1 60.4 %collective-permute-start.10 = (bf16[128,2048]{1,0:T(8,128)(2,1)}, bf16[128,2048]{1,0:T(8,128)(2,1)}, u32[]{:S(2)}, u32[]{:S(2)}) collective-permute-start(bf16[128,2048]{1,0:T(8,128)(2,1)} %param.14), channel_id=1, source_target_pairs={{0,2},{1,3},{2,0},{3,1},{4,6},{5,7},{6,4},{7,5},{8,10},{9,11},{10,... | collective-permute-start | bytes 1572872 | tf_op jit(solution)/shard_map/ppermute | solution.py:171
  131.3 139.8 %collective-permute-start.30 = (bf16[96,2048]{1,0:T(8,128)(2,1)}, bf16[96,2048]{1,0:T(8,128)(2,1)}, u32[]{:S(2)}, u32[]{:S(2)}) collective-permute-start(bf16[96,2048]{1,0:T(8,128)(2,1)} %fusion.53), channel_id=1, source_target_pairs={{0,1},{1,0},{2,3},{3,2},{4,5},{5,4},{6,7},{7,6},{8,9},{9,8},{10,11... | collective-permute-start | bytes 1179656 | tf_op jit(solution)/shard_map/ppermute | solution.py:171
  149.7 29.3 %collective-permute-start.24 = (bf16[256,2048]{1,0:T(8,128)(2,1)}, bf16[256,2048]{1,0:T(8,128)(2,1)S(1)}, u32[]{:S(2)}, u32[]{:S(2)}) collective-permute-start(bf16[256,2048]{1,0:T(8,128)(2,1)} %pad_maximum_fusion.17), channel_id=1, source_target_pairs={{0,16},{4,20},{8,24},{12,28},{16,0},{20,4},{24,8},{28,12},{1,17},{... | collective-permute-start | bytes 3145736 | tf_op jit(solution)/shard_map/ppermute | solution.py:167
  151.2 27.8 %collective-permute-start.26 = (bf16[192,2048]{1,0:T(8,128)(2,1)}, bf16[192,2048]{1,0:T(8,128)(2,1)}, u32[]{:S(2)}, u32[]{:S(2)}) collective-permute-start(bf16[192,2048]{1,0:T(8,128)(2,1)} %bitcast.33), channel_id=1, source_target_pairs={{0,8},{4,12},{8,0},{12,4},{16,24},{20,28},{24,16},{28,20},{1,9},{5... | collective-permute-start | bytes 2359304 | tf_op jit(solution)/shard_map/ppermute | solution.py:167
  153.1 25.8 %collective-permute-start.25 = (bf16[128,2048]{1,0:T(8,128)(2,1)}, bf16[128,2048]{1,0:T(8,128)(2,1)S(1)}, u32[]{:S(2)}, u32[]{:S(2)}) collective-permute-start(bf16[128,2048]{1,0:T(8,128)(2,1)} %collective-permute-done.10), channel_id=1, source_target_pairs={{0,8},{4,12},{8,0},{12,4},{16,24},{20,28},{24,16},{28,20},{1,9},{5... | collective-permute-start | bytes 1572872 | tf_op jit(solution)/shard_map/ppermute | solution.py:167
  157.7 175.7 %collective-permute-start.32 = (bf16[96,2048]{1,0:T(8,128)(2,1)}, bf16[96,2048]{1,0:T(8,128)(2,1)}, u32[]{:S(2)}, u32[]{:S(2)}) collective-permute-start(bf16[96,2048]{1,0:T(8,128)(2,1)} %fusion.55), channel_id=1, source_target_pairs={{0,3},{1,2},{2,1},{3,0},{4,7},{5,6},{6,5},{7,4},{8,11},{9,10},{10,... | collective-permute-start | bytes 1179656 | tf_op jit(solution)/shard_map/ppermute | solution.py:171
  180.5 33.0 %collective-permute-start.27 = (bf16[256,2048]{1,0:T(8,128)(2,1)S(1)}, bf16[256,2048]{1,0:T(8,128)(2,1)S(1)}, u32[]{:S(2)}, u32[]{:S(2)}) collective-permute-start(bf16[256,2048]{1,0:T(8,128)(2,1)S(1)} %pad_maximum_fusion.18), channel_id=1, source_target_pairs={{0,16},{4,20},{8,24},{12,28},{16,0},{20,4},{24,8},{28,12},{1,17},{... | collective-permute-start | bytes 3145736 | tf_op jit(solution)/shard_map/ppermute | solution.py:167
  183.6 26.5 %collective-permute-start.28 = (bf16[96,2048]{1,0:T(8,128)(2,1)S(1)}, bf16[96,2048]{1,0:T(8,128)(2,1)S(1)}, u32[]{:S(2)}, u32[]{:S(2)}) collective-permute-start(bf16[96,2048]{1,0:T(8,128)(2,1)S(1)} %fusion.158), channel_id=1, source_target_pairs={{0,16},{4,20},{8,24},{12,28},{16,0},{20,4},{24,8},{28,12},{1,17},{... | collective-permute-start | bytes 1179656 | tf_op jit(solution)/shard_map/ppermute | solution.py:167
  184.1 29.3 %collective-permute-start.29 = (bf16[128,2048]{1,0:T(8,128)(2,1)}, bf16[128,2048]{1,0:T(8,128)(2,1)S(1)}, u32[]{:S(2)}, u32[]{:S(2)}) collective-permute-start(bf16[128,2048]{1,0:T(8,128)(2,1)} %collective-permute-done.23), channel_id=1, source_target_pairs={{0,8},{4,12},{8,0},{12,4},{16,24},{20,28},{24,16},{28,20},{1,9},{5... | collective-permute-start | bytes 1572872 | tf_op jit(solution)/shard_map/ppermute | solution.py:167
  210.0 90.1 %collective-permute-start.33 = (bf16[96,2048]{1,0:T(8,128)(2,1)}, bf16[96,2048]{1,0:T(8,128)(2,1)}, u32[]{:S(2)}, u32[]{:S(2)}) collective-permute-start(bf16[96,2048]{1,0:T(8,128)(2,1)} %fusion.54), channel_id=1, source_target_pairs={{0,2},{1,3},{2,0},{3,1},{4,6},{5,7},{6,4},{7,5},{8,10},{9,11},{10,... | collective-permute-start | bytes 1179656 | tf_op jit(solution)/shard_map/ppermute | solution.py:171
  225.4 45.8 %collective-permute-start.31 = (bf16[256,2048]{1,0:T(8,128)(2,1)S(1)}, bf16[256,2048]{1,0:T(8,128)(2,1)S(1)}, u32[]{:S(2)}, u32[]{:S(2)}) collective-permute-start(bf16[256,2048]{1,0:T(8,128)(2,1)S(1)} %pad_maximum_fusion.19), channel_id=1, source_target_pairs={{0,16},{4,20},{8,24},{12,28},{16,0},{20,4},{24,8},{28,12},{1,17},{... | collective-permute-start | bytes 3145736 | tf_op jit(solution)/shard_map/ppermute | solution.py:167
  348.3 26.7 %collective-permute-start.47 = (bf16[192,2048]{1,0:T(8,128)(2,1)S(1)}, bf16[192,2048]{1,0:T(8,128)(2,1)S(1)}, u32[]{:S(2)}, u32[]{:S(2)}) collective-permute-start(bf16[192,2048]{1,0:T(8,128)(2,1)S(1)} %pad_maximum_fusion.22), channel_id=1, source_target_pairs={{0,8},{4,12},{8,0},{12,4},{16,24},{20,28},{24,16},{28,20},{1,9},{5... | collective-permute-start | bytes 2359304 | tf_op jit(solution)/shard_map/ppermute | solution.py:167
  382.3 24.7 %collective-permute-start.50 = (bf16[192,2048]{1,0:T(8,128)(2,1)S(1)}, bf16[192,2048]{1,0:T(8,128)(2,1)S(1)}, u32[]{:S(2)}, u32[]{:S(2)}) collective-permute-start(bf16[192,2048]{1,0:T(8,128)(2,1)S(1)} %pad_maximum_fusion.23), channel_id=1, source_target_pairs={{0,8},{4,12},{8,0},{12,4},{16,24},{20,28},{24,16},{28,20},{1,9},{5... | collective-permute-start | bytes 2359304 | tf_op jit(solution)/shard_map/ppermute | solution.py:167
  401.4 37.6 %collective-permute-start.58 = (bf16[96,2048]{1,0:T(8,128)(2,1)S(1)}, bf16[96,2048]{1,0:T(8,128)(2,1)S(1)}, u32[]{:S(2)}, u32[]{:S(2)}) collective-permute-start(bf16[96,2048]{1,0:T(8,128)(2,1)S(1)} %convolution_convert_fusion.15), channel_id=1, source_target_pairs={{0,3},{1,2},{2,1},{3,0},{4,7},{5,6},{6,5},{7,4},{8,11},{9,10},{10,... | collective-permute-start | bytes 1179656 | tf_op jit(solution)/shard_map/ppermute | solution.py:171
  605.2 41.4 %collective-permute-start.79 = (bf16[704,2048]{1,0:T(8,128)(2,1)S(1)}, bf16[704,2048]{1,0:T(8,128)(2,1)S(1)}, u32[]{:S(2)}, u32[]{:S(2)}) collective-permute-start(bf16[704,2048]{1,0:T(8,128)(2,1)S(1)} %slice.616), channel_id=1, source_target_pairs={{0,4},{4,0},{8,12},{12,8},{16,20},{20,16},{24,28},{28,24},{1,5},{5... | collective-permute-start | bytes 8650760 | tf_op jit(solution)/shard_map/ppermute | solution.py:167
  621.1 25.5 %collective-permute-start.82 = (bf16[192,2048]{1,0:T(8,128)(2,1)S(1)}, bf16[192,2048]{1,0:T(8,128)(2,1)S(1)}, u32[]{:S(2)}, u32[]{:S(2)}) collective-permute-start(bf16[192,2048]{1,0:T(8,128)(2,1)S(1)} %bitcast.521), channel_id=1, source_target_pairs={{0,8},{4,12},{8,0},{12,4},{16,24},{20,28},{24,16},{28,20},{1,9},{5... | collective-permute-start | bytes 2359304 | tf_op jit(solution)/shard_map/ppermute | solution.py:167
  648.7 33.2 %collective-permute-start.88 = (bf16[192,2048]{1,0:T(8,128)(2,1)S(1)}, bf16[192,2048]{1,0:T(8,128)(2,1)S(1)}, u32[]{:S(2)}, u32[]{:S(2)}) collective-permute-start(bf16[192,2048]{1,0:T(8,128)(2,1)S(1)} %bitcast.518), channel_id=1, source_target_pairs={{0,8},{4,12},{8,0},{12,4},{16,24},{20,28},{24,16},{28,20},{1,9},{5... | collective-permute-start | bytes 2359304 | tf_op jit(solution)/shard_map/ppermute | solution.py:167
  650.0 23.4 %collective-permute-start.84 = (bf16[48,2048]{1,0:T(8,128)(2,1)S(1)}, bf16[48,2048]{1,0:T(8,128)(2,1)S(1)}, u32[]{:S(2)}, u32[]{:S(2)}) collective-permute-start(bf16[48,2048]{1,0:T(8,128)(2,1)S(1)} %slice.618), channel_id=1, source_target_pairs={{0,8},{4,12},{8,0},{12,4},{16,24},{20,28},{24,16},{28,20},{1,9},{5... | collective-permute-start | bytes 589832 | tf_op jit(solution)/shard_map/ppermute | solution.py:167
  650.9 23.8 %collective-permute-start.86 = (bf16[96,2048]{1,0:T(8,128)(2,1)S(1)}, bf16[96,2048]{1,0:T(8,128)(2,1)S(1)}, u32[]{:S(2)}, u32[]{:S(2)}) collective-permute-start(bf16[96,2048]{1,0:T(8,128)(2,1)S(1)} %fusion.164), channel_id=1, source_target_pairs={{0,16},{4,20},{8,24},{12,28},{16,0},{20,4},{24,8},{28,12},{1,17},{... | collective-permute-start | bytes 1179656 | tf_op jit(solution)/shard_map/ppermute | solution.py:167
  652.4 29.4 %collective-permute-start.87 = (bf16[96,2048]{1,0:T(8,128)(2,1)S(1)}, bf16[96,2048]{1,0:T(8,128)(2,1)S(1)}, u32[]{:S(2)}, u32[]{:S(2)}) collective-permute-start(bf16[96,2048]{1,0:T(8,128)(2,1)S(1)} %collective-permute-done.77), channel_id=1, source_target_pairs={{0,8},{4,12},{8,0},{12,4},{16,24},{20,28},{24,16},{28,20},{1,9},{5... | collective-permute-start | bytes 1179656 | tf_op jit(solution)/shard_map/ppermute | solution.py:167
  682.2 31.6 %collective-permute-start.89 = (bf16[704,2048]{1,0:T(8,128)(2,1)S(1)}, bf16[704,2048]{1,0:T(8,128)(2,1)S(1)}, u32[]{:S(2)}, u32[]{:S(2)}) collective-permute-start(bf16[704,2048]{1,0:T(8,128)(2,1)S(1)} %slice.624), channel_id=1, source_target_pairs={{0,4},{4,0},{8,12},{12,8},{16,20},{20,16},{24,28},{28,24},{1,5},{5... | collective-permute-start | bytes 8650760 | tf_op jit(solution)/shard_map/ppermute | solution.py:167
  683.8 29.9 %collective-permute-start.91 = (bf16[192,2048]{1,0:T(8,128)(2,1)S(1)}, bf16[192,2048]{1,0:T(8,128)(2,1)S(1)}, u32[]{:S(2)}, u32[]{:S(2)}) collective-permute-start(bf16[192,2048]{1,0:T(8,128)(2,1)S(1)} %pad_maximum_fusion.27), channel_id=1, source_target_pairs={{0,16},{4,20},{8,24},{12,28},{16,0},{20,4},{24,8},{28,12},{1,17},{... | collective-permute-start | bytes 2359304 | tf_op jit(solution)/shard_map/ppermute | solution.py:167
  685.5 28.3 %collective-permute-start.95 = (bf16[192,2048]{1,0:T(8,128)(2,1)S(1)}, bf16[192,2048]{1,0:T(8,128)(2,1)S(1)}, u32[]{:S(2)}, u32[]{:S(2)}) collective-permute-start(bf16[192,2048]{1,0:T(8,128)(2,1)S(1)} %bitcast.519), channel_id=1, source_target_pairs={{0,8},{4,12},{8,0},{12,4},{16,24},{20,28},{24,16},{28,20},{1,9},{5... | collective-permute-start | bytes 2359304 | tf_op jit(solution)/shard_map/ppermute | solution.py:167
  725.4 44.1 %collective-permute-start.97 = (bf16[192,2048]{1,0:T(8,128)(2,1)S(1)}, bf16[192,2048]{1,0:T(8,128)(2,1)S(1)}, u32[]{:S(2)}, u32[]{:S(2)}) collective-permute-start(bf16[192,2048]{1,0:T(8,128)(2,1)S(1)} %pad_maximum_fusion.28), channel_id=1, source_target_pairs={{0,16},{4,20},{8,24},{12,28},{16,0},{20,4},{24,8},{28,12},{1,17},{... | collective-permute-start | bytes 2359304 | tf_op jit(solution)/shard_map/ppermute | solution.py:167
  726.9 42.6 %collective-permute-start.98 = (bf16[192,2048]{1,0:T(8,128)(2,1)S(1)}, bf16[192,2048]{1,0:T(8,128)(2,1)S(1)}, u32[]{:S(2)}, u32[]{:S(2)}) collective-permute-start(bf16[192,2048]{1,0:T(8,128)(2,1)S(1)} %pad_maximum_fusion.29), channel_id=1, source_target_pairs={{0,16},{4,20},{8,24},{12,28},{16,0},{20,4},{24,8},{28,12},{1,17},{... | collective-permute-start | bytes 2359304 | tf_op jit(solution)/shard_map/ppermute | solution.py:167
  727.7 41.9 %collective-permute-start.100 = (bf16[192,2048]{1,0:T(8,128)(2,1)S(1)}, bf16[192,2048]{1,0:T(8,128)(2,1)S(1)}, u32[]{:S(2)}, u32[]{:S(2)}) collective-permute-start(bf16[192,2048]{1,0:T(8,128)(2,1)S(1)} %bitcast.520), channel_id=1, source_target_pairs={{0,8},{4,12},{8,0},{12,4},{16,24},{20,28},{24,16},{28,20},{1,9},{5... | collective-permute-start | bytes 2359304 | tf_op jit(solution)/shard_map/ppermute | solution.py:167
  729.2 40.4 %collective-permute-start.99 = (bf16[96,2048]{1,0:T(8,128)(2,1)S(1)}, bf16[96,2048]{1,0:T(8,128)(2,1)S(1)}, u32[]{:S(2)}, u32[]{:S(2)}) collective-permute-start(bf16[96,2048]{1,0:T(8,128)(2,1)S(1)} %fusion.166), channel_id=1, source_target_pairs={{0,16},{4,20},{8,24},{12,28},{16,0},{20,4},{24,8},{28,12},{1,17},{... | collective-permute-start | bytes 1179656 | tf_op jit(solution)/shard_map/ppermute | solution.py:167
  769.8 27.0 %collective-permute-start.101 = (bf16[704,2048]{1,0:T(8,128)(2,1)S(1)}, bf16[704,2048]{1,0:T(8,128)(2,1)S(1)}, u32[]{:S(2)}, u32[]{:S(2)}) collective-permute-start(bf16[704,2048]{1,0:T(8,128)(2,1)S(1)} %slice.633), channel_id=1, source_target_pairs={{0,4},{4,0},{8,12},{12,8},{16,20},{20,16},{24,28},{28,24},{1,5},{5... | collective-permute-start | bytes 8650760 | tf_op jit(solution)/shard_map/ppermute | solution.py:167
  771.4 25.3 %collective-permute-start.104 = (bf16[256,2048]{1,0:T(8,128)(2,1)S(1)}, bf16[256,2048]{1,0:T(8,128)(2,1)S(1)}, u32[]{:S(2)}, u32[]{:S(2)}) collective-permute-start(bf16[256,2048]{1,0:T(8,128)(2,1)S(1)} %bitcast.516), channel_id=1, source_target_pairs={{0,8},{4,12},{8,0},{12,4},{16,24},{20,28},{24,16},{28,20},{1,9},{5... | collective-permute-start | bytes 3145736 | tf_op jit(solution)/shard_map/ppermute | solution.py:167
  800.2 24.5 %collective-permute-start.106 = (bf16[256,2048]{1,0:T(8,128)(2,1)}, bf16[256,2048]{1,0:T(8,128)(2,1)}, u32[]{:S(2)}, u32[]{:S(2)}) collective-permute-start(bf16[256,2048]{1,0:T(8,128)(2,1)} %bitcast.116), channel_id=1, source_target_pairs={{0,8},{4,12},{8,0},{12,4},{16,24},{20,28},{24,16},{28,20},{1,9},{5... | collective-permute-start | bytes 3145736 | tf_op jit(solution)/shard_map/ppermute | solution.py:167
  829.1 39.5 %collective-permute-start.107 = (bf16[128,2048]{1,0:T(8,128)(2,1)}, bf16[128,2048]{1,0:T(8,128)(2,1)}, u32[]{:S(2)}, u32[]{:S(2)}) collective-permute-start(bf16[128,2048]{1,0:T(8,128)(2,1)} %add_convert_fusion.7), channel_id=1, source_target_pairs={{0,1},{1,0},{2,3},{3,2},{4,5},{5,4},{6,7},{7,6},{8,9},{9,8},{10,11... | collective-permute-start | bytes 1572872 | tf_op jit(solution)/shard_map/ppermute | solution.py:171
  831.3 37.3 %collective-permute-start.108 = (bf16[128,2048]{1,0:T(8,128)(2,1)S(1)}, bf16[128,2048]{1,0:T(8,128)(2,1)}, u32[]{:S(2)}, u32[]{:S(2)}) collective-permute-start(bf16[128,2048]{1,0:T(8,128)(2,1)S(1)} %fusion.154), channel_id=1, source_target_pairs={{0,16},{4,20},{8,24},{12,28},{16,0},{20,4},{24,8},{28,12},{1,17},{... | collective-permute-start | bytes 1572872 | tf_op jit(solution)/shard_map/ppermute | solution.py:167
  833.7 35.0 %collective-permute-start.109 = (bf16[256,2048]{1,0:T(8,128)(2,1)}, bf16[256,2048]{1,0:T(8,128)(2,1)}, u32[]{:S(2)}, u32[]{:S(2)}) collective-permute-start(bf16[256,2048]{1,0:T(8,128)(2,1)} %bitcast.122), channel_id=1, source_target_pairs={{0,8},{4,12},{8,0},{12,4},{16,24},{20,28},{24,16},{28,20},{1,9},{5... | collective-permute-start | bytes 3145736 | tf_op jit(solution)/shard_map/ppermute | solution.py:167
  869.9 23.4 %collective-permute-start.110 = (bf16[128,2048]{1,0:T(8,128)(2,1)S(1)}, bf16[128,2048]{1,0:T(8,128)(2,1)S(1)}, u32[]{:S(2)}, u32[]{:S(2)}) collective-permute-start(bf16[128,2048]{1,0:T(8,128)(2,1)S(1)} %add_convert_fusion.6), channel_id=1, source_target_pairs={{0,2},{1,3},{2,0},{3,1},{4,6},{5,7},{6,4},{7,5},{8,10},{9,11},{10,... | collective-permute-start | bytes 1572872 | tf_op jit(solution)/shard_map/ppermute | solution.py:171
  939.3 49.8 %collective-permute-start.118 = (bf16[256,2048]{1,0:T(8,128)(2,1)S(1)}, bf16[256,2048]{1,0:T(8,128)(2,1)S(1)}, u32[]{:S(2)}, u32[]{:S(2)}) collective-permute-start(bf16[256,2048]{1,0:T(8,128)(2,1)S(1)} %slice.983), channel_id=1, source_target_pairs={{0,4},{4,0},{8,12},{12,8},{16,20},{20,16},{24,28},{28,24},{1,5},{5... | collective-permute-start | bytes 3145736 | tf_op jit(solution)/shard_map/ppermute | solution.py:167
  945.2 28.8 %collective-permute-start.119 = (bf16[128,2048]{1,0:T(8,128)(2,1)S(1)}, bf16[128,2048]{1,0:T(8,128)(2,1)S(1)}, u32[]{:S(2)}, u32[]{:S(2)}) collective-permute-start(bf16[128,2048]{1,0:T(8,128)(2,1)S(1)} %get-tuple-element.583), channel_id=1, source_target_pairs={{0,1},{1,0},{2,3},{3,2},{4,5},{5,4},{6,7},{7,6},{8,9},{9,8},{10,11... | collective-permute-start | bytes 1572872 | tf_op jit(solution)/shard_map/ppermute | solution.py:171
  950.9 38.2 %collective-permute-start.120 = (bf16[128,2048]{1,0:T(8,128)(2,1)S(1)}, bf16[128,2048]{1,0:T(8,128)(2,1)S(1)}, u32[]{:S(2)}, u32[]{:S(2)}) collective-permute-start(bf16[128,2048]{1,0:T(8,128)(2,1)S(1)} %get-tuple-element.584), channel_id=1, source_target_pairs={{0,2},{1,3},{2,0},{3,1},{4,6},{5,7},{6,4},{7,5},{8,10},{9,11},{10,... | collective-permute-start | bytes 1572872 | tf_op jit(solution)/shard_map/ppermute | solution.py:171
  951.4 37.7 %collective-permute-start.121 = (bf16[128,2048]{1,0:T(8,128)(2,1)S(1)}, bf16[128,2048]{1,0:T(8,128)(2,1)S(1)}, u32[]{:S(2)}, u32[]{:S(2)}) collective-permute-start(bf16[128,2048]{1,0:T(8,128)(2,1)S(1)} %get-tuple-element.582), channel_id=1, source_target_pairs={{0,3},{1,2},{2,1},{3,0},{4,7},{5,6},{6,5},{7,4},{8,11},{9,10},{10,... | collective-permute-start | bytes 1572872 | tf_op jit(solution)/shard_map/ppermute | solution.py:171
  (294 other events, 4257.3 us)
